TPU v7x, 32 devices: a whole 2x2x4 slice. The times are simulated.
32 devices in a mesh: dp: 8 (over z, y), mp: 4 (over x, core).
Axes of the slice: x: 2, y: 2, z: 4, core: 2. Of those that a mesh axis runs over, the one named last changes fastest.
Arguments:
- hidden_in: bfloat16 [3072, 2048], P(('dp', 'mp')), may hold values from -12 to 12
- segment_ids: int32 [8, 384], P('dp'), may hold values from 0 to 7, never falling along the last dimension, each value on 1 to 192 neighbouring positions
- page_table: int32 [8, 3], P('dp'), may hold values from 0 to 2, each once within a row
- qkv_master: float32 [2048, 6144], P(('dp', 'mp')), may hold values from -0.3 to 0.3
- up_master: float32 [2048, 8192], P(('dp', 'mp')), may hold values from -0.125 to 0.125
- dense_weight: bfloat16 [2048, 2048], P('mp'), may hold values from -0.125 to 0.125
Outputs:
- hidden_out: bfloat16 [3072, 2048], P(('dp', 'mp'))
- activated: bfloat16 [3072, 8192], P('dp', 'mp')
- cache_pages: bfloat16 [24, 2, 16, 128, 128], P('dp', None, 'mp')
Inputs may be any that keep to these rules, and one draw needn't show every extreme that they name: `segment_ids`: within a group segment ids never fall; each request holds 1 to 192 tokens and one holds exactly that many. `page_table`: each row names every slot of its group once.
All inputs are finite; a program needn't handle non-finite values.
Results may differ from a plain program's by a relative error of at most 0.015.
Values may be sent and summed in bfloat16 or wider, within the bound.
No kernel may reach another device: no remote copies, remote signals or barrier semaphores. Data moves between devices by JAX's collectives and lax.ppermute only.
A program may use at most 64 MiB of HBM per device.

v0:
```python
import jax
import jax.numpy as jnp
from jax import lax
from jax.sharding import PartitionSpec as P

H = 16
HD = 128
PAGE = 128


def layer_norm(values):
    mean_val = jnp.mean(values, -1, keepdims=True)
    centered = values - mean_val
    variance = jnp.mean(centered * centered, -1, keepdims=True)
    return centered * lax.rsqrt(variance + 1e-05)


def reorder_rows(weights, mp_count, dp_count):
    block = weights.shape[0] // (mp_count * dp_count)
    shaped = weights.reshape(mp_count, dp_count, block, weights.shape[1])
    return shaped.transpose(1, 0, 2, 3).reshape(weights.shape[0], weights.shape[1])


def attend(normed, qkv_w, segment, table, mp_index):
    group_rows = normed.shape[0]
    heads_dev = qkv_w.shape[1] // (3 * HD)
    joined = jnp.dot(normed, qkv_w, preferred_element_type=jnp.float32).astype(jnp.bfloat16)
    joined = joined.reshape(group_rows, heads_dev, 3, HD)
    query = joined[:, :, 0]
    keys = joined[:, :, 1]
    vals = joined[:, :, 2]
    head_ids = mp_index * heads_dev + jnp.arange(heads_dev)
    slopes = jnp.exp2(-8.0 * (head_ids + 1).astype(jnp.float32) / H)
    positions = jnp.arange(group_rows)
    distance = (positions[:, None] - positions[None, :]).astype(jnp.float32)
    allowed = (segment[:, None] == segment[None, :]) & (distance >= 0)
    scores = jnp.einsum("thd,shd->hts", query, keys, preferred_element_type=jnp.float32) / jnp.sqrt(
        jnp.float32(HD)
    )
    scores = scores - slopes[:, None, None] * distance[None]
    scores = jnp.where(allowed[None], scores, -jnp.inf)
    probs = jax.nn.softmax(scores, axis=-1).astype(jnp.bfloat16)
    context = jnp.einsum("hts,shd->thd", probs, vals, preferred_element_type=jnp.float32).astype(
        jnp.bfloat16
    )
    context = context.reshape(group_rows, heads_dev * HD)
    key_vals = jnp.stack([keys, vals], 1)
    pages_here = group_rows // PAGE
    key_vals = key_vals.reshape(pages_here, PAGE, 2, heads_dev, HD).transpose(0, 2, 3, 1, 4)
    cache = jnp.zeros((pages_here, 2, heads_dev, PAGE, HD), jnp.bfloat16).at[table].set(key_vals)
    return (context, cache)


def local(hidden_in, segment_ids, page_table, qkv_master, up_master, dense_weight):
    mp_count = lax.axis_size("mp")
    dp_count = lax.axis_size("dp")
    mp_index = lax.axis_index("mp")
    qkv_bf = qkv_master.astype(jnp.bfloat16)
    up_bf = up_master.astype(jnp.bfloat16)
    qkv_rows, up_rows = (
        lax.all_gather(qkv_bf, "dp", axis=0, tiled=True),
        lax.all_gather(up_bf, "dp", axis=0, tiled=True),
    )
    qkv_cols, up_cols = (
        lax.all_to_all(qkv_rows, "mp", split_axis=1, concat_axis=0, tiled=True),
        lax.all_to_all(up_rows, "mp", split_axis=1, concat_axis=0, tiled=True),
    )
    qkv_w = reorder_rows(qkv_cols, mp_count, dp_count)
    up_w = reorder_rows(up_cols, mp_count, dp_count)
    normed_own = layer_norm(hidden_in.astype(jnp.float32)).astype(jnp.bfloat16)
    normed = lax.all_gather(normed_own, "mp", axis=0, tiled=True)
    context, cache = attend(normed, qkv_w, segment_ids[0], page_table[0], mp_index)
    share = lax.psum_scatter(
        jnp.dot(context, dense_weight, preferred_element_type=jnp.float32).astype(jnp.bfloat16),
        "mp",
        scatter_dimension=0,
        tiled=True,
    ).astype(jnp.float32)
    stream_own = hidden_in.astype(jnp.float32) + share
    normed_two = lax.all_gather(
        layer_norm(stream_own).astype(jnp.bfloat16), "mp", axis=0, tiled=True
    )
    upper = jnp.dot(normed_two, up_w, preferred_element_type=jnp.float32)
    activated = jax.nn.gelu(upper, approximate=True).astype(jnp.bfloat16)
    return (stream_own.astype(jnp.bfloat16), activated, cache)


def solution(mesh):
    placed = (
        P(("dp", "mp"), None),
        P("dp", None),
        P("dp", None),
        P(("dp", "mp"), None),
        P(("dp", "mp"), None),
        P("mp", None),
    )
    return jax.shard_map(
        local,
        mesh=mesh,
        in_specs=placed,
        out_specs=(P(("dp", "mp"), None), P("dp", "mp"), P("dp", None, "mp", None, None)),
        check_vma=False,
    )
```

profile of v0, /device:TPU:0, one launch (start us, length us, event | category | flops | bytes accessed | tf_op | source)
XLA Modules:
  0.0 425.9 jit_solution(15218608388609431406)
XLA Ops:
  7.2 2.5 convert_element_type.61
  11.4 2.7 convert_element_type.72
  14.1 98.5 %all-gather.7.cloned.1.call-done = bf16[512,6144]{1,0:T(8,128)(2,1)} async-done(((bf16[64,6144]{1,0:T(8,128)(2,1)}), bf16[512,6144]{1,0:T(8,128)(2,1)}) %all-gather.7.cloned.1.call-update) | async-done | bytes 6291472 | tf_op jit(solution)/shard_map/all_gather | solution.py:61
  112.5 8.7 %copy.44 = bf16[512,6144]{0,1:T(8,128)(2,1)} copy(bf16[512,6144]{1,0:T(8,128)(2,1)} %all-gather.7.cloned.1.call-done) | data formatting | bytes 12582912 | tf_op jit(solution)/shard_map/all_gather | solution.py:61
  121.3 5.4 %all-to-all-start = ((bf16[512,4,1536]{0,2,1:T(8,128)(2,1)}), bf16[512,4,1536]{0,2,1:T(8,128)(2,1)}, u32[]{:S(2)}, u32[]{:S(2)}) async-start(bf16[512,4,1536]{0,2,1:T(8,128)(2,1)} %bitcast.71), calls=%async_computation | async-start | bytes 12582912 | tf_op jit(solution)/shard_map/all_to_all | solution.py:65
  127.1 71.5 %all-to-all-done = bf16[512,4,1536]{0,2,1:T(8,128)(2,1)} async-done(((bf16[512,4,1536]{0,2,1:T(8,128)(2,1)}), bf16[512,4,1536]{0,2,1:T(8,128)(2,1)}, u32[]{:S(2)}, u32[]{:S(2)}) %all-to-all-start) | async-done | bytes 6291488 | tf_op jit(solution)/shard_map/all_to_all | solution.py:65
  198.6 8.7 %copy.45 = bf16[4,512,1536]{2,1,0:T(8,128)(2,1)} copy(bf16[4,512,1536]{1,2,0:T(8,128)(2,1)} %bitcast.1) | data formatting | bytes 12582912 | tf_op jit(solution)/shard_map/all_to_all | solution.py:65
  207.3 6.1 %copy.46 = bf16[8,4,64,1536]{3,2,1,0:T(8,128)(2,1)} copy(bf16[8,4,64,1536]{3,2,0,1:T(8,128)(2,1)} %bitcast.72) | data formatting | bytes 12582912 | tf_op jit(solution)/shard_map/transpose | solution.py:21
  213.4 6.9 %convolution_convert_fusion.1 = bf16[384,1536]{1,0:T(8,128)(2,1)} fusion(bf16[384,2048]{1,0:T(8,128)(2,1)} %all-gather.5.cloned.1.call-done, bf16[2048,1536]{1,0:T(8,128)(2,1)} %bitcast.74), kind=kOutput, calls=%fused_computation.12 | convolution fusion | flops 2416508928 | bytes 9043968 | tf_op jit(solution)/shard_map/dot_general | solution.py:27
  220.3 2.4 copy.47
  222.7 2.3 fusion.42
  225.0 2.7 convolution_convert_fusion.2
  227.6 2.2 convolution_convert_fusion
  229.8 34.0 %all-gather.11.cloned.1.call-done = bf16[512,8192]{1,0:T(8,128)(2,1)} async-done(((bf16[64,8192]{1,0:T(8,128)(2,1)}), bf16[512,8192]{1,0:T(8,128)(2,1)}) %all-gather.11.cloned.1.call-update) | async-done | bytes 8388624 | tf_op jit(solution)/shard_map/all_gather | solution.py:62
  263.9 12.1 %copy.52 = bf16[512,8192]{0,1:T(8,128)(2,1)} copy(bf16[512,8192]{1,0:T(8,128)(2,1)} %all-gather.11.cloned.1.call-done) | data formatting | bytes 16777216 | tf_op jit(solution)/shard_map/all_gather | solution.py:62
  275.9 5.6 %all-to-all-start.1 = ((bf16[512,4,2048]{0,2,1:T(8,128)(2,1)}), bf16[512,4,2048]{0,2,1:T(8,128)(2,1)}, u32[]{:S(2)}, u32[]{:S(2)}) async-start(bf16[512,4,2048]{0,2,1:T(8,128)(2,1)} %bitcast.69), calls=%async_computation.2 | async-start | bytes 16777216 | tf_op jit(solution)/shard_map/all_to_all | solution.py:66
  281.8 19.1 %reduce-scatter.2.cloned.1.call-done = bf16[96,2048]{1,0:T(8,128)(2,1)} async-done(((bf16[384,2048]{1,0:T(8,128)(2,1)}), bf16[96,2048]{1,0:T(8,128)(2,1)}) %reduce-scatter.2.cloned.1.call-update) | async-done | bytes 393232 | tf_op jit(solution)/shard_map/reduce_scatter | solution.py:73
  300.9 1.2 fusion.19
  302.1 1.3 multiply_reduce_fusion
  303.4 2.0 multiply_convert_fusion
  307.3 83.3 %all-to-all-done.1 = bf16[512,4,2048]{0,2,1:T(8,128)(2,1)} async-done(((bf16[512,4,2048]{0,2,1:T(8,128)(2,1)}), bf16[512,4,2048]{0,2,1:T(8,128)(2,1)}, u32[]{:S(2)}, u32[]{:S(2)}) %all-to-all-start.1) | async-done | bytes 8388640 | tf_op jit(solution)/shard_map/all_to_all | solution.py:66
  390.6 11.4 %copy.53 = bf16[4,512,2048]{2,1,0:T(8,128)(2,1)} copy(bf16[4,512,2048]{1,2,0:T(8,128)(2,1)} %bitcast.12) | data formatting | bytes 16777216 | tf_op jit(solution)/shard_map/all_to_all | solution.py:66
  402.0 8.3 %copy.54 = bf16[8,4,64,2048]{3,2,1,0:T(8,128)(2,1)} copy(bf16[8,4,64,2048]{3,2,0,1:T(8,128)(2,1)} %bitcast.70) | data formatting | bytes 16777216 | tf_op jit(solution)/shard_map/transpose | solution.py:21
  410.2 9.2 %fusion.8 = bf16[384,2048]{1,0:T(8,128)(2,1)} fusion(bf16[384,2048]{1,0:T(8,128)(2,1)} %all-gather.9.cloned.1.call-done, bf16[2048,2048]{1,0:T(8,128)(2,1)} %bitcast.73), kind=kOutput, calls=%fused_computation.10 | convolution fusion | flops 3228303360 | bytes 11534336 | tf_op jit(solution)/shard_map/dot_general | solution.py:83
  (47 shorter events, 3.9 us)
Async XLA Ops:
  7.2 220.5 %copy-start = (bf16[512,2048]{1,0:T(8,128)(2,1)S(1)}, bf16[512,2048]{1,0:T(8,128)(2,1)}, u32[]{:S(2)}) copy-start(bf16[512,2048]{1,0:T(8,128)(2,1)} %param.11) | copy-start | bytes 6291460
  7.2 2.7 copy-start.2
  7.2 105.3 %all-gather.7.cloned.1.call-start = ((), (), s32[]{:S(2)}) async-start(), calls=%async_computation.4 | async-start | bytes 7077888 | tf_op jit(solution)/shard_map/all_gather | solution.py:61
  9.8 203.6 %all-gather.5.cloned.1.call-start = ((), (), s32[]{:S(2)}) async-start(), calls=%async_computation.3 | async-start | bytes 1966080 | tf_op jit(solution)/shard_map/all_gather | solution.py:71
  11.3 252.6 %all-gather.11.cloned.1.call-start = ((), (), s32[]{:S(2)}) async-start(), calls=%async_computation.7 | async-start | bytes 9437184 | tf_op jit(solution)/shard_map/all_gather | solution.py:62
  121.3 5.5 %copy-start.6 = (s32[1,384]{1,0:T(1,128)S(1)}, s32[1,384]{1,0:T(1,128)}, u32[]{:S(2)}) copy-start(s32[1,384]{1,0:T(1,128)} %param.7) | copy-start | bytes 4612
  121.3 77.3 %all-to-all-start = ((bf16[512,4,1536]{0,2,1:T(8,128)(2,1)}), bf16[512,4,1536]{0,2,1:T(8,128)(2,1)}, u32[]{:S(2)}, u32[]{:S(2)}) async-start(bf16[512,4,1536]{0,2,1:T(8,128)(2,1)} %bitcast.71), calls=%async_computation | async-start | bytes 12582912 | tf_op jit(solution)/shard_map/all_to_all | solution.py:65
  126.7 174.2 %reduce-scatter.2.cloned.1.call-start = ((), (), s32[]{:S(2)}) async-start(), calls=%async_computation.5 | async-start | bytes 1966080 | tf_op jit(solution)/shard_map/reduce_scatter | solution.py:73
  127.1 95.6 %copy-start.5 = (pred[384,384]{0,1:T(8,128)(4,1)}, pred[384,384]{0,1:T(8,128)(4,1)S(1)}, u32[]{:S(2)}) copy-start(pred[384,384]{0,1:T(8,128)(4,1)S(1)} %compare_and_fusion) | copy-start | bytes 442372
  275.9 114.6 %all-to-all-start.1 = ((bf16[512,4,2048]{0,2,1:T(8,128)(2,1)}), bf16[512,4,2048]{0,2,1:T(8,128)(2,1)}, u32[]{:S(2)}, u32[]{:S(2)}) async-start(bf16[512,4,2048]{0,2,1:T(8,128)(2,1)} %bitcast.69), calls=%async_computation.2 | async-start | bytes 16777216 | tf_op jit(solution)/shard_map/all_to_all | solution.py:66
  281.6 23.9 %copy-start.7 = (s32[1,3]{1,0:T(1,128)S(1)}, s32[1,3]{1,0:T(1,128)}, u32[]{:S(2)}) copy-start(s32[1,3]{1,0:T(1,128)} %param.8) | copy-start | bytes 40
  281.6 23.9 %copy-start.3 = (bf16[384,1536]{0,1:T(8,128)(2,1)S(1)}, bf16[384,1536]{0,1:T(8,128)(2,1)}, u32[]{:S(2)}) copy-start(bf16[384,1536]{0,1:T(8,128)(2,1)} %copy.47) | copy-start | bytes 3538948
  281.6 128.6 %all-gather.9.cloned.1.call-start = ((), (), s32[]{:S(2)}) async-start(), calls=%async_computation.6 | async-start | bytes 1966080 | tf_op jit(solution)/shard_map/all_gather | solution.py:80
  307.3 94.7 %copy-start.4 = (bf16[3,2,4,128,128]{4,3,2,1,0:T(8,128)(2,1)}, bf16[3,2,4,128,128]{4,3,2,1,0:T(8,128)(2,1)S(1)}, u32[]{:S(2)}) copy-start(bf16[3,2,4,128,128]{4,3,2,1,0:T(8,128)(2,1)S(1)} %scatter_fusion) | copy-start | bytes 2359300
  410.2 9.2 %copy-start.1 = (bf16[512,2048]{1,0:T(8,128)(2,1)S(1)}, bf16[512,2048]{1,0:T(8,128)(2,1)}, u32[]{:S(2)}) copy-start(bf16[512,2048]{1,0:T(8,128)(2,1)} %param.11) | copy-start | bytes 6291460
Sparse Core Ops, SparseCore 0:
  10.8 101.7 all-gather.6
  114.7 18.9 all-gather.4
  135.9 127.9 all-gather.10
  266.8 34.0 reduce-scatter.1
  305.6 29.0 all-gather.8
where the time goes:
time: 427 us; the launch traced here: 426 us
  waiting for transfers between devices  306 us (72%)
  local copies, waits for them, and re-layouts  59.4 us (14%)
  matrix products  23.1 us (5%)
  between operations  14 us (3%)
  starting transfers between devices  11.5 us (3%)
  other arithmetic  11.5 us (3%)
    all_gather x1, waiting for transfers between devices, local(): lax.all_gather(qkv_bf, 'dp', axis=0, tiled=True)  98.5 us
    all_to_all x1, waiting for transfers between devices, local(): lax.all_to_all(up_rows, 'mp', split_axis=1, concat_axis=0, tiled=True)  83.3 us
    all_to_all x1, waiting for transfers between devices, local(): lax.all_to_all(qkv_rows, 'mp', split_axis=1, concat_axis=0, tiled=True)  71.5 us
    all_gather x1, waiting for transfers between devices, local(): lax.all_gather(up_bf, 'dp', axis=0, tiled=True)  34 us
    reduce_scatter x1, waiting for transfers between devices, local(): lax.psum_scatter(jnp.dot(context, dense_weight, preferred_element_type=jn...  19.1 us
    transpose x2, local copies, waits for them, and re-layouts, reorder_rows(): shaped.transpose(1, 0, 2, 3).reshape(weights.shape[0], weights.shape[1])  14.4 us
    all_gather x1, local copies, waits for them, and re-layouts, local(): lax.all_gather(up_bf, 'dp', axis=0, tiled=True)  12.1 us
    all_to_all x1, local copies, waits for them, and re-layouts, local(): lax.all_to_all(up_rows, 'mp', split_axis=1, concat_axis=0, tiled=True)  11.4 us
  transfers between devices with their start and end apart: 7, of which 5 were waited for; matrix products, arithmetic and copies ran while one was open for 19% of the time, Pallas kernels for 0%

commit v1 on v0

v1 whole, which is shorter than its diff:
```python
import functools

import jax
import jax.numpy as jnp
from jax import lax
from jax.experimental import pallas as pl
from jax.experimental.pallas import tpu as pltpu
from jax.sharding import PartitionSpec as P

H = 16
HD = 128
PAGE = 128
AXES = ("dp", "mp")
BF = jnp.bfloat16
F32 = jnp.float32
VMEM_LIMIT = 48 * 1024 * 1024


def layer_norm(values):
    mean_val = jnp.mean(values, -1, keepdims=True)
    centered = values - mean_val
    variance = jnp.mean(centered * centered, -1, keepdims=True)
    return centered * lax.rsqrt(variance + 1e-05)


def attend(normed, qkv_w, segment, table, mp_index):
    group_rows = normed.shape[0]
    heads_dev = qkv_w.shape[1] // (3 * HD)
    joined = jnp.dot(normed, qkv_w, preferred_element_type=F32).astype(BF)
    joined = joined.reshape(group_rows, heads_dev, 3, HD)
    query = joined[:, :, 0]
    keys = joined[:, :, 1]
    vals = joined[:, :, 2]
    head_ids = mp_index * heads_dev + jnp.arange(heads_dev)
    slopes = jnp.exp2(-8.0 * (head_ids + 1).astype(F32) / H)
    positions = jnp.arange(group_rows)
    distance = (positions[:, None] - positions[None, :]).astype(F32)
    allowed = (segment[:, None] == segment[None, :]) & (distance >= 0)
    scores = jnp.einsum("thd,shd->hts", query, keys, preferred_element_type=F32) / jnp.sqrt(F32(HD))
    scores = scores - slopes[:, None, None] * distance[None]
    scores = jnp.where(allowed[None], scores, -jnp.inf)
    probs = jax.nn.softmax(scores, axis=-1).astype(BF)
    context = jnp.einsum("hts,shd->thd", probs, vals, preferred_element_type=F32).astype(BF)
    context = context.reshape(group_rows, heads_dev * HD)
    key_vals = jnp.stack([keys, vals], 1)
    pages_here = group_rows // PAGE
    key_vals = key_vals.reshape(pages_here, PAGE, 2, heads_dev, HD).transpose(0, 2, 3, 1, 4)
    cache = jnp.zeros((pages_here, 2, heads_dev, PAGE, HD), BF).at[table].set(key_vals)
    return context, cache


def local_any(hidden_in, segment_ids, page_table, qkv_master, up_master, dense_weight):
    mp_index = lax.axis_index("mp")

    def columns(master):
        mine = lax.all_to_all(master.astype(BF), "mp", split_axis=1, concat_axis=0, tiled=True)
        return lax.all_gather(mine, "dp", axis=0, tiled=True)

    qkv_w = columns(qkv_master)
    up_w = columns(up_master)
    normed_own = layer_norm(hidden_in.astype(F32)).astype(BF)
    normed = lax.all_gather(normed_own, "mp", axis=0, tiled=True)
    context, cache = attend(normed, qkv_w, segment_ids[0], page_table[0], mp_index)
    term = jnp.dot(context, dense_weight, preferred_element_type=F32).astype(BF)
    share = lax.psum_scatter(term, "mp", scatter_dimension=0, tiled=True).astype(F32)
    stream_own = hidden_in.astype(F32) + share
    normed_two = lax.all_gather(layer_norm(stream_own).astype(BF), "mp", axis=0, tiled=True)
    upper = jnp.dot(normed_two, up_w, preferred_element_type=F32)
    activated = jax.nn.gelu(upper, approximate=True).astype(BF)
    return stream_own.astype(BF), activated, cache


NZ, NY, NM = 4, 2, 4
PLANE = NY * NM


def pairs(move):
    out = []
    for z in range(NZ):
        for y in range(NY):
            for m in range(NM):
                to = move(z, y, m)
                if to is not None:
                    out.append(((z * NY + y) * NM + m, (to[0] * NY + to[1]) * NM + to[2]))
    return out


CORE = pairs(lambda z, y, m: (z, y, m ^ 1))
XSWAP = pairs(lambda z, y, m: (z, y, m ^ 2))
YSWAP = pairs(lambda z, y, m: (z, y ^ 1, m))
UP = pairs(lambda z, y, m: (z + 1, y, m) if z < NZ - 1 else None)
DOWN = pairs(lambda z, y, m: (z - 1, y, m) if z > 0 else None)
PLANES = [[z * PLANE + i for i in range(PLANE)] for z in range(NZ)]


def send(value, moves):
    return lax.ppermute(value, AXES, moves)


def params(**more):
    return pltpu.CompilerParams(vmem_limit_bytes=VMEM_LIMIT, **more)


ANY = pl.BlockSpec(memory_space=pl.ANY)
SMEM = pl.BlockSpec(memory_space=pltpu.SMEM)
VMEM = pl.BlockSpec(memory_space=pltpu.VMEM)


def cast_kernel(src, dst):
    dst[0] = src[...].astype(BF)


def cast_pieces(master, parts, part):
    rows, cols = master.shape
    width = cols // PLANE // parts

    def place(p):
        return (0, (2 * (p % NM) + p // NM) * parts + part)

    return pl.pallas_call(
        cast_kernel,
        grid=(PLANE,),
        in_specs=[pl.BlockSpec((rows, width), place)],
        out_specs=pl.BlockSpec((1, rows, width), lambda p: (p, 0, 0)),
        out_shape=jax.ShapeDtypeStruct((PLANE, rows, width), BF),
        compiler_params=params(),
    )(master)


def in_plane(pieces):
    return lax.all_to_all(pieces, AXES, split_axis=0, concat_axis=0, tiled=True, axis_index_groups=PLANES)


def ring(mine):
    above, below = [mine], [mine]
    for _ in range(NZ - 1):
        below.append(send(below[-1], UP))
        above.append(send(above[-1], DOWN))
    return [mine] + below[1:] + above[1:]


def load_shards(z, shards, wbuf, sem):
    own, below, above = shards[0], shards[1:NZ], shards[NZ:]
    rows = own.shape[0]

    def start(src, slot):
        pltpu.make_async_copy(src, wbuf.at[pl.ds(slot * rows, rows)], sem.at[slot]).start()

    for slot in range(NZ):
        @pl.when(z == slot)
        def _():
            start(own, slot)

        for far in range(1, NZ):
            if slot + far < NZ:
                @pl.when(z == slot + far)
                def _():
                    start(below[far - 1], slot)

            if slot - far >= 0:
                @pl.when(z == slot - far)
                def _():
                    start(above[far - 1], slot)

    def wait():
        for slot in range(NZ):
            pltpu.make_async_copy(own, wbuf.at[pl.ds(slot * rows, rows)], sem.at[slot]).wait()

    return wait


def head_kernel(pos, slope, seg_rows, seg_cols, normed, *rest):
    shards = rest[: 2 * NZ - 1]
    ctx, kv_own, kv_other, wbuf, sem = rest[2 * NZ - 1 :]
    z, y = pos[0], pos[1]
    wait = load_shards(z, shards, wbuf, sem)
    group = normed.shape[0] // NY
    here = lax.broadcasted_iota(jnp.int32, (group, group), 0)
    there = lax.broadcasted_iota(jnp.int32, (group, group), 1)
    distance = here - there
    fall = slope[0] * distance.astype(F32)
    wait()
    for g, kv in ((0, kv_own), (1, kv_other)):
        first = pl.multiple_of((y ^ g) * group, group)
        rows = pl.ds(first, group)
        joined = jnp.dot(normed[rows, :], wbuf[...], preferred_element_type=F32).astype(BF)
        query, keys, vals = joined[:, :HD], joined[:, HD : 2 * HD], joined[:, 2 * HD :]
        scores = lax.dot_general(query, keys, (((1,), (1,)), ((), ())), preferred_element_type=F32)
        scores = scores * (1.0 / HD**0.5) - fall
        allowed = (seg_cols[g] == seg_rows[g]) & (distance >= 0)
        scores = jnp.where(allowed, scores, -jnp.inf)
        top = jnp.max(scores, -1, keepdims=True)
        raised = jnp.exp(scores - top)
        probs = (raised / jnp.sum(raised, -1, keepdims=True)).astype(BF)
        ctx[rows, :] = jnp.dot(probs, vals, preferred_element_type=F32).astype(BF)
        for b in range(group // PAGE):
            kv[b, 0] = keys[b * PAGE : (b + 1) * PAGE]
            kv[b, 1] = vals[b * PAGE : (b + 1) * PAGE]


def one_head(pos, slope, seg_rows, seg_cols, normed, shards):
    tokens, depth = normed.shape
    width = shards[0].shape[1]
    kv_shape = jax.ShapeDtypeStruct((tokens // NY // PAGE, 2, PAGE, HD), BF)
    return pl.pallas_call(
        head_kernel,
        in_specs=[SMEM, SMEM, VMEM, VMEM, VMEM] + [ANY] * len(shards),
        out_specs=[VMEM, VMEM, VMEM],
        out_shape=[jax.ShapeDtypeStruct((tokens, HD), BF), kv_shape, kv_shape],
        scratch_shapes=[pltpu.VMEM((depth, width), BF), pltpu.SemaphoreType.DMA((NZ,))],
        compiler_params=params(),
        cost_estimate=pl.CostEstimate(
            flops=2 * tokens * depth * width, bytes_accessed=2 * depth * (tokens + width), transcendentals=0
        ),
    )(pos, slope, seg_rows, seg_cols, normed, *shards)


def dense_kernel(pos, hidden, ctx, *rest):
    blocks = rest[:NM]
    out, normed = rest[NM:]
    m = pos[2]
    total = None
    for r in range(NM):
        owner = m ^ r
        left = jnp.concatenate([ctx[owner], ctx[NM + owner]], axis=1)
        term = jnp.dot(left, blocks[r][...], preferred_element_type=F32).astype(BF).astype(F32)
        total = term if total is None else total + term
    stream = hidden[...].astype(F32) + total
    out[...] = stream.astype(BF)
    normed[...] = layer_norm(stream).astype(BF)


def dense_norm(pos, hidden, ctx, blocks):
    shape = jax.ShapeDtypeStruct(hidden.shape, BF)
    return pl.pallas_call(
        dense_kernel,
        in_specs=[SMEM, VMEM, VMEM] + [VMEM] * NM,
        out_specs=[VMEM, VMEM],
        out_shape=[shape, shape],
        compiler_params=params(),
    )(pos, hidden, ctx, *blocks)


def up_kernel(pos, *rest):
    pieces = rest[:10]
    shards = rest[10 : 10 + 2 * NZ - 1]
    act_own, act_other, xbuf, wbuf, xsem, sem = rest[10 + 2 * NZ - 1 :]
    z, m = pos[0], pos[2]
    wait = load_shards(z, shards, wbuf, sem)
    group = act_own.shape[0]
    share = group // NM
    half = share // 2
    place = [(0, 0, 0), (0, 1, 0), (0, 2, 0), (0, 3, 0), (1, 0, 0), (1, 1, 0)]
    place += [(1, 2, 0), (1, 2, half), (1, 3, 0), (1, 3, half)]
    copies = []
    for i, (g, r, extra) in enumerate(place):
        first = pl.multiple_of(g * group + (m ^ r) * share + extra, 16)
        copies.append(pltpu.make_async_copy(pieces[i], xbuf.at[pl.ds(first, pieces[i].shape[0])], xsem.at[i]))
    for copy in copies:
        copy.start()
    for copy in copies:
        copy.wait()
    wait()
    for g, act in ((1, act_other), (0, act_own)):
        upper = jnp.dot(xbuf[g * group : (g + 1) * group], wbuf[...], preferred_element_type=F32)
        act[...] = jax.nn.gelu(upper, approximate=True).astype(BF)


def up_part(pos, pieces, shards):
    group = pieces[0].shape[0] * NM
    depth, width = pieces[0].shape[1], shards[0].shape[1]
    shape = jax.ShapeDtypeStruct((group, width), BF)
    return pl.pallas_call(
        up_kernel,
        in_specs=[SMEM] + [ANY] * (10 + len(shards)),
        out_specs=[VMEM, VMEM],
        out_shape=[shape, shape],
        scratch_shapes=[
            pltpu.VMEM((NY * group, depth), BF),
            pltpu.VMEM((depth, width), BF),
            pltpu.SemaphoreType.DMA((10,)),
            pltpu.SemaphoreType.DMA((NZ,)),
        ],
        compiler_params=params(),
        cost_estimate=pl.CostEstimate(
            flops=4 * group * depth * width, bytes_accessed=2 * depth * (2 * group + width), transcendentals=0
        ),
    )(pos, *pieces, *shards)


def join_kernel(pos, *rest):
    *parts, out = rest
    y = pos[1]
    count = len(parts) // 2
    width = parts[0].shape[1]
    for side in range(2):
        for j in range(count):
            first = pl.multiple_of((y ^ side) * (count * width) + j * width, width)
            out[:, pl.ds(first, width)] = parts[side * count + j][...]


def join_columns(pos, own, got):
    group, width = own[0].shape
    return pl.pallas_call(
        join_kernel,
        in_specs=[SMEM] + [VMEM] * (len(own) + len(got)),
        out_specs=VMEM,
        out_shape=jax.ShapeDtypeStruct((group, width * (len(own) + len(got))), BF),
        compiler_params=params(),
    )(pos, *own, *got)


def pages_kernel(pos, table, *rest):
    *parts, out = rest
    y = pos[1]
    for b in range(parts[0].shape[0]):
        slot = table[0, b]
        for side in range(2):
            for h in range(2):
                out[slot, :, (y ^ side) * 2 + h] = parts[side * 2 + h][b]


def place_pages(pos, table, own, got):
    blocks, two, page, width = own[0].shape
    return pl.pallas_call(
        pages_kernel,
        in_specs=[SMEM, SMEM] + [VMEM] * 4,
        out_specs=VMEM,
        out_shape=jax.ShapeDtypeStruct((blocks, two, 4, page, width), BF),
        compiler_params=params(),
    )(pos, table, *own, *got)


def gather_plane(mine):
    half = mine.shape[0] // 2
    from_y = send(mine, YSWAP)
    from_x = send(mine, XSWAP)
    far_low = send(from_y[:half], XSWAP)
    far_high = send(from_x[half:], YSWAP)
    other = [send(v, CORE) for v in (mine, from_y, from_x, far_low, far_high)]
    return [mine, other[0], from_x, other[2], from_y, other[1], far_low, far_high, other[3], other[4]]


def local_planes(hidden_in, segment_ids, page_table, qkv_master, up_master, dense_weight):
    dp, mp = lax.axis_index("dp"), lax.axis_index("mp")
    z, y = dp // NY, dp % NY
    pos = jnp.stack([z, y, mp]).astype(jnp.int32)

    heads = 2
    pieces = cast_pieces(qkv_master, 1, 0)
    swapped = in_plane(pieces)
    q_shards = []
    for h in range(heads):
        width = swapped.shape[2] // heads
        q_shards.append(swapped[:, :, h * width : (h + 1) * width].reshape(-1, width))

    parts = 2
    up_pieces = [cast_pieces(up_master, parts, j) for j in range(parts)]
    up_shards = [in_plane(p) for p in up_pieces]
    up_shards = [s.reshape(-1, s.shape[2]) for s in up_shards]

    normed_own = layer_norm(hidden_in.astype(F32)).astype(BF)
    normed = lax.all_gather(normed_own, AXES, axis=0, tiled=True, axis_index_groups=PLANES)
    segments = jnp.concatenate([segment_ids, send(segment_ids, YSWAP)], 0)
    seg_rows, seg_cols = segments[:, None, :], segments[:, :, None]

    q_rings = [ring(s) for s in q_shards]

    dense_x = send(dense_weight, XSWAP)
    dense_c = send(dense_weight, CORE)
    dense_xc = send(dense_x, CORE)

    contexts, kv_own, kv_got = [], [], []
    for h in range(heads):
        head = 4 * mp + 2 * y + h
        slope = jnp.exp2(-8.0 * (head + 1).astype(F32) / H).reshape(1)
        ctx, own, other = one_head(pos, slope, seg_rows, seg_cols, normed, q_rings[h])
        contexts.append(ctx)
        kv_own.append(own)
        kv_got.append(send(other, YSWAP))
    context = jnp.concatenate(contexts, 1).reshape(PLANE, -1, heads * HD)
    ctx_own = in_plane(context)
    hidden_out, normed_two = dense_norm(
        pos, hidden_in, ctx_own, [dense_weight, dense_c, dense_x, dense_xc]
    )
    tokens = gather_plane(normed_two)

    up_rings = [ring(s) for s in up_shards]
    act_own, act_got = [], []
    for j in range(parts):
        own, other = up_part(pos, tokens, up_rings[j])
        act_own.append(own)
        act_got.append(send(other, YSWAP))
    activated = join_columns(pos, act_own, act_got)
    cache = place_pages(pos, page_table, kv_own, kv_got)
    return hidden_out, activated, cache


def solution(mesh):
    placed = (
        P(("dp", "mp"), None),
        P("dp", None),
        P("dp", None),
        P(("dp", "mp"), None),
        P(("dp", "mp"), None),
        P("mp", None),
    )
    planes = mesh.shape["dp"] == NZ * NY and mesh.shape["mp"] == NM
    return jax.shard_map(
        local_planes if planes else local_any,
        mesh=mesh,
        in_specs=placed,
        out_specs=(P(("dp", "mp"), None), P("dp", "mp"), P("dp", None, "mp", None, None)),
        check_vma=False,
    )
```

time: 427 us -> 281 us (0.66)
  waiting for transfers between devices: 306 us -> 56.9 us
  starting transfers between devices: 11.5 us -> 96 us
  blocking collectives: 0 us -> 67.6 us
  local copies, waits for them, and re-layouts: 59.4 us -> 1.19 us
  Pallas kernels: 0 us -> 38 us
  matrix products: 23.1 us -> 0 us
  other arithmetic: 11.5 us -> 5.39 us
    all_to_all x2 -> x3, waiting for transfers between devices: 155 us -> 1.68 us  [in_plane(): lax.all_to_all(pieces, AXES, split_axis=0, concat_axis=0, tiled=True, axi...]
    all_gather x4 -> x1, waiting for transfers between devices: 133 us -> 0.02 us  [local_planes(): lax.all_gather(normed_own, AXES, axis=0, tiled=True, axis_index_groups=PL...]
    ppermute x0 -> x41, starting transfers between devices: none -> 84 us  [send(): return lax.ppermute(value, AXES, moves)]
    all_to_all x0 -> x1, blocking collectives: none -> 67.6 us  [in_plane(): lax.all_to_all(pieces, AXES, split_axis=0, concat_axis=0, tiled=True, axi...]
    ppermute x0 -> x41, waiting for transfers between devices: none -> 55.1 us  [send(): return lax.ppermute(value, AXES, moves)]
    pallas_call x0 -> x10, Pallas kernels: none -> 38 us  [the longest x2 12.8 us: one_head(): pl.pallas_call(head_kernel, in_specs=[SMEM, SMEM, VMEM, VMEM, VMEM] + [AN...]
    dot_general x4 -> x0, matrix products: 20.9 us -> none  [the longest x1 9.16 us: local(): upper = jnp.dot(normed_two, up_w, preferred_element_type=jnp.float32)]
    all_gather x2 -> x0, local copies, waits for them, and re-layouts: 20.8 us -> none  [the longest x1 12.1 us: local(): lax.all_gather(up_bf, 'dp', axis=0, tiled=True)]
  transfers between devices with their start and end apart: 7 -> 45, of which waited for: 5 -> 18; matrix products, arithmetic and copies ran while one was open for 19% -> 0% of each run, Pallas kernels for 0% -> 13%
where the time goes in v1:
time: 281 us; the launch traced here: 280 us
  starting transfers between devices  96 us (34%)
  blocking collectives  67.6 us (24%)
  waiting for transfers between devices  56.9 us (20%)
  Pallas kernels  38 us (14%)
  between operations  14.7 us (5%)
  other arithmetic  5.39 us (2%)
    ppermute x41, starting transfers between devices, send(): return lax.ppermute(value, AXES, moves)  84 us
    all_to_all x1, blocking collectives, in_plane(): lax.all_to_all(pieces, AXES, split_axis=0, concat_axis=0, tiled=True, axi...  67.6 us
    ppermute x41, waiting for transfers between devices, send(): return lax.ppermute(value, AXES, moves)  55.1 us
    pallas_call x2, Pallas kernels, one_head(): pl.pallas_call(head_kernel, in_specs=[SMEM, SMEM, VMEM, VMEM, VMEM] + [AN...  12.8 us
    all_to_all x3, starting transfers between devices, in_plane(): lax.all_to_all(pieces, AXES, split_axis=0, concat_axis=0, tiled=True, axi...  11.9 us
    pallas_call x2, Pallas kernels, up_part(): pl.pallas_call(up_kernel, in_specs=[SMEM] + [ANY] * (10 + len(shards)), o...  10.4 us
    pallas_call x3, Pallas kernels, cast_pieces(): pl.pallas_call(cast_kernel, grid=(PLANE,), in_specs=[pl.BlockSpec((rows,...  5.82 us
    pallas_call x1, Pallas kernels, dense_norm(): pl.pallas_call(dense_kernel, in_specs=[SMEM, VMEM, VMEM] + [VMEM] * NM, o...  5.74 us
  transfers between devices with their start and end apart: 45, of which 18 were waited for; matrix products, arithmetic and copies ran while one was open for 0% of the time, Pallas kernels for 13%

profile of v1, /device:TPU:0, one launch (start us, length us, event | category | flops | bytes accessed | tf_op | source)
XLA Modules:
  0.0 279.7 jit_solution(9139127197339636643)
XLA Ops:
  15.3 67.6 %all_to_all.20 = bf16[8,64,768]{2,1,0:T(8,128)(2,1)S(1)} all-to-all(bf16[8,64,768]{2,1,0:T(8,128)(2,1)S(1)} %shard_map.85), channel_id=1, replica_groups={{0,1,2,3,4,5,6,7},{8,9,10,11,12,13,14,15},{16,17,18,19,20,21,22,23},{24..., dimensions={0} | all-to-all | bytes 1572864 | tf_op jit(solution)/shard_map/all_to_all | solution.py:131
  83.0 4.3 %collective-permute-start.1 = (bf16[512,384]{1,0:T(8,128)(2,1)S(1)}, bf16[512,384]{1,0:T(8,128)(2,1)}, u32[]{:S(2)}, u32[]{:S(2)}) collective-permute-start(bf16[512,384]{1,0:T(8,128)(2,1)S(1)} %bitcast.21), channel_id=1, source_target_pairs={{0,8},{1,9},{2,10},{3,11},{4,12},{5,13},{6,14},{7,15},{8,16},{9,17... | collective-permute-start | bytes 1179656 | tf_op jit(solution)/shard_map/ppermute | solution.py:97
  94.2 5.3 %collective-permute-start.7 = (bf16[512,384]{1,0:T(8,128)(2,1)S(1)}, bf16[512,384]{1,0:T(8,128)(2,1)}, u32[]{:S(2)}, u32[]{:S(2)}) collective-permute-start(bf16[512,384]{1,0:T(8,128)(2,1)S(1)} %bitcast.19), channel_id=1, source_target_pairs={{0,8},{1,9},{2,10},{3,11},{4,12},{5,13},{6,14},{7,15},{8,16},{9,17... | collective-permute-start | bytes 1179656 | tf_op jit(solution)/shard_map/ppermute | solution.py:97
  116.4 6.0 %collective-permute-start.8 = (bf16[512,384]{1,0:T(8,128)(2,1)}, bf16[512,384]{1,0:T(8,128)(2,1)}, u32[]{:S(2)}, u32[]{:S(2)}) collective-permute-start(bf16[512,384]{1,0:T(8,128)(2,1)} %collective-permute-done.7.rest_1_), channel_id=1, source_target_pairs={{0,8},{1,9},{2,10},{3,11},{4,12},{5,13},{6,14},{7,15},{8,16},{9,17... | collective-permute-start | bytes 1179656 | tf_op jit(solution)/shard_map/ppermute | solution.py:97
  122.3 3.9 %collective-permute-start.3 = (bf16[512,384]{1,0:T(8,128)(2,1)}, bf16[512,384]{1,0:T(8,128)(2,1)}, u32[]{:S(2)}, u32[]{:S(2)}) collective-permute-start(bf16[512,384]{1,0:T(8,128)(2,1)} %collective-permute-done.2.rest_2_), channel_id=1, source_target_pairs={{0,8},{1,9},{2,10},{3,11},{4,12},{5,13},{6,14},{7,15},{8,16},{9,17... | collective-permute-start | bytes 1179656 | tf_op jit(solution)/shard_map/ppermute | solution.py:97
  135.3 4.2 %all-to-all-start.2 = ((bf16[8,64,512]{2,1,0:T(8,128)(2,1)}), bf16[8,64,512]{2,1,0:T(8,128)(2,1)S(1)}, u32[]{:S(2)}, u32[]{:S(2)}) async-start(bf16[8,64,512]{2,1,0:T(8,128)(2,1)} %shard_map.89), calls=%async_computation.2 | async-start | bytes 1048576 | tf_op jit(solution)/shard_map/all_to_all | solution.py:131
  139.4 5.0 %collective-permute-start.9 = (bf16[512,384]{1,0:T(8,128)(2,1)}, bf16[512,384]{1,0:T(8,128)(2,1)S(1)}, u32[]{:S(2)}, u32[]{:S(2)}) collective-permute-start(bf16[512,384]{1,0:T(8,128)(2,1)} %collective-permute-done.8.rest_2_), channel_id=1, source_target_pairs={{0,8},{1,9},{2,10},{3,11},{4,12},{5,13},{6,14},{7,15},{8,16},{9,17... | collective-permute-start | bytes 1179656 | tf_op jit(solution)/shard_map/ppermute | solution.py:97
  144.5 4.8 %collective-permute-start.31 = (bf16[512,512]{1,0:T(8,128)(2,1)S(1)}, bf16[512,512]{1,0:T(8,128)(2,1)}, u32[]{:S(2)}, u32[]{:S(2)}) collective-permute-start(bf16[512,512]{1,0:T(8,128)(2,1)S(1)} %bitcast.12), channel_id=1, source_target_pairs={{0,8},{1,9},{2,10},{3,11},{4,12},{5,13},{6,14},{7,15},{8,16},{9,17... | collective-permute-start | bytes 1572872 | tf_op jit(solution)/shard_map/ppermute | solution.py:97
  154.2 5.1 %collective-permute-start.25 = (bf16[512,512]{1,0:T(8,128)(2,1)S(1)}, bf16[512,512]{1,0:T(8,128)(2,1)}, u32[]{:S(2)}, u32[]{:S(2)}) collective-permute-start(bf16[512,512]{1,0:T(8,128)(2,1)S(1)} %bitcast.15), channel_id=1, source_target_pairs={{0,8},{1,9},{2,10},{3,11},{4,12},{5,13},{6,14},{7,15},{8,16},{9,17... | collective-permute-start | bytes 1572872 | tf_op jit(solution)/shard_map/ppermute | solution.py:97
  159.7 6.3 %shard_map.86 = (bf16[768,128]{1,0:T(8,128)(2,1)S(1)}, bf16[3,2,128,128]{3,2,1,0:T(8,128)(2,1)S(1)}, bf16[3,2,128,128]{3,2,1,0:T(8,128)(2,1)S(1)}) custom-call(s32[3]{0:T(128)S(1)} %pad_add_fusion.1.pos, f32[1]{0:T(128)} %bitcast.3.slope, s32[2,1,384]{2,1,0:T(1,128)S(1)} %broadcast_in_dim.8.seg_rows, s32[2,384,1]{2,1,0:T(8,128)S(1)} %copy.11.seg_cols, ...), custom_call_target="tpu_custom_call" | custom-call | flops 1207959552 | bytes 4718592 | tf_op jit(solution)/shard_map/pallas_call | solution.py:205
  166.0 6.5 %shard_map.87 = (bf16[768,128]{1,0:T(8,128)(2,1)S(1)}, bf16[3,2,128,128]{3,2,1,0:T(8,128)(2,1)S(1)}, bf16[3,2,128,128]{3,2,1,0:T(8,128)(2,1)S(1)}) custom-call(s32[3]{0:T(128)S(1)} %pad_add_fusion.1.pos, f32[1]{0:T(128)} %bitcast.6.slope, s32[2,1,384]{2,1,0:T(1,128)S(1)} %broadcast_in_dim.8.seg_rows, s32[2,384,1]{2,1,0:T(8,128)S(1)} %copy.11.seg_cols, ...), custom_call_target="tpu_custom_call" | custom-call | flops 1207959552 | bytes 4718592 | tf_op jit(solution)/shard_map/pallas_call | solution.py:205
  173.8 4.6 %collective-permute-start.32 = (bf16[512,512]{1,0:T(8,128)(2,1)}, bf16[512,512]{1,0:T(8,128)(2,1)S(1)}, u32[]{:S(2)}, u32[]{:S(2)}) collective-permute-start(bf16[512,512]{1,0:T(8,128)(2,1)} %collective-permute-done.31.rest_11_), channel_id=1, source_target_pairs={{0,8},{1,9},{2,10},{3,11},{4,12},{5,13},{6,14},{7,15},{8,16},{9,17... | collective-permute-start | bytes 1572872 | tf_op jit(solution)/shard_map/ppermute | solution.py:97
  179.2 4.2 %all-to-all-start.1 = ((bf16[8,96,256]{2,1,0:T(8,128)(2,1)}), bf16[8,96,256]{2,1,0:T(8,128)(2,1)S(1)}, u32[]{:S(2)}, u32[]{:S(2)}) async-start(bf16[8,96,256]{2,1,0:T(8,128)(2,1)} %bitcast.8), calls=%async_computation.1 | async-start | bytes 786432 | tf_op jit(solution)/shard_map/all_to_all | solution.py:131
  184.8 5.3 %collective-permute-start.26 = (bf16[512,512]{1,0:T(8,128)(2,1)}, bf16[512,512]{1,0:T(8,128)(2,1)}, u32[]{:S(2)}, u32[]{:S(2)}) collective-permute-start(bf16[512,512]{1,0:T(8,128)(2,1)} %collective-permute-done.25.rest_11_), channel_id=1, source_target_pairs={{0,8},{1,9},{2,10},{3,11},{4,12},{5,13},{6,14},{7,15},{8,16},{9,17... | collective-permute-start | bytes 1572872 | tf_op jit(solution)/shard_map/ppermute | solution.py:97
  191.8 5.7 %shard_map.88 = (bf16[96,2048]{1,0:T(8,128)(2,1)}, bf16[96,2048]{1,0:T(8,128)(2,1)S(1)}) custom-call(s32[3]{0:T(128)S(1)} %pad_add_fusion.1.pos, bf16[96,2048]{1,0:T(8,128)(2,1)S(1)} %copy-done.1, bf16[8,96,256]{2,1,0:T(8,128)(2,1)S(1)} %all-to-all-done.1.ctx, bf16[512,2048]{1,0:T(8,128)(2,1)} %rest_0_.1, bf16[512,2048]{1,0:T(8,128)(2,1)} %collective-permute-done.13.rest_1_, ...), custom_call_target="tpu_custom_call" | custom-call | tf_op jit(solution)/shard_map/pallas_call | solution.py:235
  200.7 4.6 %collective-permute-start.33 = (bf16[512,512]{1,0:T(8,128)(2,1)S(1)}, bf16[512,512]{1,0:T(8,128)(2,1)S(1)}, u32[]{:S(2)}, u32[]{:S(2)}) collective-permute-start(bf16[512,512]{1,0:T(8,128)(2,1)S(1)} %collective-permute-done.32.rest_12_), channel_id=1, source_target_pairs={{0,8},{1,9},{2,10},{3,11},{4,12},{5,13},{6,14},{7,15},{8,16},{9,17... | collective-permute-start | bytes 1572872 | tf_op jit(solution)/shard_map/ppermute | solution.py:97
  211.0 4.0 %collective-permute-done.29.rest_15_ = bf16[512,512]{1,0:T(8,128)(2,1)S(1)} collective-permute-done((bf16[512,512]{1,0:T(8,128)(2,1)}, bf16[512,512]{1,0:T(8,128)(2,1)S(1)}, u32[]{:S(2)}, u32[]{:S(2)}) %collective-permute-start.29) | collective-permute-done | bytes 524320 | tf_op jit(solution)/shard_map/ppermute | solution.py:97
  216.8 7.5 %collective-permute-done.36.rest_16_ = bf16[512,512]{1,0:T(8,128)(2,1)S(1)} collective-permute-done((bf16[512,512]{1,0:T(8,128)(2,1)}, bf16[512,512]{1,0:T(8,128)(2,1)S(1)}, u32[]{:S(2)}, u32[]{:S(2)}) %collective-permute-start.36) | collective-permute-done | bytes 524320 | tf_op jit(solution)/shard_map/ppermute | solution.py:97
  224.3 4.4 %collective-permute-start.27 = (bf16[512,512]{1,0:T(8,128)(2,1)}, bf16[512,512]{1,0:T(8,128)(2,1)S(1)}, u32[]{:S(2)}, u32[]{:S(2)}) collective-permute-start(bf16[512,512]{1,0:T(8,128)(2,1)} %collective-permute-done.26.rest_12_), channel_id=1, source_target_pairs={{0,8},{1,9},{2,10},{3,11},{4,12},{5,13},{6,14},{7,15},{8,16},{9,17... | collective-permute-start | bytes 1572872 | tf_op jit(solution)/shard_map/ppermute | solution.py:97
  231.6 5.3 %shard_map.92 = (bf16[384,512]{1,0:T(8,128)(2,1)S(1)}, bf16[384,512]{1,0:T(8,128)(2,1)S(1)}) custom-call(s32[3]{0:T(128)S(1)} %pad_add_fusion.1.pos, bf16[96,2048]{1,0:T(8,128)(2,1)S(1)} %get-tuple-element.18.rest_0_, bf16[96,2048]{1,0:T(8,128)(2,1)S(1)} %collective-permute-done.16.rest_1_, bf16[96,2048]{1,0:T(8,128)(2,1)S(1)} %collective-permute-done.17.rest_2_, ...), custom_call_target="tpu_custom_call" | custom-call | flops 1610612736 | bytes 5242880 | tf_op jit(solution)/shard_map/pallas_call | solution.py:273
  237.4 3.5 %collective-permute-done.27.rest_13_ = bf16[512,512]{1,0:T(8,128)(2,1)S(1)} collective-permute-done((bf16[512,512]{1,0:T(8,128)(2,1)}, bf16[512,512]{1,0:T(8,128)(2,1)S(1)}, u32[]{:S(2)}, u32[]{:S(2)}) %collective-permute-start.27) | collective-permute-done | bytes 524320 | tf_op jit(solution)/shard_map/ppermute | solution.py:97
  240.9 3.8 %collective-permute-done.30.rest_16_ = bf16[512,512]{1,0:T(8,128)(2,1)S(1)} collective-permute-done((bf16[512,512]{1,0:T(8,128)(2,1)S(1)}, bf16[512,512]{1,0:T(8,128)(2,1)S(1)}, u32[]{:S(2)}, u32[]{:S(2)}) %collective-permute-start.30) | collective-permute-done | bytes 524320 | tf_op jit(solution)/shard_map/ppermute | solution.py:97
  245.5 5.1 %shard_map.90 = (bf16[384,512]{1,0:T(8,128)(2,1)S(1)}, bf16[384,512]{1,0:T(8,128)(2,1)S(1)}) custom-call(s32[3]{0:T(128)S(1)} %pad_add_fusion.1.pos, bf16[96,2048]{1,0:T(8,128)(2,1)S(1)} %get-tuple-element.18.rest_0_, bf16[96,2048]{1,0:T(8,128)(2,1)S(1)} %collective-permute-done.16.rest_1_, bf16[96,2048]{1,0:T(8,128)(2,1)S(1)} %collective-permute-done.17.rest_2_, ...), custom_call_target="tpu_custom_call" | custom-call | flops 1610612736 | bytes 5242880 | tf_op jit(solution)/shard_map/pallas_call | solution.py:273
  253.1 13.9 %collective-permute-done.39.rest_2_ = bf16[3,2,128,128]{3,2,1,0:T(8,128)(2,1)S(1)} collective-permute-done((bf16[3,2,128,128]{3,2,1,0:T(8,128)(2,1)S(1)}, bf16[3,2,128,128]{3,2,1,0:T(8,128)(2,1)S(1)}, u32[]{:S(2)}, u32[]{:S(2)}) %collective-permute-start.39) | collective-permute-done | bytes 196640 | tf_op jit(solution)/shard_map/ppermute | solution.py:97
  (123 shorter events, 74.2 us)
Async XLA Ops:
  7.2 152.5 %all-gather.2.cloned.1.call-start = ((), (), s32[]{:S(2)}) async-start(), calls=%async_computation.4 | async-start | bytes 3538944 | tf_op jit(solution)/shard_map/all_gather | solution.py:363
  11.8 97.0 %collective-permute-start.14 = (bf16[512,2048]{1,0:T(8,128)(2,1)}, bf16[512,2048]{1,0:T(8,128)(2,1)}, u32[]{:S(2)}, u32[]{:S(2)}) collective-permute-start(bf16[512,2048]{1,0:T(8,128)(2,1)} %rest_0_.1), channel_id=1, source_target_pairs={{0,2},{1,3},{2,0},{3,1},{4,6},{5,7},{6,4},{7,5},{8,10},{9,11},{10,... | collective-permute-start | bytes 6291464 | tf_op jit(solution)/shard_map/ppermute | solution.py:97
  88.6 18.9 %collective-permute-start.10 = (bf16[512,384]{1,0:T(8,128)(2,1)S(1)}, bf16[512,384]{1,0:T(8,128)(2,1)S(1)}, u32[]{:S(2)}, u32[]{:S(2)}) collective-permute-start(bf16[512,384]{1,0:T(8,128)(2,1)S(1)} %bitcast.18), channel_id=1, source_target_pairs={{8,0},{9,1},{10,2},{11,3},{12,4},{13,5},{14,6},{15,7},{16,8},{17,9... | collective-permute-start | bytes 1179656 | tf_op jit(solution)/shard_map/ppermute | solution.py:97
  93.5 91.2 %collective-permute-start.13 = (bf16[512,2048]{1,0:T(8,128)(2,1)}, bf16[512,2048]{1,0:T(8,128)(2,1)}, u32[]{:S(2)}, u32[]{:S(2)}) collective-permute-start(bf16[512,2048]{1,0:T(8,128)(2,1)} %rest_0_.1), channel_id=1, source_target_pairs={{0,1},{1,0},{2,3},{3,2},{4,5},{5,4},{6,7},{7,6},{8,9},{9,8},{10,11... | collective-permute-start | bytes 6291464 | tf_op jit(solution)/shard_map/ppermute | solution.py:97
  94.2 20.9 %collective-permute-start.7 = (bf16[512,384]{1,0:T(8,128)(2,1)S(1)}, bf16[512,384]{1,0:T(8,128)(2,1)}, u32[]{:S(2)}, u32[]{:S(2)}) collective-permute-start(bf16[512,384]{1,0:T(8,128)(2,1)S(1)} %bitcast.19), channel_id=1, source_target_pairs={{0,8},{1,9},{2,10},{3,11},{4,12},{5,13},{6,14},{7,15},{8,16},{9,17... | collective-permute-start | bytes 1179656 | tf_op jit(solution)/shard_map/ppermute | solution.py:97
  108.7 81.4 %collective-permute-start.15 = (bf16[512,2048]{1,0:T(8,128)(2,1)}, bf16[512,2048]{1,0:T(8,128)(2,1)}, u32[]{:S(2)}, u32[]{:S(2)}) collective-permute-start(bf16[512,2048]{1,0:T(8,128)(2,1)} %collective-permute-done.14.rest_2_), channel_id=1, source_target_pairs={{0,1},{1,0},{2,3},{3,2},{4,5},{5,4},{6,7},{7,6},{8,9},{9,8},{10,11... | collective-permute-start | bytes 6291464 | tf_op jit(solution)/shard_map/ppermute | solution.py:97
  111.5 23.7 %all-to-all-start.3 = ((bf16[8,64,512]{2,1,0:T(8,128)(2,1)}), bf16[8,64,512]{2,1,0:T(8,128)(2,1)S(1)}, u32[]{:S(2)}, u32[]{:S(2)}) async-start(bf16[8,64,512]{2,1,0:T(8,128)(2,1)} %shard_map.91), calls=%async_computation.3 | async-start | bytes 1048576 | tf_op jit(solution)/shard_map/all_to_all | solution.py:131
  122.3 17.1 %collective-permute-start.3 = (bf16[512,384]{1,0:T(8,128)(2,1)}, bf16[512,384]{1,0:T(8,128)(2,1)}, u32[]{:S(2)}, u32[]{:S(2)}) collective-permute-start(bf16[512,384]{1,0:T(8,128)(2,1)} %collective-permute-done.2.rest_2_), channel_id=1, source_target_pairs={{0,8},{1,9},{2,10},{3,11},{4,12},{5,13},{6,14},{7,15},{8,16},{9,17... | collective-permute-start | bytes 1179656 | tf_op jit(solution)/shard_map/ppermute | solution.py:97
  131.3 19.8 %collective-permute-start.12 = (bf16[512,384]{1,0:T(8,128)(2,1)}, bf16[512,384]{1,0:T(8,128)(2,1)}, u32[]{:S(2)}, u32[]{:S(2)}) collective-permute-start(bf16[512,384]{1,0:T(8,128)(2,1)} %collective-permute-done.11.rest_5_), channel_id=1, source_target_pairs={{8,0},{9,1},{10,2},{11,3},{12,4},{13,5},{14,6},{15,7},{16,8},{17,9... | collective-permute-start | bytes 1179656 | tf_op jit(solution)/shard_map/ppermute | solution.py:97
  135.3 17.1 %all-to-all-start.2 = ((bf16[8,64,512]{2,1,0:T(8,128)(2,1)}), bf16[8,64,512]{2,1,0:T(8,128)(2,1)S(1)}, u32[]{:S(2)}, u32[]{:S(2)}) async-start(bf16[8,64,512]{2,1,0:T(8,128)(2,1)} %shard_map.89), calls=%async_computation.2 | async-start | bytes 1048576 | tf_op jit(solution)/shard_map/all_to_all | solution.py:131
  144.5 28.0 %collective-permute-start.31 = (bf16[512,512]{1,0:T(8,128)(2,1)S(1)}, bf16[512,512]{1,0:T(8,128)(2,1)}, u32[]{:S(2)}, u32[]{:S(2)}) collective-permute-start(bf16[512,512]{1,0:T(8,128)(2,1)S(1)} %bitcast.12), channel_id=1, source_target_pairs={{0,8},{1,9},{2,10},{3,11},{4,12},{5,13},{6,14},{7,15},{8,16},{9,17... | collective-permute-start | bytes 1572872 | tf_op jit(solution)/shard_map/ppermute | solution.py:97
  151.1 22.7 %collective-permute-start.34 = (bf16[512,512]{1,0:T(8,128)(2,1)S(1)}, bf16[512,512]{1,0:T(8,128)(2,1)}, u32[]{:S(2)}, u32[]{:S(2)}) collective-permute-start(bf16[512,512]{1,0:T(8,128)(2,1)S(1)} %bitcast.13), channel_id=1, source_target_pairs={{8,0},{9,1},{10,2},{11,3},{12,4},{13,5},{14,6},{15,7},{16,8},{17,9... | collective-permute-start | bytes 1572872 | tf_op jit(solution)/shard_map/ppermute | solution.py:97
  154.2 29.3 %collective-permute-start.25 = (bf16[512,512]{1,0:T(8,128)(2,1)S(1)}, bf16[512,512]{1,0:T(8,128)(2,1)}, u32[]{:S(2)}, u32[]{:S(2)}) collective-permute-start(bf16[512,512]{1,0:T(8,128)(2,1)S(1)} %bitcast.15), channel_id=1, source_target_pairs={{0,8},{1,9},{2,10},{3,11},{4,12},{5,13},{6,14},{7,15},{8,16},{9,17... | collective-permute-start | bytes 1572872 | tf_op jit(solution)/shard_map/ppermute | solution.py:97
  172.5 25.6 %collective-permute-start.28 = (bf16[512,512]{1,0:T(8,128)(2,1)S(1)}, bf16[512,512]{1,0:T(8,128)(2,1)}, u32[]{:S(2)}, u32[]{:S(2)}) collective-permute-start(bf16[512,512]{1,0:T(8,128)(2,1)S(1)} %bitcast.16), channel_id=1, source_target_pairs={{8,0},{9,1},{10,2},{11,3},{12,4},{13,5},{14,6},{15,7},{16,8},{17,9... | collective-permute-start | bytes 1572872 | tf_op jit(solution)/shard_map/ppermute | solution.py:97
  173.8 25.5 %collective-permute-start.32 = (bf16[512,512]{1,0:T(8,128)(2,1)}, bf16[512,512]{1,0:T(8,128)(2,1)S(1)}, u32[]{:S(2)}, u32[]{:S(2)}) collective-permute-start(bf16[512,512]{1,0:T(8,128)(2,1)} %collective-permute-done.31.rest_11_), channel_id=1, source_target_pairs={{0,8},{1,9},{2,10},{3,11},{4,12},{5,13},{6,14},{7,15},{8,16},{9,17... | collective-permute-start | bytes 1572872 | tf_op jit(solution)/shard_map/ppermute | solution.py:97
  183.4 17.2 %collective-permute-start.35 = (bf16[512,512]{1,0:T(8,128)(2,1)}, bf16[512,512]{1,0:T(8,128)(2,1)}, u32[]{:S(2)}, u32[]{:S(2)}) collective-permute-start(bf16[512,512]{1,0:T(8,128)(2,1)} %collective-permute-done.34.rest_14_), channel_id=1, source_target_pairs={{8,0},{9,1},{10,2},{11,3},{12,4},{13,5},{14,6},{15,7},{16,8},{17,9... | collective-permute-start | bytes 1572872 | tf_op jit(solution)/shard_map/ppermute | solution.py:97
  184.8 20.5 %collective-permute-start.26 = (bf16[512,512]{1,0:T(8,128)(2,1)}, bf16[512,512]{1,0:T(8,128)(2,1)}, u32[]{:S(2)}, u32[]{:S(2)}) collective-permute-start(bf16[512,512]{1,0:T(8,128)(2,1)} %collective-permute-done.25.rest_11_), channel_id=1, source_target_pairs={{0,8},{1,9},{2,10},{3,11},{4,12},{5,13},{6,14},{7,15},{8,16},{9,17... | collective-permute-start | bytes 1572872 | tf_op jit(solution)/shard_map/ppermute | solution.py:97
  198.1 17.0 %collective-permute-start.29 = (bf16[512,512]{1,0:T(8,128)(2,1)}, bf16[512,512]{1,0:T(8,128)(2,1)S(1)}, u32[]{:S(2)}, u32[]{:S(2)}) collective-permute-start(bf16[512,512]{1,0:T(8,128)(2,1)} %collective-permute-done.28.rest_14_), channel_id=1, source_target_pairs={{8,0},{9,1},{10,2},{11,3},{12,4},{13,5},{14,6},{15,7},{16,8},{17,9... | collective-permute-start | bytes 1572872 | tf_op jit(solution)/shard_map/ppermute | solution.py:97
  205.3 19.0 %collective-permute-start.36 = (bf16[512,512]{1,0:T(8,128)(2,1)}, bf16[512,512]{1,0:T(8,128)(2,1)S(1)}, u32[]{:S(2)}, u32[]{:S(2)}) collective-permute-start(bf16[512,512]{1,0:T(8,128)(2,1)} %collective-permute-done.35.rest_15_), channel_id=1, source_target_pairs={{8,0},{9,1},{10,2},{11,3},{12,4},{13,5},{14,6},{15,7},{16,8},{17,9... | collective-permute-start | bytes 1572872 | tf_op jit(solution)/shard_map/ppermute | solution.py:97
  206.8 17.5 %collective-permute-start.16 = (bf16[96,2048]{1,0:T(8,128)(2,1)S(1)}, bf16[96,2048]{1,0:T(8,128)(2,1)S(1)}, u32[]{:S(2)}, u32[]{:S(2)}) collective-permute-start(bf16[96,2048]{1,0:T(8,128)(2,1)S(1)} %get-tuple-element.18.rest_0_), channel_id=1, source_target_pairs={{0,1},{1,0},{2,3},{3,2},{4,5},{5,4},{6,7},{7,6},{8,9},{9,8},{10,11... | collective-permute-start | bytes 1179656 | tf_op jit(solution)/shard_map/ppermute | solution.py:97
  224.3 16.6 %collective-permute-start.27 = (bf16[512,512]{1,0:T(8,128)(2,1)}, bf16[512,512]{1,0:T(8,128)(2,1)S(1)}, u32[]{:S(2)}, u32[]{:S(2)}) collective-permute-start(bf16[512,512]{1,0:T(8,128)(2,1)} %collective-permute-done.26.rest_12_), channel_id=1, source_target_pairs={{0,8},{1,9},{2,10},{3,11},{4,12},{5,13},{6,14},{7,15},{8,16},{9,17... | collective-permute-start | bytes 1572872 | tf_op jit(solution)/shard_map/ppermute | solution.py:97
  237.0 34.0 %collective-permute-start.38 = (bf16[384,512]{1,0:T(8,128)(2,1)S(1)}, bf16[384,512]{1,0:T(8,128)(2,1)S(1)}, u32[]{:S(2)}, u32[]{:S(2)}) collective-permute-start(bf16[384,512]{1,0:T(8,128)(2,1)S(1)} %get-tuple-element.22), channel_id=1, source_target_pairs={{0,4},{1,5},{2,6},{3,7},{4,0},{5,1},{6,2},{7,3},{8,12},{9,13},{10,... | collective-permute-start | bytes 1179656 | tf_op jit(solution)/shard_map/ppermute | solution.py:97
  250.6 20.4 %collective-permute-start.37 = (bf16[384,512]{1,0:T(8,128)(2,1)S(1)}, bf16[384,512]{1,0:T(8,128)(2,1)S(1)}, u32[]{:S(2)}, u32[]{:S(2)}) collective-permute-start(bf16[384,512]{1,0:T(8,128)(2,1)S(1)} %get-tuple-element.21), channel_id=1, source_target_pairs={{0,4},{1,5},{2,6},{3,7},{4,0},{5,1},{6,2},{7,3},{8,12},{9,13},{10,... | collective-permute-start | bytes 1179656 | tf_op jit(solution)/shard_map/ppermute | solution.py:97
  252.7 16.8 %collective-permute-start.40 = (bf16[3,2,128,128]{3,2,1,0:T(8,128)(2,1)S(1)}, bf16[3,2,128,128]{3,2,1,0:T(8,128)(2,1)S(1)}, u32[]{:S(2)}, u32[]{:S(2)}) collective-permute-start(bf16[3,2,128,128]{3,2,1,0:T(8,128)(2,1)S(1)} %copy-done.11), channel_id=1, source_target_pairs={{0,4},{1,5},{2,6},{3,7},{4,0},{5,1},{6,2},{7,3},{8,12},{9,13},{10,... | collective-permute-start | bytes 589832 | tf_op jit(solution)/shard_map/ppermute | solution.py:97
  (37 other events, 612.5 us)
Sparse Core Ops, SparseCore 0:
  11.9 47.6 all-gather.1

commit v2 on v0

v2 whole, which is shorter than its diff:
```python
import functools

import jax
import jax.numpy as jnp
from jax import lax
from jax.experimental import pallas as pl
from jax.experimental.pallas import tpu as pltpu
from jax.sharding import PartitionSpec as P

H = 16
HD = 128
PAGE = 128
AXES = ("dp", "mp")
BF = jnp.bfloat16
F32 = jnp.float32
VMEM_LIMIT = 56 * 1024 * 1024


def layer_norm(values):
    mean_val = jnp.mean(values, -1, keepdims=True)
    centered = values - mean_val
    variance = jnp.mean(centered * centered, -1, keepdims=True)
    return centered * lax.rsqrt(variance + 1e-05)


def attend(normed, qkv_w, segment, table, mp_index):
    group_rows = normed.shape[0]
    heads_dev = qkv_w.shape[1] // (3 * HD)
    joined = jnp.dot(normed, qkv_w, preferred_element_type=F32).astype(BF)
    joined = joined.reshape(group_rows, heads_dev, 3, HD)
    query = joined[:, :, 0]
    keys = joined[:, :, 1]
    vals = joined[:, :, 2]
    head_ids = mp_index * heads_dev + jnp.arange(heads_dev)
    slopes = jnp.exp2(-8.0 * (head_ids + 1).astype(F32) / H)
    positions = jnp.arange(group_rows)
    distance = (positions[:, None] - positions[None, :]).astype(F32)
    allowed = (segment[:, None] == segment[None, :]) & (distance >= 0)
    scores = jnp.einsum("thd,shd->hts", query, keys, preferred_element_type=F32) / jnp.sqrt(F32(HD))
    scores = scores - slopes[:, None, None] * distance[None]
    scores = jnp.where(allowed[None], scores, -jnp.inf)
    probs = jax.nn.softmax(scores, axis=-1).astype(BF)
    context = jnp.einsum("hts,shd->thd", probs, vals, preferred_element_type=F32).astype(BF)
    context = context.reshape(group_rows, heads_dev * HD)
    key_vals = jnp.stack([keys, vals], 1)
    pages_here = group_rows // PAGE
    key_vals = key_vals.reshape(pages_here, PAGE, 2, heads_dev, HD).transpose(0, 2, 3, 1, 4)
    cache = jnp.zeros((pages_here, 2, heads_dev, PAGE, HD), BF).at[table].set(key_vals)
    return context, cache


def local_any(hidden_in, segment_ids, page_table, qkv_master, up_master, dense_weight):
    mp_index = lax.axis_index("mp")

    def columns(master):
        mine = lax.all_to_all(master.astype(BF), "mp", split_axis=1, concat_axis=0, tiled=True)
        return lax.all_gather(mine, "dp", axis=0, tiled=True)

    qkv_w = columns(qkv_master)
    up_w = columns(up_master)
    normed_own = layer_norm(hidden_in.astype(F32)).astype(BF)
    normed = lax.all_gather(normed_own, "mp", axis=0, tiled=True)
    context, cache = attend(normed, qkv_w, segment_ids[0], page_table[0], mp_index)
    term = jnp.dot(context, dense_weight, preferred_element_type=F32).astype(BF)
    share = lax.psum_scatter(term, "mp", scatter_dimension=0, tiled=True).astype(F32)
    stream_own = hidden_in.astype(F32) + share
    normed_two = lax.all_gather(layer_norm(stream_own).astype(BF), "mp", axis=0, tiled=True)
    upper = jnp.dot(normed_two, up_w, preferred_element_type=F32)
    activated = jax.nn.gelu(upper, approximate=True).astype(BF)
    return stream_own.astype(BF), activated, cache


NZ, NY, NM = 4, 2, 4
PLANE = NY * NM
HEADS = H // PLANE


def pairs(move):
    out = []
    for z in range(NZ):
        for y in range(NY):
            for m in range(NM):
                to = move(z, y, m)
                if to is not None:
                    out.append(((z * NY + y) * NM + m, (to[0] * NY + to[1]) * NM + to[2]))
    return out


CORE = pairs(lambda z, y, m: (z, y, m ^ 1))
XSWAP = pairs(lambda z, y, m: (z, y, m ^ 2))
YSWAP = pairs(lambda z, y, m: (z, y ^ 1, m))
ZSWAP = pairs(lambda z, y, m: (z ^ 1, y, m))
PLANES = [[z * PLANE + i for i in range(PLANE)] for z in range(NZ)]
QUADS = [[z * PLANE + 2 * i + c for i in range(PLANE // 2)] for z in range(NZ) for c in range(2)]


def send(value, moves):
    return lax.ppermute(value, AXES, moves)


def window(*values):
    return lax.optimization_barrier(values)


def params(**more):
    return pltpu.CompilerParams(vmem_limit_bytes=VMEM_LIMIT, **more)


ANY = pl.BlockSpec(memory_space=pltpu.HBM)
SMEM = pl.BlockSpec(memory_space=pltpu.SMEM)
VMEM = pl.BlockSpec(memory_space=pltpu.VMEM)


def cast_pieces(master):
    rows, cols = master.shape
    width = cols // PLANE // 2

    def kernel(src, dst):
        for p in range(PLANE):
            for part in range(2):
                start = ((2 * (p % NM) + p // NM) * 2 + part) * width
                piece = src[:, start : start + width].astype(BF)
                for z in range(part, NZ, 2):
                    dst[z * PLANE + p] = piece

    return pl.pallas_call(
        kernel,
        in_specs=[VMEM],
        out_specs=VMEM,
        out_shape=jax.ShapeDtypeStruct((NZ * PLANE, rows, width), BF),
        compiler_params=params(),
    )(master)


def pack_kernel(*refs):
    *parts, out = refs
    at = 0
    for part in parts:
        out[at : at + part.shape[0]] = part[...]
        at += part.shape[0]


def pack_rows(*parts):
    rows = sum(part.shape[0] for part in parts)
    return pl.pallas_call(
        pack_kernel,
        in_specs=[VMEM] * len(parts),
        out_specs=VMEM,
        out_shape=jax.ShapeDtypeStruct((rows, parts[0].shape[1]), BF),
        compiler_params=params(),
    )(*parts)


def norm_kernel(hidden, out):
    out[...] = layer_norm(hidden[...].astype(F32)).astype(BF)


def norm_rows(hidden):
    return pl.pallas_call(
        norm_kernel,
        in_specs=[VMEM],
        out_specs=VMEM,
        out_shape=jax.ShapeDtypeStruct(hidden.shape, BF),
        compiler_params=params(),
    )(hidden)


def to_all(pieces):
    mine = lax.all_to_all(pieces, AXES, split_axis=0, concat_axis=0, tiled=True)
    return mine.reshape(-1, mine.shape[2])


def in_plane(pieces):
    return lax.all_to_all(pieces, AXES, split_axis=0, concat_axis=0, tiled=True, axis_index_groups=PLANES)


def token_copies(y, m, mine, other, xbuf, sem):
    share = mine.shape[0] // NM
    half = share // 2
    place = [(0, 0, 0, share), (1, 0, 0, share), (0, 2, 0, share), (1, 2, 0, half), (1, 2, half, half)]
    copies = []
    for side, src in ((0, mine), (1, other)):
        at = 0
        for dy, dm, extra, rows in place:
            first = pl.multiple_of(((y ^ dy) * NM + (m ^ dm ^ side)) * share + extra, 16)
            copies.append(
                pltpu.make_async_copy(
                    src.at[pl.ds(at, rows)], xbuf.at[pl.ds(first, rows)], sem.at[len(copies)]
                )
            )
            at += rows
    return copies


TOKEN_COPIES = 10


def head_kernel(pos, slope, seg_rows, seg_cols, mine, other, w_own, w_got, ctx, kv_own, kv_other, xbuf, wbuf, xsem, wsem):
    z, y, m = pos[0], pos[1], pos[2]
    copies = [
        pltpu.make_async_copy(w_own, wbuf.at[z % 2], wsem.at[0]),
        pltpu.make_async_copy(w_got, wbuf.at[1 - z % 2], wsem.at[1]),
    ] + token_copies(y, m, mine, other, xbuf, xsem)
    for copy in copies:
        copy.start()
    group = xbuf.shape[0] // NY
    here = lax.broadcasted_iota(jnp.int32, (group, group), 0)
    there = lax.broadcasted_iota(jnp.int32, (group, group), 1)
    distance = here - there
    away = distance.astype(F32)
    for copy in copies:
        copy.wait()
    for g, kv in ((0, kv_own), (1, kv_other)):
        first = pl.multiple_of((y ^ g) * group, group)
        rows = pl.ds(first, group)
        allowed = (seg_cols[g] == seg_rows[g]) & (distance >= 0)
        for h in range(HEADS):
            joined = jnp.dot(xbuf[rows, :], wbuf[h], preferred_element_type=F32).astype(BF)
            query, keys, vals = (joined[:, i * HD : (i + 1) * HD] for i in range(3))
            scores = lax.dot_general(query, keys, (((1,), (1,)), ((), ())), preferred_element_type=F32)
            scores = scores * (1.0 / HD**0.5) - slope[h] * away
            scores = jnp.where(allowed, scores, -jnp.inf)
            top = jnp.max(scores, -1, keepdims=True)
            raised = jnp.exp(scores - top)
            probs = (raised / jnp.sum(raised, -1, keepdims=True)).astype(BF)
            ctx[rows, h * HD : (h + 1) * HD] = jnp.dot(probs, vals, preferred_element_type=F32).astype(BF)
            for b in range(group // PAGE):
                kv[b, 0, h] = keys[b * PAGE : (b + 1) * PAGE]
                kv[b, 1, h] = vals[b * PAGE : (b + 1) * PAGE]


def two_heads(pos, slope, seg_rows, seg_cols, tokens, w_own, w_got):
    count, depth = 2 * tokens[0].shape[0], tokens[0].shape[1]
    width = w_own.shape[1]
    kv_shape = jax.ShapeDtypeStruct((count // NY // PAGE, 2, HEADS, PAGE, HD), BF)
    return pl.pallas_call(
        head_kernel,
        in_specs=[SMEM, SMEM, VMEM, VMEM] + [ANY] * 4,
        out_specs=[VMEM, VMEM, VMEM],
        out_shape=[jax.ShapeDtypeStruct((count, HEADS * HD), BF), kv_shape, kv_shape],
        scratch_shapes=[
            pltpu.VMEM((count, depth), BF),
            pltpu.VMEM((HEADS, depth, width), BF),
            pltpu.SemaphoreType.DMA((TOKEN_COPIES,)),
            pltpu.SemaphoreType.DMA((2,)),
        ],
        compiler_params=params(),
    )(pos, slope, seg_rows, seg_cols, *tokens, w_own, w_got)


def dense_kernel(pos, hidden, ctx, *rest):
    blocks = rest[:NM]
    out, normed = rest[NM:]
    y, m = pos[1], pos[2]
    half = blocks[0].shape[0] // 2
    total = None
    for r in range(NM):
        owner = m ^ r
        flip = y if r >= 2 else 0
        near = jnp.dot(ctx[flip * NM + owner], blocks[r][:half], preferred_element_type=F32)
        far = jnp.dot(ctx[(flip ^ 1) * NM + owner], blocks[r][half:], preferred_element_type=F32)
        term = (near + far).astype(BF).astype(F32)
        total = term if total is None else total + term
    stream = hidden[...].astype(F32) + total
    out[...] = stream.astype(BF)
    normed[...] = layer_norm(stream).astype(BF)


def dense_norm(pos, hidden, ctx, blocks):
    return pl.pallas_call(
        dense_kernel,
        in_specs=[SMEM] + [VMEM] * (2 + len(blocks)),
        out_specs=[VMEM, VMEM],
        out_shape=[jax.ShapeDtypeStruct(hidden.shape, BF)] * 2,
        compiler_params=params(),
    )(pos, hidden, ctx, *blocks)


def up_kernel(count, *refs):
    pieces, weights = refs[:count], refs[count : (len(refs) - 2 + count) // 2]
    acts, xbuf, sem = refs[count + len(weights) : -2], refs[-2], refs[-1]
    copies = []
    at = 0
    for i, piece in enumerate(pieces):
        rows = piece.shape[0]
        copies.append(pltpu.make_async_copy(piece, xbuf.at[at : at + rows], sem.at[i]))
        at += rows
    for copy in copies:
        copy.start()
    for copy in copies:
        copy.wait()
    for w, act in zip(weights, acts):
        upper = jnp.dot(xbuf[...], w[...], preferred_element_type=F32)
        act[...] = jax.nn.gelu(upper, approximate=True).astype(BF)


def up_part(pieces, weights):
    rows, depth = sum(piece.shape[0] for piece in pieces), pieces[0].shape[1]
    return pl.pallas_call(
        functools.partial(up_kernel, len(pieces)),
        in_specs=[ANY] * len(pieces) + [VMEM] * len(weights),
        out_specs=[VMEM] * len(weights),
        out_shape=[jax.ShapeDtypeStruct((rows, w.shape[1]), BF) for w in weights],
        scratch_shapes=[pltpu.VMEM((rows, depth), BF), pltpu.SemaphoreType.DMA((len(pieces),))],
        compiler_params=params(),
    )(*pieces, *weights)


def join_kernel(pos, own_a, own_b, got_a, got_b, out):
    z, y, m = pos[0], pos[1], pos[2]
    width = own_a.shape[1]
    share = out.shape[0] // NM
    for side, parts in ((0, (own_a, own_b)), (1, (got_a, got_b))):
        for j, part in enumerate(parts):
            first = ((y ^ side) * 2 + (z % 2 + j) % 2) * width
            for i, r in enumerate((0, 2, 1, 3)):
                rows = pl.ds(pl.multiple_of((m ^ r) * share, 16), share)
                out[rows, pl.ds(pl.multiple_of(first, width), width)] = part[i * share : (i + 1) * share]


def join_parts(pos, *parts):
    rows, width = parts[0].shape
    return pl.pallas_call(
        join_kernel,
        in_specs=[SMEM] + [VMEM] * 4,
        out_specs=VMEM,
        out_shape=jax.ShapeDtypeStruct((rows, 4 * width), BF),
        compiler_params=params(),
    )(pos, *parts)


def pages_kernel(pos, table, own, got, out):
    y = pos[1]
    for b in range(own.shape[0]):
        slot = table[0, b]
        for side, part in ((0, own), (1, got)):
            for h in range(HEADS):
                out[slot, :, (y ^ side) * HEADS + h] = part[b, :, h]


def place_pages(pos, table, own, got):
    blocks, two, heads, page, width = own.shape
    return pl.pallas_call(
        pages_kernel,
        in_specs=[SMEM, SMEM, VMEM, VMEM],
        out_specs=VMEM,
        out_shape=jax.ShapeDtypeStruct((blocks, two, NY * heads, page, width), BF),
        compiler_params=params(),
    )(pos, table, own, got)


def in_quad(copies):
    return lax.all_to_all(copies, AXES, split_axis=0, concat_axis=0, tiled=True, axis_index_groups=QUADS)


def local_planes(hidden_in, segment_ids, page_table, qkv_master, up_master, dense_weight):
    dp, mp = lax.axis_index("dp"), lax.axis_index("mp")
    z, y = dp // NY, dp % NY
    pos = jnp.stack([z, y, mp]).astype(jnp.int32)
    half = dense_weight.shape[0] // 2
    share = hidden_in.shape[0]
    head = H // NM * mp + HEADS * y + jnp.arange(HEADS)
    slopes = jnp.exp2(-8.0 * (head + 1).astype(F32) / H)

    qkv_own = to_all(cast_pieces(qkv_master))
    normed = norm_rows(hidden_in)
    from_y = send(normed, YSWAP)
    from_x = send(normed, XSWAP)
    cross_low = send(from_y[: share // 2], XSWAP)
    cross_high = send(from_x[share // 2 :], YSWAP)
    mine = pack_rows(normed, from_y, from_x, cross_low, cross_high)
    up_pieces = cast_pieces(up_master)
    give = lax.dynamic_slice_in_dim(dense_weight, y * half, half, 0)
    seg_other = send(segment_ids, YSWAP)
    qkv_own, mine, up_pieces, give, seg_other, dense_own, segment_ids = window(
        qkv_own, mine, up_pieces, give, seg_other, dense_weight, segment_ids
    )

    up_own = to_all(up_pieces)
    qkv_got = send(qkv_own, ZSWAP)
    other = send(mine, CORE)
    near = send(give, XSWAP)
    far = send(near, YSWAP)
    dense_c = send(dense_own, CORE)
    segments = jnp.concatenate([segment_ids, seg_other], 0)
    seg_rows, seg_cols = segments[:, None, :], segments[:, :, None]
    context, kv_own, kv_other = two_heads(pos, slopes, seg_rows, seg_cols, (mine, other), qkv_own, qkv_got)
    up_own, context, far, near, dense_own, dense_c, kv_own, kv_other = window(
        up_own, context, far, near, dense_own, dense_c, kv_own, kv_other
    )

    up_got = send(up_own, ZSWAP)
    dense_x = pack_rows(near, far)
    dense_xc = send(dense_x, CORE)
    ctx_own = in_plane(context.reshape(PLANE, -1, HEADS * HD))
    hidden_out, normed = dense_norm(pos, hidden_in, ctx_own, [dense_own, dense_c, dense_x, dense_xc])
    from_y = send(normed, YSWAP)
    from_x = send(normed, XSWAP)
    cross_low = send(from_y[: share // 2], XSWAP)
    cross_high = send(from_x[share // 2 :], YSWAP)
    group_own = [normed, from_x]
    group_other = [from_y, cross_low, cross_high]
    group_own += [send(piece, CORE) for piece in group_own]
    group_other += [send(piece, CORE) for piece in group_other]
    up_own, up_got, kv_own, kv_other, *tokens = window(up_own, up_got, kv_own, kv_other, *group_own, *group_other)
    group_own, group_other = tokens[:4], tokens[4:]

    weights = [up_own, up_got]
    act_got = [send(up_part(group_other, [w])[0], YSWAP) for w in weights]
    act_own = up_part(group_own, weights)
    kv_got = send(kv_other, YSWAP)
    activated = join_parts(pos, *act_own, *act_got)
    cache = place_pages(pos, page_table, kv_own, kv_got)
    return hidden_out, activated, cache


def solution(mesh):
    placed = (
        P(("dp", "mp"), None),
        P("dp", None),
        P("dp", None),
        P(("dp", "mp"), None),
        P(("dp", "mp"), None),
        P("mp", None),
    )
    planes = mesh.shape["dp"] == NZ * NY and mesh.shape["mp"] == NM
    return jax.shard_map(
        local_planes if planes else local_any,
        mesh=mesh,
        in_specs=placed,
        out_specs=(P(("dp", "mp"), None), P("dp", "mp"), P("dp", None, "mp", None, None)),
        check_vma=False,
    )
```

time: 427 us -> 222 us (0.52)
  waiting for transfers between devices: 306 us -> 118 us
  Pallas kernels: 0 us -> 50.9 us
  local copies, waits for them, and re-layouts: 59.4 us -> 8.69 us
  matrix products: 23.1 us -> 0 us
  starting transfers between devices: 11.5 us -> 30.2 us
  between operations: 14 us -> 0.88 us
  blocking collectives: 0 us -> 11.7 us
  other arithmetic: 11.5 us -> 1.19 us
    all_to_all x2, waiting for transfers between devices: 155 us -> 0.01 us  [to_all(): mine = lax.all_to_all(pieces, AXES, split_axis=0, concat_axis=0, tiled=True)]
    all_gather x4 -> x0, waiting for transfers between devices: 133 us -> none  [the longest x1 98.5 us: local(): lax.all_gather(qkv_bf, 'dp', axis=0, tiled=True)]
    ppermute x0 -> x24, waiting for transfers between devices: none -> 118 us  [send(): return lax.ppermute(value, AXES, moves)]
    pallas_call x0 -> x12, Pallas kernels: none -> 50.9 us  [the longest x3 16.3 us: up_part(): pl.pallas_call(functools.partial(up_kernel, len(pieces)), in_specs=[ANY]...]
    dot_general x4 -> x0, matrix products: 20.9 us -> none  [the longest x1 9.16 us: local(): upper = jnp.dot(normed_two, up_w, preferred_element_type=jnp.float32)]
    all_gather x2 -> x0, local copies, waits for them, and re-layouts: 20.8 us -> none  [the longest x1 12.1 us: local(): lax.all_gather(up_bf, 'dp', axis=0, tiled=True)]
    all_to_all x2 -> x0, local copies, waits for them, and re-layouts: 20.1 us -> none  [the longest x1 11.4 us: local(): lax.all_to_all(up_rows, 'mp', split_axis=1, concat_axis=0, tiled=True)]
    ppermute x0 -> x24, starting transfers between devices: none -> 19.7 us  [send(): return lax.ppermute(value, AXES, moves)]
  transfers between devices with their start and end apart: 7 -> 26, of which waited for: 5 -> 10; matrix products, arithmetic and copies ran while one was open for 19% -> 2% of each run, Pallas kernels for 0% -> 19%
where the time goes in v2:
time: 222 us; the launch traced here: 221 us
  waiting for transfers between devices  118 us (53%)
  Pallas kernels  50.9 us (23%)
  starting transfers between devices  30.2 us (14%)
  blocking collectives  11.7 us (5%)
  local copies, waits for them, and re-layouts  8.69 us (4%)
    ppermute x24, waiting for transfers between devices, send(): return lax.ppermute(value, AXES, moves)  118 us
    ppermute x24, starting transfers between devices, send(): return lax.ppermute(value, AXES, moves)  19.7 us
    pallas_call x3, Pallas kernels, up_part(): pl.pallas_call(functools.partial(up_kernel, len(pieces)), in_specs=[ANY]...  16.3 us
    all_to_all x1, blocking collectives, in_plane(): lax.all_to_all(pieces, AXES, split_axis=0, concat_axis=0, tiled=True, axi...  11.7 us
    all_to_all x2, starting transfers between devices, to_all(): mine = lax.all_to_all(pieces, AXES, split_axis=0, concat_axis=0, tiled=True)  10.5 us
    pallas_call x1, Pallas kernels, two_heads(): pl.pallas_call(head_kernel, in_specs=[SMEM, SMEM, VMEM, VMEM] + [ANY] * 4...  10.2 us
    pallas_call x1, Pallas kernels, dense_norm(): pl.pallas_call(dense_kernel, in_specs=[SMEM] + [VMEM] * (2 + len(blocks))...  6.22 us
    pallas_call x2, Pallas kernels, pack_rows(): pl.pallas_call(pack_kernel, in_specs=[VMEM] * len(parts), out_specs=VMEM,...  5.77 us
  transfers between devices with their start and end apart: 26, of which 10 were waited for; matrix products, arithmetic and copies ran while one was open for 2% of the time, Pallas kernels for 19%

profile of v2, /device:TPU:0, one launch (start us, length us, event | category | flops | bytes accessed | tf_op | source)
XLA Modules:
  0.0 221.2 jit_solution(14805499375779959751)
XLA Ops:
  0.6 2.7 %shard_map.85 = bf16[32,64,384]{2,1,0:T(8,128)(2,1)} custom-call(f32[64,6144]{1,0:T(8,128)} %src.2), custom_call_target="tpu_custom_call" | custom-call | tf_op jit(solution)/shard_map/pallas_call | solution.py:126
  3.3 7.3 %all-to-all-start = ((bf16[32,64,384]{2,1,0:T(8,128)(2,1)}), bf16[32,64,384]{2,1,0:T(8,128)(2,1)S(1)}, u32[]{:S(2)}, u32[]{:S(2)}) async-start(bf16[32,64,384]{2,1,0:T(8,128)(2,1)} %shard_map.85), calls=%async_computation | async-start | bytes 3145728 | tf_op jit(solution)/shard_map/all_to_all | solution.py:169
  10.6 2.0 shard_map.86.refs_0_
  16.5 19.5 %collective-permute-done.refs_1_ = bf16[96,2048]{1,0:T(8,128)(2,1)S(1)} collective-permute-done((bf16[96,2048]{1,0:T(8,128)(2,1)}, bf16[96,2048]{1,0:T(8,128)(2,1)S(1)}, u32[]{:S(2)}, u32[]{:S(2)}) %collective-permute-start) | collective-permute-done | bytes 393248 | tf_op jit(solution)/shard_map/ppermute | solution.py:98
  35.9 2.3 %collective-permute-start.2 = (bf16[48,2048]{1,0:T(8,128)(2,1)S(1)}, bf16[48,2048]{1,0:T(8,128)(2,1)S(1)}, u32[]{:S(2)}, u32[]{:S(2)}) collective-permute-start(bf16[48,2048]{1,0:T(8,128)(2,1)S(1)} %slice.16), channel_id=1, source_target_pairs={{0,2},{1,3},{2,0},{3,1},{4,6},{5,7},{6,4},{7,5},{8,10},{9,11},{10,... | collective-permute-start | bytes 589832 | tf_op jit(solution)/shard_map/ppermute | solution.py:98
  39.7 3.1 %shard_map.88 = bf16[32,64,512]{2,1,0:T(8,128)(2,1)} custom-call(f32[64,8192]{1,0:T(8,128)} %src.3), custom_call_target="tpu_custom_call" | custom-call | tf_op jit(solution)/shard_map/pallas_call | solution.py:126
  44.5 2.5 %collective-permute-done.3.refs_4_ = bf16[48,2048]{1,0:T(8,128)(2,1)S(1)} collective-permute-done((bf16[48,2048]{1,0:T(8,128)(2,1)S(1)}, bf16[48,2048]{1,0:T(8,128)(2,1)S(1)}, u32[]{:S(2)}, u32[]{:S(2)}) %collective-permute-start.3) | collective-permute-done | bytes 196640 | tf_op jit(solution)/shard_map/ppermute | solution.py:98
  47.7 2.6 %shard_map.87.mine = bf16[384,2048]{1,0:T(8,128)(2,1)} custom-call(bf16[96,2048]{1,0:T(8,128)(2,1)} %shard_map.86.refs_0_, bf16[96,2048]{1,0:T(8,128)(2,1)} %copy-done.8, bf16[96,2048]{1,0:T(8,128)(2,1)} %copy-done.9, bf16[48,2048]{1,0:T(8,128)(2,1)} %copy-done.20, bf16[48,2048]{1,0:T(8,128)(2,1)} %copy-done.21), custom_call_target="tpu_custom_call" | custom-call | tf_op jit(solution)/shard_map/pallas_call | solution.py:145
  51.5 3.2 %all-to-all-start.1 = ((bf16[32,64,512]{2,1,0:T(8,128)(2,1)}), bf16[32,64,512]{2,1,0:T(8,128)(2,1)S(1)}, u32[]{:S(2)}, u32[]{:S(2)}) async-start(bf16[32,64,512]{2,1,0:T(8,128)(2,1)} %shard_map.88), calls=%async_computation.1 | async-start | bytes 4194304 | tf_op jit(solution)/shard_map/all_to_all | solution.py:169
  54.7 1.8 collective-permute-start.7
  58.5 44.1 %collective-permute-done.7.refs_0_ = bf16[256,2048]{1,0:T(8,128)(2,1)} collective-permute-done((bf16[256,2048]{1,0:T(8,128)(2,1)S(1)}, bf16[256,2048]{1,0:T(8,128)(2,1)}, u32[]{:S(2)}, u32[]{:S(2)}) %collective-permute-start.7) | collective-permute-done | bytes 1048608 | tf_op jit(solution)/shard_map/ppermute | solution.py:98
  106.8 18.3 %collective-permute-done.6.w_got = bf16[2048,384]{1,0:T(8,128)(2,1)} collective-permute-done((bf16[2048,384]{1,0:T(8,128)(2,1)}, bf16[2048,384]{1,0:T(8,128)(2,1)}, u32[]{:S(2)}, u32[]{:S(2)}) %collective-permute-start.6) | collective-permute-done | bytes 1572896 | tf_op jit(solution)/shard_map/ppermute | solution.py:98
  125.1 10.2 %shard_map.89 = (bf16[768,256]{1,0:T(8,128)(2,1)}, bf16[3,2,2,128,128]{4,3,2,1,0:T(8,128)(2,1)}, bf16[3,2,2,128,128]{4,3,2,1,0:T(8,128)(2,1)}) custom-call(s32[3]{0:T(128)} %pad_add_fusion.1.pos, f32[2]{0:T(128)} %multiply_exponential_fusion.slope, s32[2,1,384]{2,1,0:T(1,128)} %broadcast_in_dim.6.seg_rows, s32[2,384,1]{2,1,0:T(8,128)} %copy.10.seg_cols, ...), custom_call_target="tpu_custom_call" | custom-call | tf_op jit(solution)/shard_map/pallas_call | solution.py:236
  136.3 3.2 %shard_map.90.rest_2_ = bf16[512,2048]{1,0:T(8,128)(2,1)} custom-call(bf16[256,2048]{1,0:T(8,128)(2,1)} %collective-permute-done.7.refs_0_, bf16[256,2048]{1,0:T(8,128)(2,1)} %copy-done.6), custom_call_target="tpu_custom_call" | custom-call | tf_op jit(solution)/shard_map/pallas_call | solution.py:145
  140.4 11.7 %all_to_all.15.ctx = bf16[8,96,256]{2,1,0:T(8,128)(2,1)} all-to-all(bf16[8,96,256]{2,1,0:T(8,128)(2,1)S(1)} %bitcast.13), channel_id=1, replica_groups={{0,1,2,3,4,5,6,7},{8,9,10,11,12,13,14,15},{16,17,18,19,20,21,22,23},{24..., dimensions={0} | all-to-all | bytes 786432 | tf_op jit(solution)/shard_map/all_to_all | solution.py:174
  153.5 6.2 %shard_map.91 = (bf16[96,2048]{1,0:T(8,128)(2,1)}, bf16[96,2048]{1,0:T(8,128)(2,1)}) custom-call(s32[3]{0:T(128)} %pad_add_fusion.1.pos, bf16[96,2048]{1,0:T(8,128)(2,1)} %hidden.3, bf16[8,96,256]{2,1,0:T(8,128)(2,1)} %all_to_all.15.ctx, bf16[512,2048]{1,0:T(8,128)(2,1)} %rest_0_, bf16[512,2048]{1,0:T(8,128)(2,1)} %collective-permute-done.9.rest_1_, ...), custom_call_target="tpu_custom_call" | custom-call | tf_op jit(solution)/shard_map/pallas_call | solution.py:270
  160.8 9.7 %collective-permute-done.15.refs_0_ = bf16[96,2048]{1,0:T(8,128)(2,1)S(1)} collective-permute-done((bf16[96,2048]{1,0:T(8,128)(2,1)}, bf16[96,2048]{1,0:T(8,128)(2,1)S(1)}, u32[]{:S(2)}, u32[]{:S(2)}) %collective-permute-start.15) | collective-permute-done | bytes 393248 | tf_op jit(solution)/shard_map/ppermute | solution.py:98
  172.4 15.1 %collective-permute-done.11.refs_5_.refs_6_ = bf16[2048,512]{1,0:T(8,128)(2,1)S(1)} collective-permute-done((bf16[2048,512]{1,0:T(8,128)(2,1)S(1)}, bf16[2048,512]{1,0:T(8,128)(2,1)S(1)}, u32[]{:S(2)}, u32[]{:S(2)}) %collective-permute-start.11) | collective-permute-done | bytes 2097184 | tf_op jit(solution)/shard_map/ppermute | solution.py:98
  191.4 4.9 %shard_map.94 = bf16[384,512]{1,0:T(8,128)(2,1)} custom-call(bf16[96,2048]{1,0:T(8,128)(2,1)} %copy-done.3, bf16[48,2048]{1,0:T(8,128)(2,1)} %copy-done.10, bf16[48,2048]{1,0:T(8,128)(2,1)} %copy-done.11, bf16[96,2048]{1,0:T(8,128)(2,1)} %copy-done.5, bf16[48,2048]{1,0:T(8,128)(2,1)} %copy-done.12, bf16[48,2048]{1,0:T(8,128)(2,1)} %copy-done.13, ...), custom_call_target="tpu_custom_call" | custom-call | tf_op jit(solution)/shard_map/pallas_call | solution.py:299
  197.1 4.9 %shard_map.93 = bf16[384,512]{1,0:T(8,128)(2,1)} custom-call(bf16[96,2048]{1,0:T(8,128)(2,1)} %copy-done.3, bf16[48,2048]{1,0:T(8,128)(2,1)} %copy-done.10, bf16[48,2048]{1,0:T(8,128)(2,1)} %copy-done.11, bf16[96,2048]{1,0:T(8,128)(2,1)} %copy-done.5, bf16[48,2048]{1,0:T(8,128)(2,1)} %copy-done.12, bf16[48,2048]{1,0:T(8,128)(2,1)} %copy-done.13, ...), custom_call_target="tpu_custom_call" | custom-call | tf_op jit(solution)/shard_map/pallas_call | solution.py:299
  203.4 6.4 %shard_map.92 = (bf16[384,512]{1,0:T(8,128)(2,1)}, bf16[384,512]{1,0:T(8,128)(2,1)}) custom-call(bf16[96,2048]{1,0:T(8,128)(2,1)} %get-tuple-element.59.refs_0_, bf16[96,2048]{1,0:T(8,128)(2,1)} %copy-done.7, bf16[96,2048]{1,0:T(8,128)(2,1)} %copy-done.14, bf16[96,2048]{1,0:T(8,128)(2,1)} %copy-done.15, bf16[2048,512]{1,0:T(8,128)(2,1)} %bitcast.10, ...), custom_call_target="tpu_custom_call" | custom-call | tf_op jit(solution)/shard_map/pallas_call | solution.py:299
  210.6 2.1 shard_map.96
  212.7 5.2 %collective-permute-done.21.got_a = bf16[384,512]{1,0:T(8,128)(2,1)S(1)} collective-permute-done((bf16[384,512]{1,0:T(8,128)(2,1)}, bf16[384,512]{1,0:T(8,128)(2,1)S(1)}, u32[]{:S(2)}, u32[]{:S(2)}) %collective-permute-start.21) | collective-permute-done | bytes 393248 | tf_op jit(solution)/shard_map/ppermute | solution.py:98
  218.6 2.6 %shard_map.95 = bf16[384,2048]{1,0:T(8,128)(2,1)} custom-call(s32[3]{0:T(128)} %pad_add_fusion.1.pos, bf16[384,512]{1,0:T(8,128)(2,1)} %get-tuple-element.65.own_a, bf16[384,512]{1,0:T(8,128)(2,1)} %get-tuple-element.66.own_b, bf16[384,512]{1,0:T(8,128)(2,1)} %copy-done.19, bf16[384,512]{1,0:T(8,128)(2,1)} %copy-done.18), custom_call_target="tpu_custom_call" | custom-call | tf_op jit(solution)/shard_map/pallas_call | solution.py:323
  (99 shorter events, 28.8 us)
Async XLA Ops:
  3.3 47.0 %all-to-all-start = ((bf16[32,64,384]{2,1,0:T(8,128)(2,1)}), bf16[32,64,384]{2,1,0:T(8,128)(2,1)S(1)}, u32[]{:S(2)}, u32[]{:S(2)}) async-start(bf16[32,64,384]{2,1,0:T(8,128)(2,1)} %shard_map.85), calls=%async_computation | async-start | bytes 3145728 | tf_op jit(solution)/shard_map/all_to_all | solution.py:169
  12.7 23.3 %collective-permute-start = (bf16[96,2048]{1,0:T(8,128)(2,1)}, bf16[96,2048]{1,0:T(8,128)(2,1)S(1)}, u32[]{:S(2)}, u32[]{:S(2)}) collective-permute-start(bf16[96,2048]{1,0:T(8,128)(2,1)} %shard_map.86.refs_0_), channel_id=1, source_target_pairs={{0,4},{1,5},{2,6},{3,7},{4,0},{5,1},{6,2},{7,3},{8,12},{9,13},{10,... | collective-permute-start | bytes 1179656 | tf_op jit(solution)/shard_map/ppermute | solution.py:98
  14.4 23.8 %collective-permute-start.1 = (bf16[96,2048]{1,0:T(8,128)(2,1)}, bf16[96,2048]{1,0:T(8,128)(2,1)S(1)}, u32[]{:S(2)}, u32[]{:S(2)}) collective-permute-start(bf16[96,2048]{1,0:T(8,128)(2,1)} %shard_map.86.refs_0_), channel_id=1, source_target_pairs={{0,2},{1,3},{2,0},{3,1},{4,6},{5,7},{6,4},{7,5},{8,10},{9,11},{10,... | collective-permute-start | bytes 1179656 | tf_op jit(solution)/shard_map/ppermute | solution.py:98
  15.9 34.4 %collective-permute-start.4 = (s32[1,384]{1,0:T(1,128)S(1)}, s32[1,384]{1,0:T(1,128)S(1)}, u32[]{:S(2)}, u32[]{:S(2)}) collective-permute-start(s32[1,384]{1,0:T(1,128)S(1)} %copy-done.22), channel_id=1, source_target_pairs={{0,4},{1,5},{2,6},{3,7},{4,0},{5,1},{6,2},{7,3},{8,12},{9,13},{10,... | collective-permute-start | bytes 4616 | tf_op jit(solution)/shard_map/ppermute | solution.py:98
  35.9 8.5 %collective-permute-start.2 = (bf16[48,2048]{1,0:T(8,128)(2,1)S(1)}, bf16[48,2048]{1,0:T(8,128)(2,1)S(1)}, u32[]{:S(2)}, u32[]{:S(2)}) collective-permute-start(bf16[48,2048]{1,0:T(8,128)(2,1)S(1)} %slice.16), channel_id=1, source_target_pairs={{0,2},{1,3},{2,0},{3,1},{4,6},{5,7},{6,4},{7,5},{8,10},{9,11},{10,... | collective-permute-start | bytes 589832 | tf_op jit(solution)/shard_map/ppermute | solution.py:98
  38.2 8.7 %collective-permute-start.3 = (bf16[48,2048]{1,0:T(8,128)(2,1)S(1)}, bf16[48,2048]{1,0:T(8,128)(2,1)S(1)}, u32[]{:S(2)}, u32[]{:S(2)}) collective-permute-start(bf16[48,2048]{1,0:T(8,128)(2,1)S(1)} %slice.17), channel_id=1, source_target_pairs={{0,4},{1,5},{2,6},{3,7},{4,0},{5,1},{6,2},{7,3},{8,12},{9,13},{10,... | collective-permute-start | bytes 589832 | tf_op jit(solution)/shard_map/ppermute | solution.py:98
  51.5 83.8 %all-to-all-start.1 = ((bf16[32,64,512]{2,1,0:T(8,128)(2,1)}), bf16[32,64,512]{2,1,0:T(8,128)(2,1)S(1)}, u32[]{:S(2)}, u32[]{:S(2)}) async-start(bf16[32,64,512]{2,1,0:T(8,128)(2,1)} %shard_map.88), calls=%async_computation.1 | async-start | bytes 4194304 | tf_op jit(solution)/shard_map/all_to_all | solution.py:169
  54.7 47.9 %collective-permute-start.7 = (bf16[256,2048]{1,0:T(8,128)(2,1)S(1)}, bf16[256,2048]{1,0:T(8,128)(2,1)}, u32[]{:S(2)}, u32[]{:S(2)}) collective-permute-start(bf16[256,2048]{1,0:T(8,128)(2,1)S(1)} %constant_dynamic-slice_fusion), channel_id=1, source_target_pairs={{0,2},{1,3},{2,0},{3,1},{4,6},{5,7},{6,4},{7,5},{8,10},{9,11},{10,... | collective-permute-start | bytes 3145736 | tf_op jit(solution)/shard_map/ppermute | solution.py:98
  56.5 78.8 %collective-permute-start.9 = (bf16[512,2048]{1,0:T(8,128)(2,1)}, bf16[512,2048]{1,0:T(8,128)(2,1)}, u32[]{:S(2)}, u32[]{:S(2)}) collective-permute-start(bf16[512,2048]{1,0:T(8,128)(2,1)} %rest_0_), channel_id=1, source_target_pairs={{0,1},{1,0},{2,3},{3,2},{4,5},{5,4},{6,7},{7,6},{8,9},{9,8},{10,11... | collective-permute-start | bytes 6291464 | tf_op jit(solution)/shard_map/ppermute | solution.py:98
  56.5 50.3 %collective-permute-start.5 = (bf16[384,2048]{1,0:T(8,128)(2,1)}, bf16[384,2048]{1,0:T(8,128)(2,1)}, u32[]{:S(2)}, u32[]{:S(2)}) collective-permute-start(bf16[384,2048]{1,0:T(8,128)(2,1)} %shard_map.87.mine), channel_id=1, source_target_pairs={{0,1},{1,0},{2,3},{3,2},{4,5},{5,4},{6,7},{7,6},{8,9},{9,8},{10,11... | collective-permute-start | bytes 4718600 | tf_op jit(solution)/shard_map/ppermute | solution.py:98
  57.0 68.0 %collective-permute-start.6 = (bf16[2048,384]{1,0:T(8,128)(2,1)}, bf16[2048,384]{1,0:T(8,128)(2,1)}, u32[]{:S(2)}, u32[]{:S(2)}) collective-permute-start(bf16[2048,384]{1,0:T(8,128)(2,1)} %bitcast.11), channel_id=1, source_target_pairs={{0,8},{1,9},{2,10},{3,11},{4,12},{5,13},{6,14},{7,15},{8,0},{9,1},... | collective-permute-start | bytes 4718600 | tf_op jit(solution)/shard_map/ppermute | solution.py:98
  102.6 32.7 %collective-permute-start.8 = (bf16[256,2048]{1,0:T(8,128)(2,1)}, bf16[256,2048]{1,0:T(8,128)(2,1)S(1)}, u32[]{:S(2)}, u32[]{:S(2)}) collective-permute-start(bf16[256,2048]{1,0:T(8,128)(2,1)} %collective-permute-done.7.refs_0_), channel_id=1, source_target_pairs={{0,4},{1,5},{2,6},{3,7},{4,0},{5,1},{6,2},{7,3},{8,12},{9,13},{10,... | collective-permute-start | bytes 3145736 | tf_op jit(solution)/shard_map/ppermute | solution.py:98
  139.4 12.7 %collective-permute-start.10 = (bf16[512,2048]{1,0:T(8,128)(2,1)}, bf16[512,2048]{1,0:T(8,128)(2,1)S(1)}, u32[]{:S(2)}, u32[]{:S(2)}) collective-permute-start(bf16[512,2048]{1,0:T(8,128)(2,1)} %shard_map.90.rest_2_), channel_id=1, source_target_pairs={{0,1},{1,0},{2,3},{3,2},{4,5},{5,4},{6,7},{7,6},{8,9},{9,8},{10,11... | collective-permute-start | bytes 6291464 | tf_op jit(solution)/shard_map/ppermute | solution.py:98
  139.4 48.0 %collective-permute-start.11 = (bf16[2048,512]{1,0:T(8,128)(2,1)S(1)}, bf16[2048,512]{1,0:T(8,128)(2,1)S(1)}, u32[]{:S(2)}, u32[]{:S(2)}) collective-permute-start(bf16[2048,512]{1,0:T(8,128)(2,1)S(1)} %bitcast.8), channel_id=1, source_target_pairs={{0,8},{1,9},{2,10},{3,11},{4,12},{5,13},{6,14},{7,15},{8,0},{9,1},... | collective-permute-start | bytes 6291464 | tf_op jit(solution)/shard_map/ppermute | solution.py:98
  159.7 10.9 %collective-permute-start.15 = (bf16[96,2048]{1,0:T(8,128)(2,1)}, bf16[96,2048]{1,0:T(8,128)(2,1)S(1)}, u32[]{:S(2)}, u32[]{:S(2)}) collective-permute-start(bf16[96,2048]{1,0:T(8,128)(2,1)} %get-tuple-element.59.refs_0_), channel_id=1, source_target_pairs={{0,4},{1,5},{2,6},{3,7},{4,0},{5,1},{6,2},{7,3},{8,12},{9,13},{10,... | collective-permute-start | bytes 1179656 | tf_op jit(solution)/shard_map/ppermute | solution.py:98
  160.2 11.1 %collective-permute-start.12 = (bf16[96,2048]{1,0:T(8,128)(2,1)}, bf16[96,2048]{1,0:T(8,128)(2,1)S(1)}, u32[]{:S(2)}, u32[]{:S(2)}) collective-permute-start(bf16[96,2048]{1,0:T(8,128)(2,1)} %get-tuple-element.59.refs_0_), channel_id=1, source_target_pairs={{0,2},{1,3},{2,0},{3,1},{4,6},{5,7},{6,4},{7,5},{8,10},{9,11},{10,... | collective-permute-start | bytes 1179656 | tf_op jit(solution)/shard_map/ppermute | solution.py:98
  160.8 27.3 %collective-permute-start.13 = (bf16[96,2048]{1,0:T(8,128)(2,1)}, bf16[96,2048]{1,0:T(8,128)(2,1)S(1)}, u32[]{:S(2)}, u32[]{:S(2)}) collective-permute-start(bf16[96,2048]{1,0:T(8,128)(2,1)} %get-tuple-element.59.refs_0_), channel_id=1, source_target_pairs={{0,1},{1,0},{2,3},{3,2},{4,5},{5,4},{6,7},{7,6},{8,9},{9,8},{10,11... | collective-permute-start | bytes 1179656 | tf_op jit(solution)/shard_map/ppermute | solution.py:98
  170.6 16.9 %collective-permute-start.16 = (bf16[48,2048]{1,0:T(8,128)(2,1)S(1)}, bf16[48,2048]{1,0:T(8,128)(2,1)S(1)}, u32[]{:S(2)}, u32[]{:S(2)}) collective-permute-start(bf16[48,2048]{1,0:T(8,128)(2,1)S(1)} %slice.18), channel_id=1, source_target_pairs={{0,2},{1,3},{2,0},{3,1},{4,6},{5,7},{6,4},{7,5},{8,10},{9,11},{10,... | collective-permute-start | bytes 589832 | tf_op jit(solution)/shard_map/ppermute | solution.py:98
  171.3 16.6 %collective-permute-start.17 = (bf16[48,2048]{1,0:T(8,128)(2,1)S(1)}, bf16[48,2048]{1,0:T(8,128)(2,1)S(1)}, u32[]{:S(2)}, u32[]{:S(2)}) collective-permute-start(bf16[48,2048]{1,0:T(8,128)(2,1)S(1)} %slice.19), channel_id=1, source_target_pairs={{0,4},{1,5},{2,6},{3,7},{4,0},{5,1},{6,2},{7,3},{8,12},{9,13},{10,... | collective-permute-start | bytes 589832 | tf_op jit(solution)/shard_map/ppermute | solution.py:98
  172.4 17.4 %collective-permute-start.14 = (bf16[96,2048]{1,0:T(8,128)(2,1)S(1)}, bf16[96,2048]{1,0:T(8,128)(2,1)S(1)}, u32[]{:S(2)}, u32[]{:S(2)}) collective-permute-start(bf16[96,2048]{1,0:T(8,128)(2,1)S(1)} %collective-permute-done.12.refs_1_), channel_id=1, source_target_pairs={{0,1},{1,0},{2,3},{3,2},{4,5},{5,4},{6,7},{7,6},{8,9},{9,8},{10,11... | collective-permute-start | bytes 1179656 | tf_op jit(solution)/shard_map/ppermute | solution.py:98
  187.5 2.3 %collective-permute-start.18 = (bf16[96,2048]{1,0:T(8,128)(2,1)S(1)}, bf16[96,2048]{1,0:T(8,128)(2,1)S(1)}, u32[]{:S(2)}, u32[]{:S(2)}) collective-permute-start(bf16[96,2048]{1,0:T(8,128)(2,1)S(1)} %collective-permute-done.15.refs_0_), channel_id=1, source_target_pairs={{0,1},{1,0},{2,3},{3,2},{4,5},{5,4},{6,7},{7,6},{8,9},{9,8},{10,11... | collective-permute-start | bytes 1179656 | tf_op jit(solution)/shard_map/ppermute | solution.py:98
  189.8 20.1 %collective-permute-start.23 = (bf16[3,2,2,128,128]{4,3,2,1,0:T(8,128)(2,1)S(1)}, bf16[3,2,2,128,128]{4,3,2,1,0:T(8,128)(2,1)S(1)}, u32[]{:S(2)}, u32[]{:S(2)}) collective-permute-start(bf16[3,2,2,128,128]{4,3,2,1,0:T(8,128)(2,1)S(1)} %copy-done.23), channel_id=1, source_target_pairs={{0,4},{1,5},{2,6},{3,7},{4,0},{5,1},{6,2},{7,3},{8,12},{9,13},{10,... | collective-permute-start | bytes 1179656 | tf_op jit(solution)/shard_map/ppermute | solution.py:98
  196.3 16.3 %collective-permute-start.22 = (bf16[384,512]{1,0:T(8,128)(2,1)}, bf16[384,512]{1,0:T(8,128)(2,1)S(1)}, u32[]{:S(2)}, u32[]{:S(2)}) collective-permute-start(bf16[384,512]{1,0:T(8,128)(2,1)} %shard_map.94), channel_id=1, source_target_pairs={{0,4},{1,5},{2,6},{3,7},{4,0},{5,1},{6,2},{7,3},{8,12},{9,13},{10,... | collective-permute-start | bytes 1179656 | tf_op jit(solution)/shard_map/ppermute | solution.py:98
  202.0 15.9 %collective-permute-start.21 = (bf16[384,512]{1,0:T(8,128)(2,1)}, bf16[384,512]{1,0:T(8,128)(2,1)S(1)}, u32[]{:S(2)}, u32[]{:S(2)}) collective-permute-start(bf16[384,512]{1,0:T(8,128)(2,1)} %shard_map.93), channel_id=1, source_target_pairs={{0,4},{1,5},{2,6},{3,7},{4,0},{5,1},{6,2},{7,3},{8,12},{9,13},{10,... | collective-permute-start | bytes 1179656 | tf_op jit(solution)/shard_map/ppermute | solution.py:98
  (26 other events, 178.2 us)

commit v3 on v2

--- a/solution.py
+++ b/solution.py
@@ -90,6 +90,7 @@
 XSWAP = pairs(lambda z, y, m: (z, y, m ^ 2))
 YSWAP = pairs(lambda z, y, m: (z, y ^ 1, m))
 ZSWAP = pairs(lambda z, y, m: (z ^ 1, y, m))
+ZFAR = pairs(lambda z, y, m: (z ^ 2, y, m))
 PLANES = [[z * PLANE + i for i in range(PLANE)] for z in range(NZ)]
 QUADS = [[z * PLANE + 2 * i + c for i in range(PLANE // 2)] for z in range(NZ) for c in range(2)]
 
@@ -106,7 +107,8 @@
     return pltpu.CompilerParams(vmem_limit_bytes=VMEM_LIMIT, **more)
 
 
-ANY = pl.BlockSpec(memory_space=pltpu.HBM)
+HBM = pl.BlockSpec(memory_space=pltpu.HBM)
+ANY = pl.BlockSpec(memory_space=pl.ANY)
 SMEM = pl.BlockSpec(memory_space=pltpu.SMEM)
 VMEM = pl.BlockSpec(memory_space=pltpu.VMEM)
 
@@ -130,6 +132,45 @@
         out_shape=jax.ShapeDtypeStruct((NZ * PLANE, rows, width), BF),
         compiler_params=params(),
     )(master)
+
+
+def cast_halves(pos, master):
+    rows, cols = master.shape
+    half = cols // PLANE // 2
+
+    def kernel(pos, src, *dst):
+        parity = pos[0] % 2
+        for p in range(PLANE):
+            start = (2 * (p % NM) + p // NM) * 2 * half
+            for i in range(2):
+                first = pl.multiple_of(start + (parity ^ i) * half, half)
+                dst[i][p] = src[:, pl.ds(first, half)].astype(BF)
+
+    shape = jax.ShapeDtypeStruct((PLANE, rows, half), BF)
+    return pl.pallas_call(
+        kernel,
+        in_specs=[SMEM, VMEM],
+        out_specs=[VMEM, VMEM],
+        out_shape=[shape, shape],
+        compiler_params=params(),
+    )(pos, master)
+
+
+def stack_kernel(own, got, out):
+    rows = own.shape[1]
+    out[:, :rows] = own[...]
+    out[:, rows:] = got[...]
+
+
+def stack_rows(own, got):
+    count, rows, width = own.shape
+    return pl.pallas_call(
+        stack_kernel,
+        in_specs=[VMEM, VMEM],
+        out_specs=VMEM,
+        out_shape=jax.ShapeDtypeStruct((count, 2 * rows, width), BF),
+        compiler_params=params(),
+    )(own, got)
 
 
 def pack_kernel(*refs):
@@ -197,9 +238,12 @@
 
 def head_kernel(pos, slope, seg_rows, seg_cols, mine, other, w_own, w_got, ctx, kv_own, kv_other, xbuf, wbuf, xsem, wsem):
     z, y, m = pos[0], pos[1], pos[2]
+    width = w_own.shape[1]
     copies = [
-        pltpu.make_async_copy(w_own, wbuf.at[z % 2], wsem.at[0]),
-        pltpu.make_async_copy(w_got, wbuf.at[1 - z % 2], wsem.at[1]),
+        pltpu.make_async_copy(
+            src, wbuf.at[:, pl.ds(pl.multiple_of((z % 2 ^ i) * width, width), width)], wsem.at[i]
+        )
+        for i, src in enumerate((w_own, w_got))
     ] + token_copies(y, m, mine, other, xbuf, xsem)
     for copy in copies:
         copy.start()
@@ -214,15 +258,14 @@
         first = pl.multiple_of((y ^ g) * group, group)
         rows = pl.ds(first, group)
         allowed = (seg_cols[g] == seg_rows[g]) & (distance >= 0)
+        joined = jnp.dot(xbuf[rows, :], wbuf[...], preferred_element_type=F32).astype(BF)
         for h in range(HEADS):
-            joined = jnp.dot(xbuf[rows, :], wbuf[h], preferred_element_type=F32).astype(BF)
-            query, keys, vals = (joined[:, i * HD : (i + 1) * HD] for i in range(3))
+            query, keys, vals = (joined[:, (3 * h + i) * HD : (3 * h + i + 1) * HD] for i in range(3))
             scores = lax.dot_general(query, keys, (((1,), (1,)), ((), ())), preferred_element_type=F32)
             scores = scores * (1.0 / HD**0.5) - slope[h] * away
             scores = jnp.where(allowed, scores, -jnp.inf)
-            top = jnp.max(scores, -1, keepdims=True)
-            raised = jnp.exp(scores - top)
-            probs = (raised / jnp.sum(raised, -1, keepdims=True)).astype(BF)
+            raised = jnp.exp(scores - jnp.max(scores, -1, keepdims=True))
+            probs = (raised * (1.0 / jnp.sum(raised, -1, keepdims=True))).astype(BF)
             ctx[rows, h * HD : (h + 1) * HD] = jnp.dot(probs, vals, preferred_element_type=F32).astype(BF)
             for b in range(group // PAGE):
                 kv[b, 0, h] = keys[b * PAGE : (b + 1) * PAGE]
@@ -235,12 +278,12 @@
     kv_shape = jax.ShapeDtypeStruct((count // NY // PAGE, 2, HEADS, PAGE, HD), BF)
     return pl.pallas_call(
         head_kernel,
-        in_specs=[SMEM, SMEM, VMEM, VMEM] + [ANY] * 4,
+        in_specs=[SMEM, SMEM, VMEM, VMEM] + [HBM] * 4,
         out_specs=[VMEM, VMEM, VMEM],
         out_shape=[jax.ShapeDtypeStruct((count, HEADS * HD), BF), kv_shape, kv_shape],
         scratch_shapes=[
             pltpu.VMEM((count, depth), BF),
-            pltpu.VMEM((HEADS, depth, width), BF),
+            pltpu.VMEM((depth, HEADS * width), BF),
             pltpu.SemaphoreType.DMA((TOKEN_COPIES,)),
             pltpu.SemaphoreType.DMA((2,)),
         ],
@@ -248,18 +291,29 @@
     )(pos, slope, seg_rows, seg_cols, *tokens, w_own, w_got)
 
 
-def dense_kernel(pos, hidden, ctx, *rest):
-    blocks = rest[:NM]
-    out, normed = rest[NM:]
+def dense_kernel(pos, hidden, ctx, own, cross, *rest):
+    halves, (out, normed, dense, sem) = rest[:4], rest[4:]
     y, m = pos[1], pos[2]
-    half = blocks[0].shape[0] // 2
+    size = own.shape[0]
+    half = size // 2
+    loads = [[pltpu.make_async_copy(own, dense.at[0], sem.at[0])], [pltpu.make_async_copy(cross, dense.at[1], sem.at[1])]]
+    for r in (2, 3):
+        copies = []
+        for i in range(2):
+            first = pl.multiple_of((y ^ i) * half, half)
+            index = (r - 2) * 2 + i
+            copies.append(pltpu.make_async_copy(halves[index], dense.at[r, pl.ds(first, half)], sem.at[2 + index]))
+        loads.append(copies)
+    for copies in loads:
+        for copy in copies:
+            copy.start()
     total = None
     for r in range(NM):
         owner = m ^ r
-        flip = y if r >= 2 else 0
-        near = jnp.dot(ctx[flip * NM + owner], blocks[r][:half], preferred_element_type=F32)
-        far = jnp.dot(ctx[(flip ^ 1) * NM + owner], blocks[r][half:], preferred_element_type=F32)
-        term = (near + far).astype(BF).astype(F32)
+        left = jnp.concatenate([ctx[owner], ctx[NM + owner]], axis=1)
+        for copy in loads[r]:
+            copy.wait()
+        term = jnp.dot(left, dense[r], preferred_element_type=F32).astype(BF).astype(F32)
         total = term if total is None else total + term
     stream = hidden[...].astype(F32) + total
     out[...] = stream.astype(BF)
@@ -269,64 +323,91 @@
 def dense_norm(pos, hidden, ctx, blocks):
     return pl.pallas_call(
         dense_kernel,
-        in_specs=[SMEM] + [VMEM] * (2 + len(blocks)),
+        in_specs=[SMEM, VMEM, VMEM] + [HBM] * len(blocks),
         out_specs=[VMEM, VMEM],
         out_shape=[jax.ShapeDtypeStruct(hidden.shape, BF)] * 2,
+        scratch_shapes=[
+            pltpu.VMEM((NM,) + blocks[0].shape, BF),
+            pltpu.SemaphoreType.DMA((len(blocks),)),
+        ],
         compiler_params=params(),
     )(pos, hidden, ctx, *blocks)
 
 
-def up_kernel(count, *refs):
-    pieces, weights = refs[:count], refs[count : (len(refs) - 2 + count) // 2]
-    acts, xbuf, sem = refs[count + len(weights) : -2], refs[-2], refs[-1]
+def up_kernel(count, half, pos, *refs):
+    pieces, (near, *fars), (act, xbuf, wbuf, xsem, wsem) = refs[:count], refs[count:-5], refs[-5:]
+    z = pos[0]
+    rows, width = near.shape[1] // 2, wbuf.shape[3]
+    loads = [[] for _ in range(NZ)]
+    for side in range(2):
+        src = near.at[:, side * rows : (side + 1) * rows]
+        loads[side].append(pltpu.make_async_copy(src, wbuf.at[side], wsem.at[side, 0]))
+        at = 0
+        for i, far in enumerate(fars):
+            part = far.shape[2]
+            src = far.at[:, side * rows : (side + 1) * rows]
+            r = 2 + (side ^ half)
+            dst = wbuf.at[r, :, :, at : at + part]
+            loads[r].append(pltpu.make_async_copy(src, dst, wsem.at[r, i]))
+            at += part
     copies = []
     at = 0
     for i, piece in enumerate(pieces):
-        rows = piece.shape[0]
-        copies.append(pltpu.make_async_copy(piece, xbuf.at[at : at + rows], sem.at[i]))
-        at += rows
-    for copy in copies:
+        copies.append(pltpu.make_async_copy(piece, xbuf.at[at : at + piece.shape[0]], xsem.at[i]))
+        at += piece.shape[0]
+    for copy in copies + [load for group in loads for load in group]:
         copy.start()
     for copy in copies:
         copy.wait()
-    for w, act in zip(weights, acts):
-        upper = jnp.dot(xbuf[...], w[...], preferred_element_type=F32)
-        act[...] = jax.nn.gelu(upper, approximate=True).astype(BF)
-
-
-def up_part(pieces, weights):
+    depth = wbuf.shape[1] * rows
+    upper = None
+    for r in range(NZ):
+        for load in loads[r]:
+            load.wait()
+        left = xbuf[:, pl.ds(pl.multiple_of((z ^ r) * depth, depth), depth)]
+        term = jnp.dot(left, wbuf[r].reshape(depth, width), preferred_element_type=F32)
+        upper = term if upper is None else upper + term
+    act[...] = jax.nn.gelu(upper, approximate=True).astype(BF)
+
+
+def up_part(pos, half, pieces, near, fars):
     rows, depth = sum(piece.shape[0] for piece in pieces), pieces[0].shape[1]
-    return pl.pallas_call(
-        functools.partial(up_kernel, len(pieces)),
-        in_specs=[ANY] * len(pieces) + [VMEM] * len(weights),
-        out_specs=[VMEM] * len(weights),
-        out_shape=[jax.ShapeDtypeStruct((rows, w.shape[1]), BF) for w in weights],
-        scratch_shapes=[pltpu.VMEM((rows, depth), BF), pltpu.SemaphoreType.DMA((len(pieces),))],
-        compiler_params=params(),
-    )(*pieces, *weights)
-
-
-def join_kernel(pos, own_a, own_b, got_a, got_b, out):
+    width = near.shape[2]
+    return pl.pallas_call(
+        functools.partial(up_kernel, len(pieces), half),
+        in_specs=[SMEM] + [ANY] * len(pieces) + [HBM] * (1 + len(fars)),
+        out_specs=VMEM,
+        out_shape=jax.ShapeDtypeStruct((rows, width), BF),
+        scratch_shapes=[
+            pltpu.VMEM((rows, depth), BF),
+            pltpu.VMEM((NZ, near.shape[0], near.shape[1] // 2, width), BF),
+            pltpu.SemaphoreType.DMA((len(pieces),)),
+            pltpu.SemaphoreType.DMA((NZ, len(fars))),
+        ],
+        compiler_params=params(),
+    )(pos, *pieces, near, *fars)
+
+
+def join_kernel(places, pos, *refs):
+    *parts, out = refs
     z, y, m = pos[0], pos[1], pos[2]
-    width = own_a.shape[1]
     share = out.shape[0] // NM
-    for side, parts in ((0, (own_a, own_b)), (1, (got_a, got_b))):
-        for j, part in enumerate(parts):
-            first = ((y ^ side) * 2 + (z % 2 + j) % 2) * width
-            for i, r in enumerate((0, 2, 1, 3)):
-                rows = pl.ds(pl.multiple_of((m ^ r) * share, 16), share)
-                out[rows, pl.ds(pl.multiple_of(first, width), width)] = part[i * share : (i + 1) * share]
-
-
-def join_parts(pos, *parts):
-    rows, width = parts[0].shape
-    return pl.pallas_call(
-        join_kernel,
-        in_specs=[SMEM] + [VMEM] * 4,
-        out_specs=VMEM,
-        out_shape=jax.ShapeDtypeStruct((rows, 4 * width), BF),
-        compiler_params=params(),
-    )(pos, *parts)
+    for part, (side, half, devices) in zip(parts, places):
+        width = part.shape[1]
+        columns = pl.ds(pl.multiple_of(((y ^ side) * 2 + (z % 2 ^ half)) * width, width), width)
+        for i, r in enumerate(devices):
+            rows = pl.ds(pl.multiple_of((m ^ r) * share, 16), share)
+            out[rows, columns] = part[i * share : (i + 1) * share]
+
+
+def join_parts(pos, shape, parts):
+    return pl.pallas_call(
+        functools.partial(join_kernel, [part[1:] for part in parts]),
+        in_specs=[SMEM] + [VMEM] * len(parts),
+        out_specs=VMEM,
+        out_shape=jax.ShapeDtypeStruct(shape, BF),
+        compiler_params=params(),
+    )(pos, *(part[0] for part in parts))
 
 
 def pages_kernel(pos, table, own, got, out):
@@ -357,59 +438,76 @@
     dp, mp = lax.axis_index("dp"), lax.axis_index("mp")
     z, y = dp // NY, dp % NY
     pos = jnp.stack([z, y, mp]).astype(jnp.int32)
-    half = dense_weight.shape[0] // 2
     share = hidden_in.shape[0]
     head = H // NM * mp + HEADS * y + jnp.arange(HEADS)
     slopes = jnp.exp2(-8.0 * (head + 1).astype(F32) / H)
 
     qkv_own = to_all(cast_pieces(qkv_master))
+    up_0, up_1 = cast_halves(pos, up_master)
+    raw_0 = send(up_1, ZSWAP)
     normed = norm_rows(hidden_in)
     from_y = send(normed, YSWAP)
     from_x = send(normed, XSWAP)
     cross_low = send(from_y[: share // 2], XSWAP)
     cross_high = send(from_x[share // 2 :], YSWAP)
     mine = pack_rows(normed, from_y, from_x, cross_low, cross_high)
-    up_pieces = cast_pieces(up_master)
+    half = dense_weight.shape[0] // 2
     give = lax.dynamic_slice_in_dim(dense_weight, y * half, half, 0)
     seg_other = send(segment_ids, YSWAP)
-    qkv_own, mine, up_pieces, give, seg_other, dense_own, segment_ids = window(
-        qkv_own, mine, up_pieces, give, seg_other, dense_weight, segment_ids
+    segments = jnp.concatenate([segment_ids, seg_other], 0)
+    seg_rows, seg_cols = segments[:, None, :], segments[:, :, None]
+    qkv_own, mine, up_0, up_1, raw_0, give, seg_rows, seg_cols, slopes, pos, dense_own = window(
+        qkv_own, mine, up_0, up_1, raw_0, give, seg_rows, seg_cols, slopes, pos, dense_weight
     )
 
-    up_own = to_all(up_pieces)
     qkv_got = send(qkv_own, ZSWAP)
+    near_w0 = in_plane(stack_rows(up_0, raw_0))
     other = send(mine, CORE)
     near = send(give, XSWAP)
+    dense_c = send(dense_own, CORE)
+    qkv_own, qkv_got, near_w0, up_0, up_1, mine, other, near, dense_own, dense_c = window(
+        qkv_own, qkv_got, near_w0, up_0, up_1, mine, other, near, dense_own, dense_c
+    )
+
+    part = near_w0.shape[2] // 2
+    far_a = send(near_w0[:, :, :part], ZFAR)
+    raw_1 = send(up_0, ZSWAP)
     far = send(near, YSWAP)
-    dense_c = send(dense_own, CORE)
-    segments = jnp.concatenate([segment_ids, seg_other], 0)
-    seg_rows, seg_cols = segments[:, None, :], segments[:, :, None]
+    near_c = send(near, CORE)
     context, kv_own, kv_other = two_heads(pos, slopes, seg_rows, seg_cols, (mine, other), qkv_own, qkv_got)
-    up_own, context, far, near, dense_own, dense_c, kv_own, kv_other = window(
-        up_own, context, far, near, dense_own, dense_c, kv_own, kv_other
+    ctx_own = in_plane(context.reshape(PLANE, -1, HEADS * HD))
+    near_w0, raw_1, up_1, far_a, ctx_own, near, far, near_c, dense_own, dense_c, kv_own, kv_other = window(
+        near_w0, raw_1, up_1, far_a, ctx_own, near, far, near_c, dense_own, dense_c, kv_own, kv_other
     )
 
-    up_got = send(up_own, ZSWAP)
-    dense_x = pack_rows(near, far)
-    dense_xc = send(dense_x, CORE)
-    ctx_own = in_plane(context.reshape(PLANE, -1, HEADS * HD))
-    hidden_out, normed = dense_norm(pos, hidden_in, ctx_own, [dense_own, dense_c, dense_x, dense_xc])
+    far_b = send(near_w0[:, :, part:], ZFAR)
+    near_w1 = in_plane(stack_rows(up_1, raw_1))
+    got_a = send(far_a, ZSWAP)
+    blocks = [dense_own, dense_c, near, far, near_c, send(far, CORE)]
+    hidden_out, normed = dense_norm(pos, hidden_in, ctx_own, blocks)
     from_y = send(normed, YSWAP)
     from_x = send(normed, XSWAP)
+    near_w0, near_w1, far_a, far_b, got_a, normed, from_y, from_x, kv_own, kv_other = window(
+        near_w0, near_w1, far_a, far_b, got_a, normed, from_y, from_x, kv_own, kv_other
+    )
+
+    got_b = send(far_b, ZSWAP)
     cross_low = send(from_y[: share // 2], XSWAP)
     cross_high = send(from_x[share // 2 :], YSWAP)
-    group_own = [normed, from_x]
-    group_other = [from_y, cross_low, cross_high]
-    group_own += [send(piece, CORE) for piece in group_own]
-    group_other += [send(piece, CORE) for piece in group_other]
-    up_own, up_got, kv_own, kv_other, *tokens = window(up_own, up_got, kv_own, kv_other, *group_own, *group_other)
-    group_own, group_other = tokens[:4], tokens[4:]
-
-    weights = [up_own, up_got]
-    act_got = [send(up_part(group_other, [w])[0], YSWAP) for w in weights]
-    act_own = up_part(group_own, weights)
-    kv_got = send(kv_other, YSWAP)
-    activated = join_parts(pos, *act_own, *act_got)
+    kv_got = send(window(kv_other, cross_high)[0], YSWAP)
+    other = [from_y, cross_low, cross_high]
+    other += [send(piece, CORE) for piece in other]
+    own = [normed, from_x, send(normed, CORE), send(from_x, CORE)]
+    near_w0, near_w1, far_a, far_b, got_a, *tokens = window(near_w0, near_w1, far_a, far_b, got_a, *other, *own)
+    other, own = tokens[:6], tokens[6:]
+    weights = [(near_w0, (far_a, far_b)), (near_w1, (got_a, got_b))]
+    parts = []
+    done = pos
+    for half, side, pieces in ((0, 1, other), (1, 1, other), (0, 0, own), (1, 0, own)):
+        first, _ = window(pieces[0], done)
+        done = up_part(pos, half, [first] + pieces[1:], *weights[half])
+        parts.append((send(done, YSWAP) if side else done, side, half, (0, 2, 1, 3)))
+    activated = join_parts(pos, (NM * share, up_master.shape[1] // NM), parts)
     cache = place_pages(pos, page_table, kv_own, kv_got)
     return hidden_out, activated, cache
 

time: 222 us -> 193 us (0.87)
  waiting for transfers between devices: 118 us -> 40.7 us
  blocking collectives: 11.7 us -> 46.2 us
  starting transfers between devices: 30.2 us -> 40.9 us
    ppermute x24 -> x30, waiting for transfers between devices: 118 us -> 40.7 us  [send(): return lax.ppermute(value, AXES, moves)]
    all_to_all x1 -> x2, blocking collectives: 11.7 us -> 46.2 us  [in_plane(): lax.all_to_all(pieces, AXES, split_axis=0, concat_axis=0, tiled=True, axi...]
    ppermute x24 -> x30, starting transfers between devices: 19.7 us -> 29.7 us  [send(): return lax.ppermute(value, AXES, moves)]
    pallas_call x6 -> x10, Pallas kernels: 35.3 us -> 43.2 us  [the longest x4 17.9 us: up_part(): pl.pallas_call(functools.partial(up_kernel, len(pieces), half), in_specs=...]
    all_to_all x0 -> x1, starting transfers between devices: none -> 3.74 us  [in_plane(): lax.all_to_all(pieces, AXES, split_axis=0, concat_axis=0, tiled=True, axi...]
    pallas_call x2 -> x1, Pallas kernels: 5.77 us -> 2.62 us  [pack_rows(): pl.pallas_call(pack_kernel, in_specs=[VMEM] * len(parts), out_specs=VMEM,...]
    all_to_all x2 -> x1, starting transfers between devices: 10.5 us -> 7.41 us  [to_all(): mine = lax.all_to_all(pieces, AXES, split_axis=0, concat_axis=0, tiled=True)]
    pallas_call x2 -> x1, Pallas kernels: 5.75 us -> 2.74 us  [cast_pieces(): pl.pallas_call(kernel, in_specs=[VMEM], out_specs=VMEM, out_shape=jax.Sha...]
  transfers between devices with their start and end apart: 26 -> 32, of which waited for: 10 -> 10; matrix products, arithmetic and copies ran while one was open for 2% -> 3% of each run, Pallas kernels for 19% -> 25%
where the time goes in v3:
time: 193 us
  Pallas kernels  52.7 us (27%)
  blocking collectives  46.2 us (24%)
  starting transfers between devices  40.9 us (21%)
  waiting for transfers between devices  40.7 us (21%)
  local copies, waits for them, and re-layouts  9.75 us (5%)
    all_to_all x2, blocking collectives, in_plane(): lax.all_to_all(pieces, AXES, split_axis=0, concat_axis=0, tiled=True, axi...  46.2 us
    ppermute x30, waiting for transfers between devices, send(): return lax.ppermute(value, AXES, moves)  40.7 us
    ppermute x30, starting transfers between devices, send(): return lax.ppermute(value, AXES, moves)  29.7 us
    pallas_call x4, Pallas kernels, up_part(): pl.pallas_call(functools.partial(up_kernel, len(pieces), half), in_specs=...  17.9 us
    pallas_call x1, Pallas kernels, two_heads(): pl.pallas_call(head_kernel, in_specs=[SMEM, SMEM, VMEM, VMEM] + [HBM] * 4...  9.35 us
    all_to_all x1, starting transfers between devices, to_all(): mine = lax.all_to_all(pieces, AXES, split_axis=0, concat_axis=0, tiled=True)  7.41 us
    pallas_call x1, Pallas kernels, dense_norm(): pl.pallas_call(dense_kernel, in_specs=[SMEM, VMEM, VMEM] + [HBM] * len(bl...  6.05 us
    unnamed x54, local copies, waits for them, and re-layouts  4.83 us
  transfers between devices with their start and end apart: 32, of which 10 were waited for; matrix products, arithmetic and copies ran while one was open for 3% of the time, Pallas kernels for 25%

profile of v3, /device:TPU:0, one launch (start us, length us, event | category | flops | bytes accessed | tf_op | source)
XLA Modules:
  0.0 192.5 jit_solution(16079363257714814726)
XLA Ops:
  0.6 2.7 %shard_map.85 = bf16[32,64,384]{2,1,0:T(8,128)(2,1)} custom-call(f32[64,6144]{1,0:T(8,128)} %src.2), custom_call_target="tpu_custom_call" | custom-call | tf_op jit(solution)/shard_map/pallas_call | solution.py:128
  3.4 7.4 %all-to-all-start = ((bf16[32,64,384]{2,1,0:T(8,128)(2,1)}), bf16[32,64,384]{2,1,0:T(8,128)(2,1)}, u32[]{:S(2)}, u32[]{:S(2)}) async-start(bf16[32,64,384]{2,1,0:T(8,128)(2,1)} %shard_map.85), calls=%async_computation | async-start | bytes 3145728 | tf_op jit(solution)/shard_map/all_to_all | solution.py:210
  16.7 2.7 %shard_map.88 = (bf16[8,64,512]{2,1,0:T(8,128)(2,1)}, bf16[8,64,512]{2,1,0:T(8,128)(2,1)}) custom-call(s32[3]{0:T(128)} %pad_add_fusion.1.pos, f32[64,8192]{1,0:T(8,128)} %src.3), custom_call_target="tpu_custom_call" | custom-call | tf_op jit(solution)/shard_map/pallas_call | solution.py:150
  21.4 2.3 %constant_dynamic-slice_fusion = bf16[256,2048]{1,0:T(8,128)(2,1)} fusion(bf16[512,2048]{1,0:T(8,128)(2,1)} %own, s32[]{:T(128)S(6)} %select_n.16), kind=kLoop, calls=%fused_computation.3 | loop fusion | bytes 2097156 | tf_op jit(solution)/shard_map/dynamic_slice | solution.py:455
  23.8 12.2 %collective-permute-done.refs_1_ = bf16[96,2048]{1,0:T(8,128)(2,1)S(1)} collective-permute-done((bf16[96,2048]{1,0:T(8,128)(2,1)}, bf16[96,2048]{1,0:T(8,128)(2,1)S(1)}, u32[]{:S(2)}, u32[]{:S(2)}) %collective-permute-start) | collective-permute-done | bytes 393248 | tf_op jit(solution)/shard_map/ppermute | solution.py:99
  36.0 2.3 %collective-permute-start.2 = (bf16[48,2048]{1,0:T(8,128)(2,1)S(1)}, bf16[48,2048]{1,0:T(8,128)(2,1)S(1)}, u32[]{:S(2)}, u32[]{:S(2)}) collective-permute-start(bf16[48,2048]{1,0:T(8,128)(2,1)S(1)} %slice.24), channel_id=1, source_target_pairs={{0,2},{1,3},{2,0},{3,1},{4,6},{5,7},{6,4},{7,5},{8,10},{9,11},{10,... | collective-permute-start | bytes 589832 | tf_op jit(solution)/shard_map/ppermute | solution.py:99
  39.6 5.1 %collective-permute-done.2.refs_3_ = bf16[48,2048]{1,0:T(8,128)(2,1)S(1)} collective-permute-done((bf16[48,2048]{1,0:T(8,128)(2,1)S(1)}, bf16[48,2048]{1,0:T(8,128)(2,1)S(1)}, u32[]{:S(2)}, u32[]{:S(2)}) %collective-permute-start.2) | collective-permute-done | bytes 196640 | tf_op jit(solution)/shard_map/ppermute | solution.py:99
  44.7 2.5 %collective-permute-done.3.refs_4_ = bf16[48,2048]{1,0:T(8,128)(2,1)S(1)} collective-permute-done((bf16[48,2048]{1,0:T(8,128)(2,1)S(1)}, bf16[48,2048]{1,0:T(8,128)(2,1)S(1)}, u32[]{:S(2)}, u32[]{:S(2)}) %collective-permute-start.3) | collective-permute-done | bytes 196640 | tf_op jit(solution)/shard_map/ppermute | solution.py:99
  47.9 2.6 %shard_map.87.mine = bf16[384,2048]{1,0:T(8,128)(2,1)} custom-call(bf16[96,2048]{1,0:T(8,128)(2,1)} %shard_map.86.refs_0_, bf16[96,2048]{1,0:T(8,128)(2,1)} %copy-done.13, bf16[96,2048]{1,0:T(8,128)(2,1)} %copy-done.14, bf16[48,2048]{1,0:T(8,128)(2,1)} %copy-done.23, bf16[48,2048]{1,0:T(8,128)(2,1)} %copy-done.24), custom_call_target="tpu_custom_call" | custom-call | tf_op jit(solution)/shard_map/pallas_call | solution.py:186
  52.7 2.3 %shard_map.89 = bf16[8,128,512]{2,1,0:T(8,128)(2,1)} custom-call(bf16[8,64,512]{2,1,0:T(8,128)(2,1)} %get-tuple-element.84.own, bf16[8,64,512]{2,1,0:T(8,128)(2,1)} %copy-done.19), custom_call_target="tpu_custom_call" | custom-call | tf_op jit(solution)/shard_map/pallas_call | solution.py:167
  55.0 33.8 %all_to_all.20.refs_6_.refs_4_ = bf16[8,128,512]{2,1,0:T(8,128)(2,1)S(1)} all-to-all(bf16[8,128,512]{2,1,0:T(8,128)(2,1)} %shard_map.89), channel_id=1, replica_groups={{0,1,2,3,4,5,6,7},{8,9,10,11,12,13,14,15},{16,17,18,19,20,21,22,23},{24..., dimensions={0} | all-to-all | bytes 2097152 | tf_op jit(solution)/shard_map/all_to_all | solution.py:215
  91.6 2.3 %collective-permute-start.11 = (bf16[8,128,256]{2,1,0:T(8,128)(2,1)}, bf16[8,128,256]{2,1,0:T(8,128)(2,1)S(1)}, u32[]{:S(2)}, u32[]{:S(2)}) collective-permute-start(bf16[8,128,256]{2,1,0:T(8,128)(2,1)} %slice.20), channel_id=1, source_target_pairs={{0,16},{1,17},{2,18},{3,19},{4,20},{5,21},{6,22},{7,23},{8,24},{9,... | collective-permute-start | bytes 1572872 | tf_op jit(solution)/shard_map/ppermute | solution.py:99
  96.5 9.3 %shard_map.90 = (bf16[768,256]{1,0:T(8,128)(2,1)}, bf16[3,2,2,128,128]{4,3,2,1,0:T(8,128)(2,1)}, bf16[3,2,2,128,128]{4,3,2,1,0:T(8,128)(2,1)}) custom-call(s32[3]{0:T(128)} %pad_add_fusion.1.pos, f32[2]{0:T(128)} %multiply_exponential_fusion.slope, s32[2,1,384]{2,1,0:T(1,128)} %broadcast_in_dim.6.seg_rows, s32[2,384,1]{2,1,0:T(8,128)} %copy.10.seg_cols, ...), custom_call_target="tpu_custom_call" | custom-call | tf_op jit(solution)/shard_map/pallas_call | solution.py:279
  105.8 12.4 %all_to_all.21.ctx = bf16[8,96,256]{2,1,0:T(8,128)(2,1)} all-to-all(bf16[8,96,256]{2,1,0:T(8,128)(2,1)} %bitcast.7), channel_id=1, replica_groups={{0,1,2,3,4,5,6,7},{8,9,10,11,12,13,14,15},{16,17,18,19,20,21,22,23},{24..., dimensions={0} | all-to-all | bytes 786432 | tf_op jit(solution)/shard_map/all_to_all | solution.py:215
  118.4 2.3 %shard_map.92 = bf16[8,128,512]{2,1,0:T(8,128)(2,1)} custom-call(bf16[8,64,512]{2,1,0:T(8,128)(2,1)} %get-tuple-element.107.own, bf16[8,64,512]{2,1,0:T(8,128)(2,1)} %collective-permute-done.10.got), custom_call_target="tpu_custom_call" | custom-call | tf_op jit(solution)/shard_map/pallas_call | solution.py:167
  120.7 3.7 %all-to-all-start.3 = ((bf16[8,128,512]{2,1,0:T(8,128)(2,1)}), bf16[8,128,512]{2,1,0:T(8,128)(2,1)S(1)}, u32[]{:S(2)}, u32[]{:S(2)}) async-start(bf16[8,128,512]{2,1,0:T(8,128)(2,1)} %shard_map.92), calls=%async_computation.3 | async-start | bytes 2097152 | tf_op jit(solution)/shard_map/all_to_all | solution.py:215
  128.0 6.1 %shard_map.91 = (bf16[96,2048]{1,0:T(8,128)(2,1)}, bf16[96,2048]{1,0:T(8,128)(2,1)}) custom-call(s32[3]{0:T(128)} %pad_add_fusion.1.pos, bf16[96,2048]{1,0:T(8,128)(2,1)} %hidden.3, bf16[8,96,256]{2,1,0:T(8,128)(2,1)} %all_to_all.21.ctx, bf16[512,2048]{1,0:T(8,128)(2,1)} %own, bf16[512,2048]{1,0:T(8,128)(2,1)} %copy-done.7, ...), custom_call_target="tpu_custom_call" | custom-call | tf_op jit(solution)/shard_map/pallas_call | solution.py:324
  137.4 13.6 %collective-permute-done.15.refs_8_.refs_6_ = bf16[8,128,256]{2,1,0:T(8,128)(2,1)S(1)} collective-permute-done((bf16[8,128,256]{2,1,0:T(8,128)(2,1)S(1)}, bf16[8,128,256]{2,1,0:T(8,128)(2,1)S(1)}, u32[]{:S(2)}, u32[]{:S(2)}) %collective-permute-start.15) | collective-permute-done | bytes 524320 | tf_op jit(solution)/shard_map/ppermute | solution.py:99
  155.1 2.5 %collective-permute-done.19.refs_1_ = bf16[48,2048]{1,0:T(8,128)(2,1)S(1)} collective-permute-done((bf16[48,2048]{1,0:T(8,128)(2,1)S(1)}, bf16[48,2048]{1,0:T(8,128)(2,1)S(1)}, u32[]{:S(2)}, u32[]{:S(2)}) %collective-permute-start.19) | collective-permute-done | bytes 196640 | tf_op jit(solution)/shard_map/ppermute | solution.py:99
  163.3 4.5 %shard_map.93 = bf16[384,512]{1,0:T(8,128)(2,1)} custom-call(s32[3]{0:T(128)} %pad_add_fusion.1.pos, bf16[96,2048]{1,0:T(8,128)(2,1)} %copy-done.3, bf16[48,2048]{1,0:T(8,128)(2,1)} %copy-done.15, bf16[48,2048]{1,0:T(8,128)(2,1)} %copy-done.16, bf16[96,2048]{1,0:T(8,128)(2,1)} %copy-done.10, bf16[48,2048]{1,0:T(8,128)(2,1)} %copy-done.17, ...), custom_call_target="tpu_custom_call" | custom-call | tf_op jit(solution)/shard_map/pallas_call | solution.py:376
  169.3 4.5 %shard_map.94 = bf16[384,512]{1,0:T(8,128)(2,1)} custom-call(s32[3]{0:T(128)} %pad_add_fusion.1.pos, bf16[96,2048]{1,0:T(8,128)(2,1)} %copy-done.3, bf16[48,2048]{1,0:T(8,128)(2,1)} %copy-done.15, bf16[48,2048]{1,0:T(8,128)(2,1)} %copy-done.16, bf16[96,2048]{1,0:T(8,128)(2,1)} %copy-done.10, bf16[48,2048]{1,0:T(8,128)(2,1)} %copy-done.17, ...), custom_call_target="tpu_custom_call" | custom-call | tf_op jit(solution)/shard_map/pallas_call | solution.py:376
  175.4 4.4 %shard_map.95.refs_2_ = bf16[384,512]{1,0:T(8,128)(2,1)} custom-call(s32[3]{0:T(128)} %pad_add_fusion.1.pos, bf16[96,2048]{1,0:T(8,128)(2,1)} %get-tuple-element.139.refs_0_, bf16[96,2048]{1,0:T(8,128)(2,1)} %copy-done.2, bf16[96,2048]{1,0:T(8,128)(2,1)} %copy-done.8, bf16[96,2048]{1,0:T(8,128)(2,1)} %copy-done.9, bf16[8,128,512]{2,1,0:T(8,128)(2,1)} %copy-done, ...), custom_call_target="tpu_custom_call" | custom-call | tf_op jit(solution)/shard_map/pallas_call | solution.py:376
  179.8 4.4 %shard_map.96.refs_3_ = bf16[384,512]{1,0:T(8,128)(2,1)} custom-call(s32[3]{0:T(128)} %pad_add_fusion.1.pos, bf16[96,2048]{1,0:T(8,128)(2,1)} %get-tuple-element.139.refs_0_, bf16[96,2048]{1,0:T(8,128)(2,1)} %copy-done.2, bf16[96,2048]{1,0:T(8,128)(2,1)} %copy-done.8, bf16[96,2048]{1,0:T(8,128)(2,1)} %copy-done.9, bf16[8,128,512]{2,1,0:T(8,128)(2,1)} %copy-done.1, ...), custom_call_target="tpu_custom_call" | custom-call | tf_op jit(solution)/shard_map/pallas_call | solution.py:376
  189.9 2.6 %shard_map.97 = bf16[384,2048]{1,0:T(8,128)(2,1)} custom-call(s32[3]{0:T(128)} %pad_add_fusion.1.pos, bf16[384,512]{1,0:T(8,128)(2,1)} %copy-done.21, bf16[384,512]{1,0:T(8,128)(2,1)} %copy-done.22, bf16[384,512]{1,0:T(8,128)(2,1)} %shard_map.95.refs_2_, bf16[384,512]{1,0:T(8,128)(2,1)} %shard_map.96.refs_3_), custom_call_target="tpu_custom_call" | custom-call | tf_op jit(solution)/shard_map/pallas_call | solution.py:404
  (122 shorter events, 42.7 us)
Async XLA Ops:
  3.4 47.1 %all-to-all-start = ((bf16[32,64,384]{2,1,0:T(8,128)(2,1)}), bf16[32,64,384]{2,1,0:T(8,128)(2,1)}, u32[]{:S(2)}, u32[]{:S(2)}) async-start(bf16[32,64,384]{2,1,0:T(8,128)(2,1)} %shard_map.85), calls=%async_computation | async-start | bytes 3145728 | tf_op jit(solution)/shard_map/all_to_all | solution.py:210
  12.9 23.1 %collective-permute-start = (bf16[96,2048]{1,0:T(8,128)(2,1)}, bf16[96,2048]{1,0:T(8,128)(2,1)S(1)}, u32[]{:S(2)}, u32[]{:S(2)}) collective-permute-start(bf16[96,2048]{1,0:T(8,128)(2,1)} %shard_map.86.refs_0_), channel_id=1, source_target_pairs={{0,4},{1,5},{2,6},{3,7},{4,0},{5,1},{6,2},{7,3},{8,12},{9,13},{10,... | collective-permute-start | bytes 1179656 | tf_op jit(solution)/shard_map/ppermute | solution.py:99
  14.6 23.7 %collective-permute-start.1 = (bf16[96,2048]{1,0:T(8,128)(2,1)}, bf16[96,2048]{1,0:T(8,128)(2,1)S(1)}, u32[]{:S(2)}, u32[]{:S(2)}) collective-permute-start(bf16[96,2048]{1,0:T(8,128)(2,1)} %shard_map.86.refs_0_), channel_id=1, source_target_pairs={{0,2},{1,3},{2,0},{3,1},{4,6},{5,7},{6,4},{7,5},{8,10},{9,11},{10,... | collective-permute-start | bytes 1179656 | tf_op jit(solution)/shard_map/ppermute | solution.py:99
  19.4 31.1 %collective-permute-start.4 = (bf16[8,64,512]{2,1,0:T(8,128)(2,1)}, bf16[8,64,512]{2,1,0:T(8,128)(2,1)S(1)}, u32[]{:S(2)}, u32[]{:S(2)}) collective-permute-start(bf16[8,64,512]{2,1,0:T(8,128)(2,1)} %get-tuple-element.107.own), channel_id=1, source_target_pairs={{0,8},{1,9},{2,10},{3,11},{4,12},{5,13},{6,14},{7,15},{8,0},{9,1},... | collective-permute-start | bytes 1572872 | tf_op jit(solution)/shard_map/ppermute | solution.py:99
  20.9 18.1 %collective-permute-start.5 = (s32[1,384]{1,0:T(1,128)S(1)}, s32[1,384]{1,0:T(1,128)S(1)}, u32[]{:S(2)}, u32[]{:S(2)}) collective-permute-start(s32[1,384]{1,0:T(1,128)S(1)} %copy-done.25), channel_id=1, source_target_pairs={{0,4},{1,5},{2,6},{3,7},{4,0},{5,1},{6,2},{7,3},{8,12},{9,13},{10,... | collective-permute-start | bytes 4616 | tf_op jit(solution)/shard_map/ppermute | solution.py:99
  38.3 8.9 %collective-permute-start.3 = (bf16[48,2048]{1,0:T(8,128)(2,1)S(1)}, bf16[48,2048]{1,0:T(8,128)(2,1)S(1)}, u32[]{:S(2)}, u32[]{:S(2)}) collective-permute-start(bf16[48,2048]{1,0:T(8,128)(2,1)S(1)} %slice.25), channel_id=1, source_target_pairs={{0,4},{1,5},{2,6},{3,7},{4,0},{5,1},{6,2},{7,3},{8,12},{9,13},{10,... | collective-permute-start | bytes 589832 | tf_op jit(solution)/shard_map/ppermute | solution.py:99
  50.5 38.3 %collective-permute-start.9 = (bf16[512,2048]{1,0:T(8,128)(2,1)}, bf16[512,2048]{1,0:T(8,128)(2,1)S(1)}, u32[]{:S(2)}, u32[]{:S(2)}) collective-permute-start(bf16[512,2048]{1,0:T(8,128)(2,1)} %own), channel_id=1, source_target_pairs={{0,1},{1,0},{2,3},{3,2},{4,5},{5,4},{6,7},{7,6},{8,9},{9,8},{10,11... | collective-permute-start | bytes 6291464 | tf_op jit(solution)/shard_map/ppermute | solution.py:99
  50.6 38.2 %collective-permute-start.6 = (bf16[2048,384]{1,0:T(8,128)(2,1)}, bf16[2048,384]{1,0:T(8,128)(2,1)S(1)}, u32[]{:S(2)}, u32[]{:S(2)}) collective-permute-start(bf16[2048,384]{1,0:T(8,128)(2,1)} %bitcast.w_own), channel_id=1, source_target_pairs={{0,8},{1,9},{2,10},{3,11},{4,12},{5,13},{6,14},{7,15},{8,0},{9,1},... | collective-permute-start | bytes 4718600 | tf_op jit(solution)/shard_map/ppermute | solution.py:99
  50.9 37.8 %collective-permute-start.7 = (bf16[384,2048]{1,0:T(8,128)(2,1)}, bf16[384,2048]{1,0:T(8,128)(2,1)S(1)}, u32[]{:S(2)}, u32[]{:S(2)}) collective-permute-start(bf16[384,2048]{1,0:T(8,128)(2,1)} %shard_map.87.mine), channel_id=1, source_target_pairs={{0,1},{1,0},{2,3},{3,2},{4,5},{5,4},{6,7},{7,6},{8,9},{9,8},{10,11... | collective-permute-start | bytes 4718600 | tf_op jit(solution)/shard_map/ppermute | solution.py:99
  51.1 37.7 %collective-permute-start.8 = (bf16[256,2048]{1,0:T(8,128)(2,1)}, bf16[256,2048]{1,0:T(8,128)(2,1)}, u32[]{:S(2)}, u32[]{:S(2)}) collective-permute-start(bf16[256,2048]{1,0:T(8,128)(2,1)} %constant_dynamic-slice_fusion), channel_id=1, source_target_pairs={{0,2},{1,3},{2,0},{3,1},{4,6},{5,7},{6,4},{7,5},{8,10},{9,11},{10,... | collective-permute-start | bytes 3145736 | tf_op jit(solution)/shard_map/ppermute | solution.py:99
  88.8 29.5 %collective-permute-start.12 = (bf16[256,2048]{1,0:T(8,128)(2,1)}, bf16[256,2048]{1,0:T(8,128)(2,1)}, u32[]{:S(2)}, u32[]{:S(2)}) collective-permute-start(bf16[256,2048]{1,0:T(8,128)(2,1)} %collective-permute-done.8.rest_0_), channel_id=1, source_target_pairs={{0,4},{1,5},{2,6},{3,7},{4,0},{5,1},{6,2},{7,3},{8,12},{9,13},{10,... | collective-permute-start | bytes 3145736 | tf_op jit(solution)/shard_map/ppermute | solution.py:99
  89.5 28.8 %collective-permute-start.13 = (bf16[256,2048]{1,0:T(8,128)(2,1)}, bf16[256,2048]{1,0:T(8,128)(2,1)}, u32[]{:S(2)}, u32[]{:S(2)}) collective-permute-start(bf16[256,2048]{1,0:T(8,128)(2,1)} %collective-permute-done.8.rest_0_), channel_id=1, source_target_pairs={{0,1},{1,0},{2,3},{3,2},{4,5},{5,4},{6,7},{7,6},{8,9},{9,8},{10,11... | collective-permute-start | bytes 3145736 | tf_op jit(solution)/shard_map/ppermute | solution.py:99
  91.6 26.7 %collective-permute-start.11 = (bf16[8,128,256]{2,1,0:T(8,128)(2,1)}, bf16[8,128,256]{2,1,0:T(8,128)(2,1)S(1)}, u32[]{:S(2)}, u32[]{:S(2)}) collective-permute-start(bf16[8,128,256]{2,1,0:T(8,128)(2,1)} %slice.20), channel_id=1, source_target_pairs={{0,16},{1,17},{2,18},{3,19},{4,20},{5,21},{6,22},{7,23},{8,24},{9,... | collective-permute-start | bytes 1572872 | tf_op jit(solution)/shard_map/ppermute | solution.py:99
  93.8 24.4 %collective-permute-start.10 = (bf16[8,64,512]{2,1,0:T(8,128)(2,1)}, bf16[8,64,512]{2,1,0:T(8,128)(2,1)}, u32[]{:S(2)}, u32[]{:S(2)}) collective-permute-start(bf16[8,64,512]{2,1,0:T(8,128)(2,1)} %get-tuple-element.84.own), channel_id=1, source_target_pairs={{0,8},{1,9},{2,10},{3,11},{4,12},{5,13},{6,14},{7,15},{8,0},{9,1},... | collective-permute-start | bytes 1572872 | tf_op jit(solution)/shard_map/ppermute | solution.py:99
  118.3 9.7 %collective-permute-start.14 = (bf16[256,2048]{1,0:T(8,128)(2,1)}, bf16[256,2048]{1,0:T(8,128)(2,1)}, u32[]{:S(2)}, u32[]{:S(2)}) collective-permute-start(bf16[256,2048]{1,0:T(8,128)(2,1)} %collective-permute-done.12.rest_1_), channel_id=1, source_target_pairs={{0,1},{1,0},{2,3},{3,2},{4,5},{5,4},{6,7},{7,6},{8,9},{9,8},{10,11... | collective-permute-start | bytes 3145736 | tf_op jit(solution)/shard_map/ppermute | solution.py:99
  120.7 30.4 %all-to-all-start.3 = ((bf16[8,128,512]{2,1,0:T(8,128)(2,1)}), bf16[8,128,512]{2,1,0:T(8,128)(2,1)S(1)}, u32[]{:S(2)}, u32[]{:S(2)}) async-start(bf16[8,128,512]{2,1,0:T(8,128)(2,1)} %shard_map.92), calls=%async_computation.3 | async-start | bytes 2097152 | tf_op jit(solution)/shard_map/all_to_all | solution.py:215
  124.5 26.5 %collective-permute-start.15 = (bf16[8,128,256]{2,1,0:T(8,128)(2,1)S(1)}, bf16[8,128,256]{2,1,0:T(8,128)(2,1)S(1)}, u32[]{:S(2)}, u32[]{:S(2)}) collective-permute-start(bf16[8,128,256]{2,1,0:T(8,128)(2,1)S(1)} %slice.21), channel_id=1, source_target_pairs={{0,16},{1,17},{2,18},{3,19},{4,20},{5,21},{6,22},{7,23},{8,24},{9,... | collective-permute-start | bytes 1572872 | tf_op jit(solution)/shard_map/ppermute | solution.py:99
  126.3 24.8 %collective-permute-start.16 = (bf16[8,128,256]{2,1,0:T(8,128)(2,1)S(1)}, bf16[8,128,256]{2,1,0:T(8,128)(2,1)}, u32[]{:S(2)}, u32[]{:S(2)}) collective-permute-start(bf16[8,128,256]{2,1,0:T(8,128)(2,1)S(1)} %collective-permute-done.11.refs_7_.refs_5_), channel_id=1, source_target_pairs={{0,8},{1,9},{2,10},{3,11},{4,12},{5,13},{6,14},{7,15},{8,0},{9,1},... | collective-permute-start | bytes 1572872 | tf_op jit(solution)/shard_map/ppermute | solution.py:99
  134.1 17.0 %collective-permute-start.17 = (bf16[96,2048]{1,0:T(8,128)(2,1)}, bf16[96,2048]{1,0:T(8,128)(2,1)S(1)}, u32[]{:S(2)}, u32[]{:S(2)}) collective-permute-start(bf16[96,2048]{1,0:T(8,128)(2,1)} %get-tuple-element.139.refs_0_), channel_id=1, source_target_pairs={{0,4},{1,5},{2,6},{3,7},{4,0},{5,1},{6,2},{7,3},{8,12},{9,13},{10,... | collective-permute-start | bytes 1179656 | tf_op jit(solution)/shard_map/ppermute | solution.py:99
  135.9 15.2 %collective-permute-start.18 = (bf16[96,2048]{1,0:T(8,128)(2,1)}, bf16[96,2048]{1,0:T(8,128)(2,1)S(1)}, u32[]{:S(2)}, u32[]{:S(2)}) collective-permute-start(bf16[96,2048]{1,0:T(8,128)(2,1)} %get-tuple-element.139.refs_0_), channel_id=1, source_target_pairs={{0,2},{1,3},{2,0},{3,1},{4,6},{5,7},{6,4},{7,5},{8,10},{9,11},{10,... | collective-permute-start | bytes 1179656 | tf_op jit(solution)/shard_map/ppermute | solution.py:99
  154.4 14.1 %collective-permute-start.27 = (bf16[8,128,256]{2,1,0:T(8,128)(2,1)S(1)}, bf16[8,128,256]{2,1,0:T(8,128)(2,1)S(1)}, u32[]{:S(2)}, u32[]{:S(2)}) collective-permute-start(bf16[8,128,256]{2,1,0:T(8,128)(2,1)S(1)} %collective-permute-done.15.refs_8_.refs_6_), channel_id=1, source_target_pairs={{0,8},{1,9},{2,10},{3,11},{4,12},{5,13},{6,14},{7,15},{8,0},{9,1},... | collective-permute-start | bytes 1572872 | tf_op jit(solution)/shard_map/ppermute | solution.py:99
  161.1 23.2 %collective-permute-start.29 = (bf16[3,2,2,128,128]{4,3,2,1,0:T(8,128)(2,1)S(1)}, bf16[3,2,2,128,128]{4,3,2,1,0:T(8,128)(2,1)S(1)}, u32[]{:S(2)}, u32[]{:S(2)}) collective-permute-start(bf16[3,2,2,128,128]{4,3,2,1,0:T(8,128)(2,1)S(1)} %copy-done.26), channel_id=1, source_target_pairs={{0,4},{1,5},{2,6},{3,7},{4,0},{5,1},{6,2},{7,3},{8,12},{9,13},{10,... | collective-permute-start | bytes 1179656 | tf_op jit(solution)/shard_map/ppermute | solution.py:99
  167.9 19.2 %collective-permute-start.26 = (bf16[384,512]{1,0:T(8,128)(2,1)}, bf16[384,512]{1,0:T(8,128)(2,1)S(1)}, u32[]{:S(2)}, u32[]{:S(2)}) collective-permute-start(bf16[384,512]{1,0:T(8,128)(2,1)} %shard_map.93), channel_id=1, source_target_pairs={{0,4},{1,5},{2,6},{3,7},{4,0},{5,1},{6,2},{7,3},{8,12},{9,13},{10,... | collective-permute-start | bytes 1179656 | tf_op jit(solution)/shard_map/ppermute | solution.py:99
  173.8 15.4 %collective-permute-start.28 = (bf16[384,512]{1,0:T(8,128)(2,1)}, bf16[384,512]{1,0:T(8,128)(2,1)S(1)}, u32[]{:S(2)}, u32[]{:S(2)}) collective-permute-start(bf16[384,512]{1,0:T(8,128)(2,1)} %shard_map.94), channel_id=1, source_target_pairs={{0,4},{1,5},{2,6},{3,7},{4,0},{5,1},{6,2},{7,3},{8,12},{9,13},{10,... | collective-permute-start | bytes 1179656 | tf_op jit(solution)/shard_map/ppermute | solution.py:99
  (35 other events, 251.2 us)

commit v4 on v3

--- a/solution.py
+++ b/solution.py
@@ -14,6 +14,7 @@
 BF = jnp.bfloat16
 F32 = jnp.float32
 VMEM_LIMIT = 56 * 1024 * 1024
+SMALL_LIMIT = 16 * 1024 * 1024
 
 
 def layer_norm(values):
@@ -103,8 +104,8 @@
     return lax.optimization_barrier(values)
 
 
-def params(**more):
-    return pltpu.CompilerParams(vmem_limit_bytes=VMEM_LIMIT, **more)
+def params(limit=VMEM_LIMIT):
+    return pltpu.CompilerParams(vmem_limit_bytes=limit)
 
 
 HBM = pl.BlockSpec(memory_space=pltpu.HBM)
@@ -173,25 +174,6 @@
     )(own, got)
 
 
-def pack_kernel(*refs):
-    *parts, out = refs
-    at = 0
-    for part in parts:
-        out[at : at + part.shape[0]] = part[...]
-        at += part.shape[0]
-
-
-def pack_rows(*parts):
-    rows = sum(part.shape[0] for part in parts)
-    return pl.pallas_call(
-        pack_kernel,
-        in_specs=[VMEM] * len(parts),
-        out_specs=VMEM,
-        out_shape=jax.ShapeDtypeStruct((rows, parts[0].shape[1]), BF),
-        compiler_params=params(),
-    )(*parts)
-
-
 def norm_kernel(hidden, out):
     out[...] = layer_norm(hidden[...].astype(F32)).astype(BF)
 
@@ -215,36 +197,28 @@
     return lax.all_to_all(pieces, AXES, split_axis=0, concat_axis=0, tiled=True, axis_index_groups=PLANES)
 
 
-def token_copies(y, m, mine, other, xbuf, sem):
-    share = mine.shape[0] // NM
+TOKEN_PIECES = 10
+
+
+def token_copies(y, m, pieces, xbuf, sem):
+    share = pieces[0].shape[0]
     half = share // 2
-    place = [(0, 0, 0, share), (1, 0, 0, share), (0, 2, 0, share), (1, 2, 0, half), (1, 2, half, half)]
+    place = [(0, 0, 0), (1, 0, 0), (0, 2, 0), (1, 2, 0), (1, 2, half)]
+    place += [(dy, dm ^ 1, extra) for dy, dm, extra in place]
     copies = []
-    for side, src in ((0, mine), (1, other)):
-        at = 0
-        for dy, dm, extra, rows in place:
-            first = pl.multiple_of(((y ^ dy) * NM + (m ^ dm ^ side)) * share + extra, 16)
-            copies.append(
-                pltpu.make_async_copy(
-                    src.at[pl.ds(at, rows)], xbuf.at[pl.ds(first, rows)], sem.at[len(copies)]
-                )
-            )
-            at += rows
+    for i, (dy, dm, extra) in enumerate(place):
+        first = pl.multiple_of(((y ^ dy) * NM + (m ^ dm)) * share + extra, 16)
+        copies.append(pltpu.make_async_copy(pieces[i], xbuf.at[pl.ds(first, pieces[i].shape[0])], sem.at[i]))
     return copies
 
 
-TOKEN_COPIES = 10
-
-
-def head_kernel(pos, slope, seg_rows, seg_cols, mine, other, w_own, w_got, ctx, kv_own, kv_other, xbuf, wbuf, xsem, wsem):
+def head_kernel(last, pos, slope, seg_rows, *refs):
+    pieces, refs = refs[:TOKEN_PIECES], refs[TOKEN_PIECES:]
+    if last:
+        before, refs = refs[:3], refs[3:]
+    weights, ctx, kv_own, kv_other, xbuf, wbuf, xsem, wsem = refs
     z, y, m = pos[0], pos[1], pos[2]
-    width = w_own.shape[1]
-    copies = [
-        pltpu.make_async_copy(
-            src, wbuf.at[:, pl.ds(pl.multiple_of((z % 2 ^ i) * width, width), width)], wsem.at[i]
-        )
-        for i, src in enumerate((w_own, w_got))
-    ] + token_copies(y, m, mine, other, xbuf, xsem)
+    copies = [pltpu.make_async_copy(weights, wbuf, wsem)] + token_copies(y, m, pieces, xbuf, xsem)
     for copy in copies:
         copy.start()
     group = xbuf.shape[0] // NY
@@ -252,57 +226,61 @@
     there = lax.broadcasted_iota(jnp.int32, (group, group), 1)
     distance = here - there
     away = distance.astype(F32)
+    h = 1 - z % 2 if last else z % 2
+    if last:
+        for src, dst in zip(before, (ctx, kv_own, kv_other)):
+            dst[...] = src[...]
     for copy in copies:
         copy.wait()
     for g, kv in ((0, kv_own), (1, kv_other)):
-        first = pl.multiple_of((y ^ g) * group, group)
-        rows = pl.ds(first, group)
-        allowed = (seg_cols[g] == seg_rows[g]) & (distance >= 0)
+        rows = pl.ds(pl.multiple_of((y ^ g) * group, group), group)
+        seg_cols = jnp.broadcast_to(seg_rows[g], (PAGE, group)).T[:, :1]
+        allowed = (seg_cols == seg_rows[g]) & (distance >= 0)
         joined = jnp.dot(xbuf[rows, :], wbuf[...], preferred_element_type=F32).astype(BF)
-        for h in range(HEADS):
-            query, keys, vals = (joined[:, (3 * h + i) * HD : (3 * h + i + 1) * HD] for i in range(3))
-            scores = lax.dot_general(query, keys, (((1,), (1,)), ((), ())), preferred_element_type=F32)
-            scores = scores * (1.0 / HD**0.5) - slope[h] * away
-            scores = jnp.where(allowed, scores, -jnp.inf)
-            raised = jnp.exp(scores - jnp.max(scores, -1, keepdims=True))
-            probs = (raised * (1.0 / jnp.sum(raised, -1, keepdims=True))).astype(BF)
-            ctx[rows, h * HD : (h + 1) * HD] = jnp.dot(probs, vals, preferred_element_type=F32).astype(BF)
-            for b in range(group // PAGE):
-                kv[b, 0, h] = keys[b * PAGE : (b + 1) * PAGE]
-                kv[b, 1, h] = vals[b * PAGE : (b + 1) * PAGE]
-
-
-def two_heads(pos, slope, seg_rows, seg_cols, tokens, w_own, w_got):
-    count, depth = 2 * tokens[0].shape[0], tokens[0].shape[1]
-    width = w_own.shape[1]
+        query, keys, vals = (joined[:, j * HD : (j + 1) * HD] for j in range(3))
+        scores = lax.dot_general(query, keys, (((1,), (1,)), ((), ())), preferred_element_type=F32)
+        scores = scores * (1.0 / HD**0.5) - slope[h] * away
+        scores = jnp.where(allowed, scores, -jnp.inf)
+        raised = jnp.exp(scores - jnp.max(scores, -1, keepdims=True))
+        probs = (raised * (1.0 / jnp.sum(raised, -1, keepdims=True))).astype(BF)
+        result = jnp.dot(probs, vals, preferred_element_type=F32).astype(BF)
+        ctx[rows, pl.ds(pl.multiple_of(h * HD, HD), HD)] = result
+        for b in range(group // PAGE):
+            kv[b, 0, h] = keys[b * PAGE : (b + 1) * PAGE]
+            kv[b, 1, h] = vals[b * PAGE : (b + 1) * PAGE]
+
+
+def one_head(pos, slope, seg_rows, tokens, weights, before=()):
+    count, depth = PLANE * tokens[0].shape[0], tokens[0].shape[1]
+    width = weights.shape[1]
     kv_shape = jax.ShapeDtypeStruct((count // NY // PAGE, 2, HEADS, PAGE, HD), BF)
     return pl.pallas_call(
-        head_kernel,
-        in_specs=[SMEM, SMEM, VMEM, VMEM] + [HBM] * 4,
+        functools.partial(head_kernel, bool(before)),
+        in_specs=[SMEM, SMEM, VMEM] + [ANY] * TOKEN_PIECES + [VMEM] * len(before) + [HBM],
         out_specs=[VMEM, VMEM, VMEM],
         out_shape=[jax.ShapeDtypeStruct((count, HEADS * HD), BF), kv_shape, kv_shape],
         scratch_shapes=[
             pltpu.VMEM((count, depth), BF),
-            pltpu.VMEM((depth, HEADS * width), BF),
-            pltpu.SemaphoreType.DMA((TOKEN_COPIES,)),
-            pltpu.SemaphoreType.DMA((2,)),
+            pltpu.VMEM((depth, width), BF),
+            pltpu.SemaphoreType.DMA((TOKEN_PIECES,)),
+            pltpu.SemaphoreType.DMA,
         ],
         compiler_params=params(),
-    )(pos, slope, seg_rows, seg_cols, *tokens, w_own, w_got)
+    )(pos, slope, seg_rows, *tokens, *before, weights)
 
 
 def dense_kernel(pos, hidden, ctx, own, cross, *rest):
-    halves, (out, normed, dense, sem) = rest[:4], rest[4:]
+    rows, (out, normed, dense, sem) = rest[:6], rest[6:]
     y, m = pos[1], pos[2]
     size = own.shape[0]
     half = size // 2
     loads = [[pltpu.make_async_copy(own, dense.at[0], sem.at[0])], [pltpu.make_async_copy(cross, dense.at[1], sem.at[1])]]
     for r in (2, 3):
         copies = []
-        for i in range(2):
-            first = pl.multiple_of((y ^ i) * half, half)
-            index = (r - 2) * 2 + i
-            copies.append(pltpu.make_async_copy(halves[index], dense.at[r, pl.ds(first, half)], sem.at[2 + index]))
+        for i, first in enumerate((y * half, (1 - y) * half, (1 - y) * half + half // 2)):
+            index = (r - 2) * 3 + i
+            dst = dense.at[r, pl.ds(pl.multiple_of(first, half // 2), rows[index].shape[0])]
+            copies.append(pltpu.make_async_copy(rows[index], dst, sem.at[2 + index]))
         loads.append(copies)
     for copies in loads:
         for copy in copies:
@@ -335,21 +313,20 @@
 
 
 def up_kernel(count, half, pos, *refs):
-    pieces, (near, *fars), (act, xbuf, wbuf, xsem, wsem) = refs[:count], refs[count:-5], refs[-5:]
+    pieces, (*nears, far_a, far_b), (act, xbuf, wbuf, xsem, wsem) = refs[:count], refs[count:-5], refs[-5:]
     z = pos[0]
-    rows, width = near.shape[1] // 2, wbuf.shape[3]
+    fars = (far_a, far_b)
+    rows, width = wbuf.shape[2], wbuf.shape[3]
     loads = [[] for _ in range(NZ)]
     for side in range(2):
-        src = near.at[:, side * rows : (side + 1) * rows]
+        src = nears[side] if len(nears) == 2 else nears[0].at[:, side * rows : (side + 1) * rows]
         loads[side].append(pltpu.make_async_copy(src, wbuf.at[side], wsem.at[side, 0]))
+        r = 2 + (side ^ half)
         at = 0
         for i, far in enumerate(fars):
-            part = far.shape[2]
-            src = far.at[:, side * rows : (side + 1) * rows]
-            r = 2 + (side ^ half)
-            dst = wbuf.at[r, :, :, at : at + part]
-            loads[r].append(pltpu.make_async_copy(src, dst, wsem.at[r, i]))
-            at += part
+            dst = wbuf.at[r, at : at + far.shape[0]]
+            loads[r].append(pltpu.make_async_copy(far.at[:, side * rows : (side + 1) * rows], dst, wsem.at[r, i]))
+            at += far.shape[0]
     copies = []
     at = 0
     for i, piece in enumerate(pieces):
@@ -370,22 +347,22 @@
     act[...] = jax.nn.gelu(upper, approximate=True).astype(BF)
 
 
-def up_part(pos, half, pieces, near, fars):
+def up_part(pos, half, pieces, nears, fars):
     rows, depth = sum(piece.shape[0] for piece in pieces), pieces[0].shape[1]
-    width = near.shape[2]
+    count, rows_in, width = 2 * fars[0].shape[0], fars[0].shape[1] // 2, nears[0].shape[2]
     return pl.pallas_call(
         functools.partial(up_kernel, len(pieces), half),
-        in_specs=[SMEM] + [ANY] * len(pieces) + [HBM] * (1 + len(fars)),
+        in_specs=[SMEM] + [ANY] * len(pieces) + [HBM] * (len(nears) + len(fars)),
         out_specs=VMEM,
         out_shape=jax.ShapeDtypeStruct((rows, width), BF),
         scratch_shapes=[
             pltpu.VMEM((rows, depth), BF),
-            pltpu.VMEM((NZ, near.shape[0], near.shape[1] // 2, width), BF),
+            pltpu.VMEM((NZ, count, rows_in, width), BF),
             pltpu.SemaphoreType.DMA((len(pieces),)),
             pltpu.SemaphoreType.DMA((NZ, len(fars))),
         ],
-        compiler_params=params(),
-    )(pos, *pieces, near, *fars)
+        compiler_params=params(SMALL_LIMIT),
+    )(pos, *pieces, *nears, *fars)
 
 
 def join_kernel(places, pos, *refs):
@@ -406,7 +383,7 @@
         in_specs=[SMEM] + [VMEM] * len(parts),
         out_specs=VMEM,
         out_shape=jax.ShapeDtypeStruct(shape, BF),
-        compiler_params=params(),
+        compiler_params=params(SMALL_LIMIT),
     )(pos, *(part[0] for part in parts))
 
 
@@ -426,7 +403,7 @@
         in_specs=[SMEM, SMEM, VMEM, VMEM],
         out_specs=VMEM,
         out_shape=jax.ShapeDtypeStruct((blocks, two, NY * heads, page, width), BF),
-        compiler_params=params(),
+        compiler_params=params(SMALL_LIMIT),
     )(pos, table, own, got)
 
 
@@ -450,57 +427,62 @@
     from_x = send(normed, XSWAP)
     cross_low = send(from_y[: share // 2], XSWAP)
     cross_high = send(from_x[share // 2 :], YSWAP)
-    mine = pack_rows(normed, from_y, from_x, cross_low, cross_high)
+    tokens = [normed, from_y, from_x, cross_low, cross_high]
     half = dense_weight.shape[0] // 2
     give = lax.dynamic_slice_in_dim(dense_weight, y * half, half, 0)
+    give_far = lax.dynamic_slice_in_dim(dense_weight, (1 - y) * half + half // 2, half // 2, 0)
     seg_other = send(segment_ids, YSWAP)
     segments = jnp.concatenate([segment_ids, seg_other], 0)
-    seg_rows, seg_cols = segments[:, None, :], segments[:, :, None]
-    qkv_own, mine, up_0, up_1, raw_0, give, seg_rows, seg_cols, slopes, pos, dense_own = window(
-        qkv_own, mine, up_0, up_1, raw_0, give, seg_rows, seg_cols, slopes, pos, dense_weight
+    seg_rows = segments[:, None, :]
+    tokens += [send(piece, CORE) for piece in tokens[:3]]
+    qkv_own, up_0, up_1, raw_0, give, give_far, seg_rows, slopes, pos, dense_own, *tokens = window(
+        qkv_own, up_0, up_1, raw_0, give, give_far, seg_rows, slopes, pos, dense_weight, *tokens
     )
 
     qkv_got = send(qkv_own, ZSWAP)
-    near_w0 = in_plane(stack_rows(up_0, raw_0))
-    other = send(mine, CORE)
+    near_0 = in_plane(stack_rows(up_0, raw_0))
     near = send(give, XSWAP)
     dense_c = send(dense_own, CORE)
-    qkv_own, qkv_got, near_w0, up_0, up_1, mine, other, near, dense_own, dense_c = window(
-        qkv_own, qkv_got, near_w0, up_0, up_1, mine, other, near, dense_own, dense_c
+    tokens += [send(piece, CORE) for piece in tokens[3:5]]
+    before = one_head(pos, slopes, seg_rows, tokens, qkv_own)
+    qkv_got, near_0, up_1, near, give_far, dense_own, dense_c, *state = window(
+        qkv_got, near_0, up_1, near, give_far, dense_own, dense_c, *tokens, *before
     )
-
-    part = near_w0.shape[2] // 2
-    far_a = send(near_w0[:, :, :part], ZFAR)
-    raw_1 = send(up_0, ZSWAP)
-    far = send(near, YSWAP)
-    near_c = send(near, CORE)
-    context, kv_own, kv_other = two_heads(pos, slopes, seg_rows, seg_cols, (mine, other), qkv_own, qkv_got)
+    tokens, before = state[:TOKEN_PIECES], state[TOKEN_PIECES:]
+
+    part = PLANE // 2
+    far_a = send(near_0[:part], ZFAR)
+    near_got = send(near_0[:, : near_0.shape[1] // 2], ZSWAP)
+    far_y = send(near[: half // 2], YSWAP)
+    far_x = send(give_far, XSWAP)
+    context, kv_own, kv_other = one_head(pos, slopes, seg_rows, tokens, qkv_got, before)
     ctx_own = in_plane(context.reshape(PLANE, -1, HEADS * HD))
-    near_w0, raw_1, up_1, far_a, ctx_own, near, far, near_c, dense_own, dense_c, kv_own, kv_other = window(
-        near_w0, raw_1, up_1, far_a, ctx_own, near, far, near_c, dense_own, dense_c, kv_own, kv_other
+    kv_got = send(kv_other, YSWAP)
+    near_0, near_got, up_1, far_a, ctx_own, near, far_y, far_x, dense_own, dense_c, kv_own, kv_got = window(
+        near_0, near_got, up_1, far_a, ctx_own, near, far_y, far_x, dense_own, dense_c, kv_own, kv_got
     )
 
-    far_b = send(near_w0[:, :, part:], ZFAR)
-    near_w1 = in_plane(stack_rows(up_1, raw_1))
+    far_b = send(near_0[part:], ZFAR)
+    near_own = in_plane(up_1)
     got_a = send(far_a, ZSWAP)
-    blocks = [dense_own, dense_c, near, far, near_c, send(far, CORE)]
+    blocks = [dense_own, dense_c, near, far_y, far_x]
+    blocks += [send(block, CORE) for block in blocks[2:]]
     hidden_out, normed = dense_norm(pos, hidden_in, ctx_own, blocks)
     from_y = send(normed, YSWAP)
     from_x = send(normed, XSWAP)
-    near_w0, near_w1, far_a, far_b, got_a, normed, from_y, from_x, kv_own, kv_other = window(
-        near_w0, near_w1, far_a, far_b, got_a, normed, from_y, from_x, kv_own, kv_other
+    near_0, near_own, near_got, far_a, far_b, got_a, normed, from_y, from_x, kv_own, kv_got = window(
+        near_0, near_own, near_got, far_a, far_b, got_a, normed, from_y, from_x, kv_own, kv_got
     )
 
     got_b = send(far_b, ZSWAP)
     cross_low = send(from_y[: share // 2], XSWAP)
     cross_high = send(from_x[share // 2 :], YSWAP)
-    kv_got = send(window(kv_other, cross_high)[0], YSWAP)
     other = [from_y, cross_low, cross_high]
     other += [send(piece, CORE) for piece in other]
     own = [normed, from_x, send(normed, CORE), send(from_x, CORE)]
-    near_w0, near_w1, far_a, far_b, got_a, *tokens = window(near_w0, near_w1, far_a, far_b, got_a, *other, *own)
+    *tokens, near_0, far_a, far_b = window(*other, *own, near_0, far_a, far_b)
     other, own = tokens[:6], tokens[6:]
-    weights = [(near_w0, (far_a, far_b)), (near_w1, (got_a, got_b))]
+    weights = [((near_0,), (far_a, far_b)), ((near_own, near_got), (got_a, got_b))]
     parts = []
     done = pos
     for half, side, pieces in ((0, 1, other), (1, 1, other), (0, 0, own), (1, 0, own)):

time: 193 us -> 183 us (0.948)
  blocking collectives: 46.2 us -> 13.6 us
  waiting for transfers between devices: 40.7 us -> 68.3 us
  Pallas kernels: 52.7 us -> 47.5 us
  starting transfers between devices: 40.9 us -> 43.5 us
  local copies, waits for them, and re-layouts: 9.75 us -> 7.15 us
    all_to_all x2 -> x1, blocking collectives: 46.2 us -> 13.6 us  [in_plane(): lax.all_to_all(pieces, AXES, split_axis=0, concat_axis=0, tiled=True, axi...]
    all_to_all x1 -> x2, waiting for transfers between devices: 0.01 us -> 20.3 us  [in_plane(): lax.all_to_all(pieces, AXES, split_axis=0, concat_axis=0, tiled=True, axi...]
    ppermute x30 -> x36, waiting for transfers between devices: 40.7 us -> 47.9 us  [send(): return lax.ppermute(value, AXES, moves)]
    pallas_call x4, Pallas kernels: 17.9 us -> 14.1 us  [up_part(): pl.pallas_call(functools.partial(up_kernel, len(pieces), half), in_specs=...]
    all_to_all x1 -> x2, starting transfers between devices: 3.74 us -> 7.26 us  [in_plane(): lax.all_to_all(pieces, AXES, split_axis=0, concat_axis=0, tiled=True, axi...]
    pallas_call x2 -> x1, Pallas kernels: 4.63 us -> 2.24 us  [stack_rows(): pl.pallas_call(stack_kernel, in_specs=[VMEM, VMEM], out_specs=VMEM, out_s...]
    unnamed x54 -> x32, local copies, waits for them, and re-layouts: 4.83 us -> 2.55 us
    pallas_call x2, Pallas kernels: 12 us -> 14.1 us  [one_head(): pl.pallas_call(functools.partial(head_kernel, bool(before)), in_specs=[SM...]
  transfers between devices with their start and end apart: 32 -> 39, of which waited for: 10 -> 13; matrix products, arithmetic and copies ran while one was open for 3% -> 3% of each run, Pallas kernels for 25% -> 24%
where the time goes in v4:
time: 183 us; the launch traced here: 182 us
  waiting for transfers between devices  68.3 us (37%)
  Pallas kernels  47.5 us (26%)
  starting transfers between devices  43.5 us (24%)
  blocking collectives  13.6 us (7%)
  local copies, waits for them, and re-layouts  7.15 us (4%)
    ppermute x36, waiting for transfers between devices, send(): return lax.ppermute(value, AXES, moves)  47.9 us
    ppermute x36, starting transfers between devices, send(): return lax.ppermute(value, AXES, moves)  28.8 us
    all_to_all x2, waiting for transfers between devices, in_plane(): lax.all_to_all(pieces, AXES, split_axis=0, concat_axis=0, tiled=True, axi...  20.3 us
    pallas_call x4, Pallas kernels, up_part(): pl.pallas_call(functools.partial(up_kernel, len(pieces), half), in_specs=...  14.1 us
    pallas_call x2, Pallas kernels, one_head(): pl.pallas_call(functools.partial(head_kernel, bool(before)), in_specs=[SM...  14.1 us
    all_to_all x1, blocking collectives, in_plane(): lax.all_to_all(pieces, AXES, split_axis=0, concat_axis=0, tiled=True, axi...  13.6 us
    all_to_all x1, starting transfers between devices, to_all(): mine = lax.all_to_all(pieces, AXES, split_axis=0, concat_axis=0, tiled=True)  7.41 us
    all_to_all x2, starting transfers between devices, in_plane(): lax.all_to_all(pieces, AXES, split_axis=0, concat_axis=0, tiled=True, axi...  7.26 us
  transfers between devices with their start and end apart: 39, of which 13 were waited for; matrix products, arithmetic and copies ran while one was open for 3% of the time, Pallas kernels for 24%

profile of v4, /device:TPU:0, one launch (start us, length us, event | category | flops | bytes accessed | tf_op | source)
XLA Modules:
  0.0 182.2 jit_solution(15272402906754782823)
XLA Ops:
  0.6 2.7 %shard_map.85 = bf16[32,64,384]{2,1,0:T(8,128)(2,1)} custom-call(f32[64,6144]{1,0:T(8,128)} %src.2), custom_call_target="tpu_custom_call" | custom-call | tf_op jit(solution)/shard_map/pallas_call | solution.py:129
  3.3 7.4 %all-to-all-start = ((bf16[32,64,384]{2,1,0:T(8,128)(2,1)}), bf16[32,64,384]{2,1,0:T(8,128)(2,1)}, u32[]{:S(2)}, u32[]{:S(2)}) async-start(bf16[32,64,384]{2,1,0:T(8,128)(2,1)} %shard_map.85), calls=%async_computation | async-start | bytes 3145728 | tf_op jit(solution)/shard_map/all_to_all | solution.py:192
  10.8 2.2 %shard_map.87.refs_0_ = bf16[96,2048]{1,0:T(8,128)(2,1)} custom-call(bf16[96,2048]{1,0:T(8,128)(2,1)} %hidden.3), custom_call_target="tpu_custom_call" | custom-call | tf_op jit(solution)/shard_map/pallas_call | solution.py:182
  16.7 2.7 %shard_map.86 = (bf16[8,64,512]{2,1,0:T(8,128)(2,1)}, bf16[8,64,512]{2,1,0:T(8,128)(2,1)}) custom-call(s32[3]{0:T(128)} %pad_add_fusion.1.pos, f32[64,8192]{1,0:T(8,128)} %src.3), custom_call_target="tpu_custom_call" | custom-call | tf_op jit(solution)/shard_map/pallas_call | solution.py:151
  22.5 13.5 %collective-permute-done.2.refs_1_ = bf16[96,2048]{1,0:T(8,128)(2,1)S(1)} collective-permute-done((bf16[96,2048]{1,0:T(8,128)(2,1)}, bf16[96,2048]{1,0:T(8,128)(2,1)S(1)}, u32[]{:S(2)}, u32[]{:S(2)}) %collective-permute-start.2) | collective-permute-done | bytes 393248 | tf_op jit(solution)/shard_map/ppermute | solution.py:100
  37.6 2.0 %collective-permute-start.4 = (bf16[48,2048]{1,0:T(8,128)(2,1)S(1)}, bf16[48,2048]{1,0:T(8,128)(2,1)S(1)}, u32[]{:S(2)}, u32[]{:S(2)}) collective-permute-start(bf16[48,2048]{1,0:T(8,128)(2,1)S(1)} %slice.32), channel_id=1, source_target_pairs={{0,2},{1,3},{2,0},{3,1},{4,6},{5,7},{6,4},{7,5},{8,10},{9,11},{10,... | collective-permute-start | bytes 589832 | tf_op jit(solution)/shard_map/ppermute | solution.py:100
  40.9 9.2 %collective-permute-done.got = bf16[8,64,512]{2,1,0:T(8,128)(2,1)} collective-permute-done((bf16[8,64,512]{2,1,0:T(8,128)(2,1)}, bf16[8,64,512]{2,1,0:T(8,128)(2,1)}, u32[]{:S(2)}, u32[]{:S(2)}) %collective-permute-start) | collective-permute-done | bytes 524320 | tf_op jit(solution)/shard_map/ppermute | solution.py:100
  53.1 2.2 %shard_map.88 = bf16[8,128,512]{2,1,0:T(8,128)(2,1)} custom-call(bf16[8,64,512]{2,1,0:T(8,128)(2,1)} %get-tuple-element.95.own, bf16[8,64,512]{2,1,0:T(8,128)(2,1)} %collective-permute-done.got), custom_call_target="tpu_custom_call" | custom-call | tf_op jit(solution)/shard_map/pallas_call | solution.py:168
  55.4 3.6 %all-to-all-start.1 = ((bf16[8,128,512]{2,1,0:T(8,128)(2,1)}), bf16[8,128,512]{2,1,0:T(8,128)(2,1)S(1)}, u32[]{:S(2)}, u32[]{:S(2)}) async-start(bf16[8,128,512]{2,1,0:T(8,128)(2,1)} %shard_map.88), calls=%async_computation.1 | async-start | bytes 2097152 | tf_op jit(solution)/shard_map/all_to_all | solution.py:197
  62.0 6.8 %shard_map.89 = (bf16[768,256]{1,0:T(8,128)(2,1)}, bf16[3,2,2,128,128]{4,3,2,1,0:T(8,128)(2,1)}, bf16[3,2,2,128,128]{4,3,2,1,0:T(8,128)(2,1)}) custom-call(s32[3]{0:T(128)} %pad_add_fusion.1.pos, f32[2]{0:T(128)} %multiply_exponential_fusion.slope, s32[2,1,384]{2,1,0:T(1,128)} %broadcast_in_dim.3.seg_rows, bf16[96,2048]{1,0:T(8,128)(2,1)} %shard_map.87.refs_0_, ...), custom_call_target="tpu_custom_call" | custom-call | tf_op jit(solution)/shard_map/pallas_call | solution.py:257
  68.9 20.3 %all-to-all-done.1.refs_6_.refs_4_ = bf16[8,128,512]{2,1,0:T(8,128)(2,1)S(1)} async-done(((bf16[8,128,512]{2,1,0:T(8,128)(2,1)}), bf16[8,128,512]{2,1,0:T(8,128)(2,1)S(1)}, u32[]{:S(2)}, u32[]{:S(2)}) %all-to-all-start.1) | async-done | bytes 1048608 | tf_op jit(solution)/shard_map/all_to_all | solution.py:197
  90.8 2.5 %collective-permute-start.15 = (bf16[4,128,512]{2,1,0:T(8,128)(2,1)S(1)}, bf16[4,128,512]{2,1,0:T(8,128)(2,1)S(1)}, u32[]{:S(2)}, u32[]{:S(2)}) collective-permute-start(bf16[4,128,512]{2,1,0:T(8,128)(2,1)S(1)} %slice.27), channel_id=1, source_target_pairs={{0,16},{1,17},{2,18},{3,19},{4,20},{5,21},{6,22},{7,23},{8,24},{9,... | collective-permute-start | bytes 1572872 | tf_op jit(solution)/shard_map/ppermute | solution.py:100
  96.5 7.3 %shard_map.90 = (bf16[768,256]{1,0:T(8,128)(2,1)}, bf16[3,2,2,128,128]{4,3,2,1,0:T(8,128)(2,1)}, bf16[3,2,2,128,128]{4,3,2,1,0:T(8,128)(2,1)}) custom-call(s32[3]{0:T(128)} %pad_add_fusion.1.pos, f32[2]{0:T(128)} %multiply_exponential_fusion.slope, s32[2,1,384]{2,1,0:T(1,128)} %broadcast_in_dim.3.seg_rows, bf16[96,2048]{1,0:T(8,128)(2,1)} %shard_map.87.refs_0_, ...), custom_call_target="tpu_custom_call" | custom-call | tf_op jit(solution)/shard_map/pallas_call | solution.py:257
  104.3 13.6 %all_to_all.20.ctx = bf16[8,96,256]{2,1,0:T(8,128)(2,1)} all-to-all(bf16[8,96,256]{2,1,0:T(8,128)(2,1)} %bitcast.5), channel_id=1, replica_groups={{0,1,2,3,4,5,6,7},{8,9,10,11,12,13,14,15},{16,17,18,19,20,21,22,23},{24..., dimensions={0} | all-to-all | bytes 786432 | tf_op jit(solution)/shard_map/all_to_all | solution.py:197
  122.2 3.7 %all-to-all-start.3 = ((bf16[8,64,512]{2,1,0:T(8,128)(2,1)}), bf16[8,64,512]{2,1,0:T(8,128)(2,1)S(1)}, u32[]{:S(2)}, u32[]{:S(2)}) async-start(bf16[8,64,512]{2,1,0:T(8,128)(2,1)} %get-tuple-element.145), calls=%async_computation.3 | async-start | bytes 1048576 | tf_op jit(solution)/shard_map/all_to_all | solution.py:197
  125.9 6.2 %shard_map.91 = (bf16[96,2048]{1,0:T(8,128)(2,1)}, bf16[96,2048]{1,0:T(8,128)(2,1)}) custom-call(s32[3]{0:T(128)} %pad_add_fusion.1.pos, bf16[96,2048]{1,0:T(8,128)(2,1)} %hidden.3, bf16[8,96,256]{2,1,0:T(8,128)(2,1)} %all_to_all.20.ctx, bf16[512,2048]{1,0:T(8,128)(2,1)} %own, bf16[512,2048]{1,0:T(8,128)(2,1)} %collective-permute-done.11.cross, ...), custom_call_target="tpu_custom_call" | custom-call | tf_op jit(solution)/shard_map/pallas_call | solution.py:302
  132.2 2.1 %collective-permute-start.24 = (bf16[96,2048]{1,0:T(8,128)(2,1)}, bf16[96,2048]{1,0:T(8,128)(2,1)S(1)}, u32[]{:S(2)}, u32[]{:S(2)}) collective-permute-start(bf16[96,2048]{1,0:T(8,128)(2,1)} %get-tuple-element.176.refs_0_), channel_id=1, source_target_pairs={{0,4},{1,5},{2,6},{3,7},{4,0},{5,1},{6,2},{7,3},{8,12},{9,13},{10,... | collective-permute-start | bytes 1179656 | tf_op jit(solution)/shard_map/ppermute | solution.py:100
  135.7 11.2 %collective-permute-done.22.refs_8_.refs_6_ = bf16[4,128,512]{2,1,0:T(8,128)(2,1)} collective-permute-done((bf16[4,128,512]{2,1,0:T(8,128)(2,1)}, bf16[4,128,512]{2,1,0:T(8,128)(2,1)}, u32[]{:S(2)}, u32[]{:S(2)}) %collective-permute-start.22) | collective-permute-done | bytes 524320 | tf_op jit(solution)/shard_map/ppermute | solution.py:100
  150.1 3.4 %collective-permute-done.26.refs_1_ = bf16[48,2048]{1,0:T(8,128)(2,1)S(1)} collective-permute-done((bf16[48,2048]{1,0:T(8,128)(2,1)S(1)}, bf16[48,2048]{1,0:T(8,128)(2,1)S(1)}, u32[]{:S(2)}, u32[]{:S(2)}) %collective-permute-start.26) | collective-permute-done | bytes 196640 | tf_op jit(solution)/shard_map/ppermute | solution.py:100
  156.8 3.9 %shard_map.92 = bf16[384,512]{1,0:T(8,128)(2,1)S(1)} custom-call(s32[3]{0:T(128)S(1)} %copy-done.4, bf16[96,2048]{1,0:T(8,128)(2,1)S(1)} %collective-permute-done.24.refs_0_, bf16[48,2048]{1,0:T(8,128)(2,1)S(1)} %collective-permute-done.26.refs_1_, bf16[48,2048]{1,0:T(8,128)(2,1)S(1)} %collective-permute-done.27.refs_2_, ...), custom_call_target="tpu_custom_call" | custom-call | tf_op jit(solution)/shard_map/pallas_call | solution.py:353
  163.2 3.8 %shard_map.93 = bf16[384,512]{1,0:T(8,128)(2,1)S(1)} custom-call(s32[3]{0:T(128)S(1)} %copy-done.4, bf16[96,2048]{1,0:T(8,128)(2,1)S(1)} %collective-permute-done.24.refs_0_, bf16[48,2048]{1,0:T(8,128)(2,1)S(1)} %collective-permute-done.26.refs_1_, bf16[48,2048]{1,0:T(8,128)(2,1)S(1)} %collective-permute-done.27.refs_2_, ...), custom_call_target="tpu_custom_call" | custom-call | tf_op jit(solution)/shard_map/pallas_call | solution.py:353
  169.2 3.2 %shard_map.94.refs_2_ = bf16[384,512]{1,0:T(8,128)(2,1)S(1)} custom-call(s32[3]{0:T(128)S(1)} %copy-done.4, bf16[96,2048]{1,0:T(8,128)(2,1)S(1)} %copy-done, bf16[96,2048]{1,0:T(8,128)(2,1)S(1)} %collective-permute-done.25.refs_1_, bf16[96,2048]{1,0:T(8,128)(2,1)S(1)} %collective-permute-done.31.refs_2_, ...), custom_call_target="tpu_custom_call" | custom-call | tf_op jit(solution)/shard_map/pallas_call | solution.py:353
  172.4 3.2 %shard_map.95.refs_3_ = bf16[384,512]{1,0:T(8,128)(2,1)S(1)} custom-call(s32[3]{0:T(128)S(1)} %copy-done.4, bf16[96,2048]{1,0:T(8,128)(2,1)S(1)} %copy-done, bf16[96,2048]{1,0:T(8,128)(2,1)S(1)} %collective-permute-done.25.refs_1_, bf16[96,2048]{1,0:T(8,128)(2,1)S(1)} %collective-permute-done.31.refs_2_, ...), custom_call_target="tpu_custom_call" | custom-call | tf_op jit(solution)/shard_map/pallas_call | solution.py:353
  175.6 4.8 %collective-permute-done.35.refs_1_ = bf16[384,512]{1,0:T(8,128)(2,1)S(1)} collective-permute-done((bf16[384,512]{1,0:T(8,128)(2,1)S(1)}, bf16[384,512]{1,0:T(8,128)(2,1)S(1)}, u32[]{:S(2)}, u32[]{:S(2)}) %collective-permute-start.35) | collective-permute-done | bytes 393248 | tf_op jit(solution)/shard_map/ppermute | solution.py:100
  (114 shorter events, 39.7 us)
Async XLA Ops:
  3.3 47.5 %all-to-all-start = ((bf16[32,64,384]{2,1,0:T(8,128)(2,1)}), bf16[32,64,384]{2,1,0:T(8,128)(2,1)}, u32[]{:S(2)}, u32[]{:S(2)}) async-start(bf16[32,64,384]{2,1,0:T(8,128)(2,1)} %shard_map.85), calls=%async_computation | async-start | bytes 3145728 | tf_op jit(solution)/shard_map/all_to_all | solution.py:192
  13.0 23.0 %collective-permute-start.2 = (bf16[96,2048]{1,0:T(8,128)(2,1)}, bf16[96,2048]{1,0:T(8,128)(2,1)S(1)}, u32[]{:S(2)}, u32[]{:S(2)}) collective-permute-start(bf16[96,2048]{1,0:T(8,128)(2,1)} %shard_map.87.refs_0_), channel_id=1, source_target_pairs={{0,4},{1,5},{2,6},{3,7},{4,0},{5,1},{6,2},{7,3},{8,12},{9,13},{10,... | collective-permute-start | bytes 1179656 | tf_op jit(solution)/shard_map/ppermute | solution.py:100
  14.7 22.0 %collective-permute-start.3 = (bf16[96,2048]{1,0:T(8,128)(2,1)}, bf16[96,2048]{1,0:T(8,128)(2,1)S(1)}, u32[]{:S(2)}, u32[]{:S(2)}) collective-permute-start(bf16[96,2048]{1,0:T(8,128)(2,1)} %shard_map.87.refs_0_), channel_id=1, source_target_pairs={{0,2},{1,3},{2,0},{3,1},{4,6},{5,7},{6,4},{7,5},{8,10},{9,11},{10,... | collective-permute-start | bytes 1179656 | tf_op jit(solution)/shard_map/ppermute | solution.py:100
  16.1 23.5 %collective-permute-start.6 = (bf16[96,2048]{1,0:T(8,128)(2,1)}, bf16[96,2048]{1,0:T(8,128)(2,1)S(1)}, u32[]{:S(2)}, u32[]{:S(2)}) collective-permute-start(bf16[96,2048]{1,0:T(8,128)(2,1)} %shard_map.87.refs_0_), channel_id=1, source_target_pairs={{0,1},{1,0},{2,3},{3,2},{4,5},{5,4},{6,7},{7,6},{8,9},{9,8},{10,11... | collective-permute-start | bytes 1179656 | tf_op jit(solution)/shard_map/ppermute | solution.py:100
  19.4 30.7 %collective-permute-start = (bf16[8,64,512]{2,1,0:T(8,128)(2,1)}, bf16[8,64,512]{2,1,0:T(8,128)(2,1)}, u32[]{:S(2)}, u32[]{:S(2)}) collective-permute-start(bf16[8,64,512]{2,1,0:T(8,128)(2,1)} %get-tuple-element.145), channel_id=1, source_target_pairs={{0,8},{1,9},{2,10},{3,11},{4,12},{5,13},{6,14},{7,15},{8,0},{9,1},... | collective-permute-start | bytes 1572872 | tf_op jit(solution)/shard_map/ppermute | solution.py:100
  20.9 16.8 %collective-permute-start.1 = (s32[1,384]{1,0:T(1,128)S(1)}, s32[1,384]{1,0:T(1,128)S(1)}, u32[]{:S(2)}, u32[]{:S(2)}) collective-permute-start(s32[1,384]{1,0:T(1,128)S(1)} %copy-done.15), channel_id=1, source_target_pairs={{0,4},{1,5},{2,6},{3,7},{4,0},{5,1},{6,2},{7,3},{8,12},{9,13},{10,... | collective-permute-start | bytes 4616 | tf_op jit(solution)/shard_map/ppermute | solution.py:100
  35.9 14.2 %collective-permute-start.7 = (bf16[96,2048]{1,0:T(8,128)(2,1)S(1)}, bf16[96,2048]{1,0:T(8,128)(2,1)}, u32[]{:S(2)}, u32[]{:S(2)}) collective-permute-start(bf16[96,2048]{1,0:T(8,128)(2,1)S(1)} %collective-permute-done.2.refs_1_), channel_id=1, source_target_pairs={{0,1},{1,0},{2,3},{3,2},{4,5},{5,4},{6,7},{7,6},{8,9},{9,8},{10,11... | collective-permute-start | bytes 1179656 | tf_op jit(solution)/shard_map/ppermute | solution.py:100
  36.7 14.2 %collective-permute-start.8 = (bf16[96,2048]{1,0:T(8,128)(2,1)S(1)}, bf16[96,2048]{1,0:T(8,128)(2,1)}, u32[]{:S(2)}, u32[]{:S(2)}) collective-permute-start(bf16[96,2048]{1,0:T(8,128)(2,1)S(1)} %collective-permute-done.3.refs_2_), channel_id=1, source_target_pairs={{0,1},{1,0},{2,3},{3,2},{4,5},{5,4},{6,7},{7,6},{8,9},{9,8},{10,11... | collective-permute-start | bytes 1179656 | tf_op jit(solution)/shard_map/ppermute | solution.py:100
  50.9 38.3 %collective-permute-start.11 = (bf16[512,2048]{1,0:T(8,128)(2,1)S(1)}, bf16[512,2048]{1,0:T(8,128)(2,1)}, u32[]{:S(2)}, u32[]{:S(2)}) collective-permute-start(bf16[512,2048]{1,0:T(8,128)(2,1)S(1)} %copy-done.6), channel_id=1, source_target_pairs={{0,1},{1,0},{2,3},{3,2},{4,5},{5,4},{6,7},{7,6},{8,9},{9,8},{10,11... | collective-permute-start | bytes 6291464 | tf_op jit(solution)/shard_map/ppermute | solution.py:100
  50.9 38.3 %collective-permute-start.9 = (bf16[2048,384]{1,0:T(8,128)(2,1)}, bf16[2048,384]{1,0:T(8,128)(2,1)}, u32[]{:S(2)}, u32[]{:S(2)}) collective-permute-start(bf16[2048,384]{1,0:T(8,128)(2,1)} %bitcast.refs_10_), channel_id=1, source_target_pairs={{0,8},{1,9},{2,10},{3,11},{4,12},{5,13},{6,14},{7,15},{8,0},{9,1},... | collective-permute-start | bytes 4718600 | tf_op jit(solution)/shard_map/ppermute | solution.py:100
  51.7 37.5 %collective-permute-start.10 = (bf16[256,2048]{1,0:T(8,128)(2,1)}, bf16[256,2048]{1,0:T(8,128)(2,1)}, u32[]{:S(2)}, u32[]{:S(2)}) collective-permute-start(bf16[256,2048]{1,0:T(8,128)(2,1)} %constant_dynamic-slice_fusion.1), channel_id=1, source_target_pairs={{0,2},{1,3},{2,0},{3,1},{4,6},{5,7},{6,4},{7,5},{8,10},{9,11},{10,... | collective-permute-start | bytes 3145736 | tf_op jit(solution)/shard_map/ppermute | solution.py:100
  55.4 33.8 %all-to-all-start.1 = ((bf16[8,128,512]{2,1,0:T(8,128)(2,1)}), bf16[8,128,512]{2,1,0:T(8,128)(2,1)S(1)}, u32[]{:S(2)}, u32[]{:S(2)}) async-start(bf16[8,128,512]{2,1,0:T(8,128)(2,1)} %shard_map.88), calls=%async_computation.1 | async-start | bytes 2097152 | tf_op jit(solution)/shard_map/all_to_all | solution.py:197
  89.3 29.4 %collective-permute-start.14 = (bf16[8,64,512]{2,1,0:T(8,128)(2,1)S(1)}, bf16[8,64,512]{2,1,0:T(8,128)(2,1)S(1)}, u32[]{:S(2)}, u32[]{:S(2)}) collective-permute-start(bf16[8,64,512]{2,1,0:T(8,128)(2,1)S(1)} %slice.26), channel_id=1, source_target_pairs={{0,8},{1,9},{2,10},{3,11},{4,12},{5,13},{6,14},{7,15},{8,0},{9,1},... | collective-permute-start | bytes 1572872 | tf_op jit(solution)/shard_map/ppermute | solution.py:100
  90.8 27.9 %collective-permute-start.15 = (bf16[4,128,512]{2,1,0:T(8,128)(2,1)S(1)}, bf16[4,128,512]{2,1,0:T(8,128)(2,1)S(1)}, u32[]{:S(2)}, u32[]{:S(2)}) collective-permute-start(bf16[4,128,512]{2,1,0:T(8,128)(2,1)S(1)} %slice.27), channel_id=1, source_target_pairs={{0,16},{1,17},{2,18},{3,19},{4,20},{5,21},{6,22},{7,23},{8,24},{9,... | collective-permute-start | bytes 1572872 | tf_op jit(solution)/shard_map/ppermute | solution.py:100
  94.4 24.3 %collective-permute-start.16 = (bf16[128,2048]{1,0:T(8,128)(2,1)S(1)}, bf16[128,2048]{1,0:T(8,128)(2,1)}, u32[]{:S(2)}, u32[]{:S(2)}) collective-permute-start(bf16[128,2048]{1,0:T(8,128)(2,1)S(1)} %slice.28), channel_id=1, source_target_pairs={{0,4},{1,5},{2,6},{3,7},{4,0},{5,1},{6,2},{7,3},{8,12},{9,13},{10,... | collective-permute-start | bytes 1572872 | tf_op jit(solution)/shard_map/ppermute | solution.py:100
  94.9 23.8 %collective-permute-start.17 = (bf16[128,2048]{1,0:T(8,128)(2,1)S(1)}, bf16[128,2048]{1,0:T(8,128)(2,1)}, u32[]{:S(2)}, u32[]{:S(2)}) collective-permute-start(bf16[128,2048]{1,0:T(8,128)(2,1)S(1)} %copy-done.14), channel_id=1, source_target_pairs={{0,2},{1,3},{2,0},{3,1},{4,6},{5,7},{6,4},{7,5},{8,10},{9,11},{10,... | collective-permute-start | bytes 1572872 | tf_op jit(solution)/shard_map/ppermute | solution.py:100
  103.7 14.2 %collective-permute-start.18 = (bf16[3,2,2,128,128]{4,3,2,1,0:T(8,128)(2,1)}, bf16[3,2,2,128,128]{4,3,2,1,0:T(8,128)(2,1)S(1)}, u32[]{:S(2)}, u32[]{:S(2)}) collective-permute-start(bf16[3,2,2,128,128]{4,3,2,1,0:T(8,128)(2,1)} %get-tuple-element.136), channel_id=1, source_target_pairs={{0,4},{1,5},{2,6},{3,7},{4,0},{5,1},{6,2},{7,3},{8,12},{9,13},{10,... | collective-permute-start | bytes 1179656 | tf_op jit(solution)/shard_map/ppermute | solution.py:100
  120.2 26.7 %collective-permute-start.22 = (bf16[4,128,512]{2,1,0:T(8,128)(2,1)}, bf16[4,128,512]{2,1,0:T(8,128)(2,1)}, u32[]{:S(2)}, u32[]{:S(2)}) collective-permute-start(bf16[4,128,512]{2,1,0:T(8,128)(2,1)} %slice.29), channel_id=1, source_target_pairs={{0,16},{1,17},{2,18},{3,19},{4,20},{5,21},{6,22},{7,23},{8,24},{9,... | collective-permute-start | bytes 1572872 | tf_op jit(solution)/shard_map/ppermute | solution.py:100
  121.2 25.8 %collective-permute-start.23 = (bf16[4,128,512]{2,1,0:T(8,128)(2,1)S(1)}, bf16[4,128,512]{2,1,0:T(8,128)(2,1)}, u32[]{:S(2)}, u32[]{:S(2)}) collective-permute-start(bf16[4,128,512]{2,1,0:T(8,128)(2,1)S(1)} %collective-permute-done.15.refs_7_.refs_5_), channel_id=1, source_target_pairs={{0,8},{1,9},{2,10},{3,11},{4,12},{5,13},{6,14},{7,15},{8,0},{9,1},... | collective-permute-start | bytes 1572872 | tf_op jit(solution)/shard_map/ppermute | solution.py:100
  122.2 13.5 %all-to-all-start.3 = ((bf16[8,64,512]{2,1,0:T(8,128)(2,1)}), bf16[8,64,512]{2,1,0:T(8,128)(2,1)S(1)}, u32[]{:S(2)}, u32[]{:S(2)}) async-start(bf16[8,64,512]{2,1,0:T(8,128)(2,1)} %get-tuple-element.145), calls=%async_computation.3 | async-start | bytes 1048576 | tf_op jit(solution)/shard_map/all_to_all | solution.py:197
  132.2 14.8 %collective-permute-start.24 = (bf16[96,2048]{1,0:T(8,128)(2,1)}, bf16[96,2048]{1,0:T(8,128)(2,1)S(1)}, u32[]{:S(2)}, u32[]{:S(2)}) collective-permute-start(bf16[96,2048]{1,0:T(8,128)(2,1)} %get-tuple-element.176.refs_0_), channel_id=1, source_target_pairs={{0,4},{1,5},{2,6},{3,7},{4,0},{5,1},{6,2},{7,3},{8,12},{9,13},{10,... | collective-permute-start | bytes 1179656 | tf_op jit(solution)/shard_map/ppermute | solution.py:100
  150.1 13.1 %collective-permute-start.34 = (bf16[4,128,512]{2,1,0:T(8,128)(2,1)}, bf16[4,128,512]{2,1,0:T(8,128)(2,1)S(1)}, u32[]{:S(2)}, u32[]{:S(2)}) collective-permute-start(bf16[4,128,512]{2,1,0:T(8,128)(2,1)} %collective-permute-done.22.refs_8_.refs_6_), channel_id=1, source_target_pairs={{0,8},{1,9},{2,10},{3,11},{4,12},{5,13},{6,14},{7,15},{8,0},{9,1},... | collective-permute-start | bytes 1572872 | tf_op jit(solution)/shard_map/ppermute | solution.py:100
  160.7 14.9 %collective-permute-start.33 = (bf16[384,512]{1,0:T(8,128)(2,1)S(1)}, bf16[384,512]{1,0:T(8,128)(2,1)S(1)}, u32[]{:S(2)}, u32[]{:S(2)}) collective-permute-start(bf16[384,512]{1,0:T(8,128)(2,1)S(1)} %shard_map.92), channel_id=1, source_target_pairs={{0,4},{1,5},{2,6},{3,7},{4,0},{5,1},{6,2},{7,3},{8,12},{9,13},{10,... | collective-permute-start | bytes 1179656 | tf_op jit(solution)/shard_map/ppermute | solution.py:100
  167.1 13.3 %collective-permute-start.35 = (bf16[384,512]{1,0:T(8,128)(2,1)S(1)}, bf16[384,512]{1,0:T(8,128)(2,1)S(1)}, u32[]{:S(2)}, u32[]{:S(2)}) collective-permute-start(bf16[384,512]{1,0:T(8,128)(2,1)S(1)} %shard_map.93), channel_id=1, source_target_pairs={{0,4},{1,5},{2,6},{3,7},{4,0},{5,1},{6,2},{7,3},{8,12},{9,13},{10,... | collective-permute-start | bytes 1179656 | tf_op jit(solution)/shard_map/ppermute | solution.py:100
  (31 other events, 236.9 us)

commit v5 on v4

--- a/solution.py
+++ b/solution.py
@@ -135,26 +135,27 @@
     )(master)
 
 
-def cast_halves(pos, master):
+def cast_and_norm(pos, master, hidden):
     rows, cols = master.shape
     half = cols // PLANE // 2
 
-    def kernel(pos, src, *dst):
+    def kernel(pos, src, hidden, first, second, normed):
         parity = pos[0] % 2
         for p in range(PLANE):
             start = (2 * (p % NM) + p // NM) * 2 * half
-            for i in range(2):
-                first = pl.multiple_of(start + (parity ^ i) * half, half)
-                dst[i][p] = src[:, pl.ds(first, half)].astype(BF)
+            for i, dst in ((0, first), (1, second)):
+                column = pl.multiple_of(start + (parity ^ i) * half, half)
+                dst[p] = src[:, pl.ds(column, half)].astype(BF)
+        normed[...] = layer_norm(hidden[...].astype(F32)).astype(BF)
 
     shape = jax.ShapeDtypeStruct((PLANE, rows, half), BF)
     return pl.pallas_call(
         kernel,
-        in_specs=[SMEM, VMEM],
-        out_specs=[VMEM, VMEM],
-        out_shape=[shape, shape],
+        in_specs=[SMEM, VMEM, VMEM],
+        out_specs=[VMEM, VMEM, VMEM],
+        out_shape=[shape, shape, jax.ShapeDtypeStruct(hidden.shape, BF)],
         compiler_params=params(),
-    )(pos, master)
+    )(pos, master, hidden)
 
 
 def stack_kernel(own, got, out):
@@ -172,20 +173,6 @@
         out_shape=jax.ShapeDtypeStruct((count, 2 * rows, width), BF),
         compiler_params=params(),
     )(own, got)
-
-
-def norm_kernel(hidden, out):
-    out[...] = layer_norm(hidden[...].astype(F32)).astype(BF)
-
-
-def norm_rows(hidden):
-    return pl.pallas_call(
-        norm_kernel,
-        in_specs=[VMEM],
-        out_specs=VMEM,
-        out_shape=jax.ShapeDtypeStruct(hidden.shape, BF),
-        compiler_params=params(),
-    )(hidden)
 
 
 def to_all(pieces):
@@ -301,7 +288,7 @@
 def dense_norm(pos, hidden, ctx, blocks):
     return pl.pallas_call(
         dense_kernel,
-        in_specs=[SMEM, VMEM, VMEM] + [HBM] * len(blocks),
+        in_specs=[SMEM, VMEM, VMEM] + [HBM] * 2 + [ANY] * (len(blocks) - 2),
         out_specs=[VMEM, VMEM],
         out_shape=[jax.ShapeDtypeStruct(hidden.shape, BF)] * 2,
         scratch_shapes=[
@@ -365,26 +352,41 @@
     )(pos, *pieces, *nears, *fars)
 
 
-def join_kernel(places, pos, *refs):
-    *parts, out = refs
+def join_copies(places, pos, parts, out, sem):
     z, y, m = pos[0], pos[1], pos[2]
     share = out.shape[0] // NM
+    copies = []
     for part, (side, half, devices) in zip(parts, places):
         width = part.shape[1]
         columns = pl.ds(pl.multiple_of(((y ^ side) * 2 + (z % 2 ^ half)) * width, width), width)
         for i, r in enumerate(devices):
             rows = pl.ds(pl.multiple_of((m ^ r) * share, 16), share)
-            out[rows, columns] = part[i * share : (i + 1) * share]
-
-
-def join_parts(pos, shape, parts):
-    return pl.pallas_call(
-        functools.partial(join_kernel, [part[1:] for part in parts]),
-        in_specs=[SMEM] + [VMEM] * len(parts),
-        out_specs=VMEM,
+            src = part.at[i * share : (i + 1) * share]
+            copies.append(pltpu.make_async_copy(src, out.at[rows, columns], sem.at[len(copies)]))
+    return copies
+
+
+def join_kernel(places, pos, *refs):
+    *parts, out, sem = refs
+    copies = join_copies(places, pos, parts[-len(places) :], out, sem)
+    for copy in copies:
+        copy.start()
+    for copy in copies:
+        copy.wait()
+
+
+def join_parts(pos, shape, parts, before=None):
+    places = [part[1:] for part in parts]
+    started = [] if before is None else [before]
+    return pl.pallas_call(
+        functools.partial(join_kernel, places),
+        in_specs=[SMEM] + [HBM] * len(started) + [ANY] * len(parts),
+        out_specs=HBM,
         out_shape=jax.ShapeDtypeStruct(shape, BF),
+        scratch_shapes=[pltpu.SemaphoreType.DMA((sum(len(devices) for _, _, devices in places),))],
+        input_output_aliases={1: 0} if started else {},
         compiler_params=params(SMALL_LIMIT),
-    )(pos, *(part[0] for part in parts))
+    )(pos, *started, *(part[0] for part in parts))
 
 
 def pages_kernel(pos, table, own, got, out):
@@ -420,9 +422,8 @@
     slopes = jnp.exp2(-8.0 * (head + 1).astype(F32) / H)
 
     qkv_own = to_all(cast_pieces(qkv_master))
-    up_0, up_1 = cast_halves(pos, up_master)
+    up_0, up_1, normed = cast_and_norm(pos, up_master, hidden_in)
     raw_0 = send(up_1, ZSWAP)
-    normed = norm_rows(hidden_in)
     from_y = send(normed, YSWAP)
     from_x = send(normed, XSWAP)
     cross_low = send(from_y[: share // 2], XSWAP)
@@ -434,7 +435,6 @@
     seg_other = send(segment_ids, YSWAP)
     segments = jnp.concatenate([segment_ids, seg_other], 0)
     seg_rows = segments[:, None, :]
-    tokens += [send(piece, CORE) for piece in tokens[:3]]
     qkv_own, up_0, up_1, raw_0, give, give_far, seg_rows, slopes, pos, dense_own, *tokens = window(
         qkv_own, up_0, up_1, raw_0, give, give_far, seg_rows, slopes, pos, dense_weight, *tokens
     )
@@ -443,7 +443,7 @@
     near_0 = in_plane(stack_rows(up_0, raw_0))
     near = send(give, XSWAP)
     dense_c = send(dense_own, CORE)
-    tokens += [send(piece, CORE) for piece in tokens[3:5]]
+    tokens += [send(piece, CORE) for piece in tokens]
     before = one_head(pos, slopes, seg_rows, tokens, qkv_own)
     qkv_got, near_0, up_1, near, give_far, dense_own, dense_c, *state = window(
         qkv_got, near_0, up_1, near, give_far, dense_own, dense_c, *tokens, *before
@@ -489,7 +489,9 @@
         first, _ = window(pieces[0], done)
         done = up_part(pos, half, [first] + pieces[1:], *weights[half])
         parts.append((send(done, YSWAP) if side else done, side, half, (0, 2, 1, 3)))
-    activated = join_parts(pos, (NM * share, up_master.shape[1] // NM), parts)
+    shape = (NM * share, up_master.shape[1] // NM)
+    activated = join_parts(pos, shape, [parts[0]] + parts[2:])
+    activated = join_parts(pos, shape, parts[1:2], activated)
     cache = place_pages(pos, page_table, kv_own, kv_got)
     return hidden_out, activated, cache
 

time: 183 us -> 182 us (level)
    all_to_all x2, waiting for transfers between devices: 20.3 us -> 16.6 us  [in_plane(): lax.all_to_all(pieces, AXES, split_axis=0, concat_axis=0, tiled=True, axi...]
    ppermute x36, waiting for transfers between devices: 47.9 us -> 50.9 us  [send(): return lax.ppermute(value, AXES, moves)]
  transfers between devices with their start and end apart: 39 -> 39, of which waited for: 13 -> 14; matrix products, arithmetic and copies ran while one was open for 3% -> 3% of each run, Pallas kernels for 24% -> 24%
where the time goes in v5:
time: 182 us; the launch traced here: 181 us
  waiting for transfers between devices  67.5 us (37%)
  Pallas kernels  46.8 us (26%)
  starting transfers between devices  44.7 us (25%)
  blocking collectives  13.6 us (7%)
  local copies, waits for them, and re-layouts  6.28 us (3%)
    ppermute x36, waiting for transfers between devices, send(): return lax.ppermute(value, AXES, moves)  50.9 us
    ppermute x36, starting transfers between devices, send(): return lax.ppermute(value, AXES, moves)  30 us
    all_to_all x2, waiting for transfers between devices, in_plane(): lax.all_to_all(pieces, AXES, split_axis=0, concat_axis=0, tiled=True, axi...  16.6 us
    pallas_call x4, Pallas kernels, up_part(): pl.pallas_call(functools.partial(up_kernel, len(pieces), half), in_specs=...  14.1 us
    pallas_call x2, Pallas kernels, one_head(): pl.pallas_call(functools.partial(head_kernel, bool(before)), in_specs=[SM...  14.1 us
    all_to_all x1, blocking collectives, in_plane(): lax.all_to_all(pieces, AXES, split_axis=0, concat_axis=0, tiled=True, axi...  13.6 us
    all_to_all x1, starting transfers between devices, to_all(): mine = lax.all_to_all(pieces, AXES, split_axis=0, concat_axis=0, tiled=True)  7.41 us
    all_to_all x2, starting transfers between devices, in_plane(): lax.all_to_all(pieces, AXES, split_axis=0, concat_axis=0, tiled=True, axi...  7.26 us
  transfers between devices with their start and end apart: 39, of which 14 were waited for; matrix products, arithmetic and copies ran while one was open for 3% of the time, Pallas kernels for 24%

profile of v5, /device:TPU:0, one launch (start us, length us, event | category | flops | bytes accessed | tf_op | source)
XLA Modules:
  0.0 181.2 jit_solution(5385987144223022873)
XLA Ops:
  0.6 2.7 %shard_map.85 = bf16[32,64,384]{2,1,0:T(8,128)(2,1)} custom-call(f32[64,6144]{1,0:T(8,128)} %src.2), custom_call_target="tpu_custom_call" | custom-call | tf_op jit(solution)/shard_map/pallas_call | solution.py:129
  3.3 7.4 %all-to-all-start = ((bf16[32,64,384]{2,1,0:T(8,128)(2,1)}), bf16[32,64,384]{2,1,0:T(8,128)(2,1)}, u32[]{:S(2)}, u32[]{:S(2)}) async-start(bf16[32,64,384]{2,1,0:T(8,128)(2,1)} %shard_map.85), calls=%async_computation | async-start | bytes 3145728 | tf_op jit(solution)/shard_map/all_to_all | solution.py:179
  11.4 3.0 %shard_map.86 = (bf16[8,64,512]{2,1,0:T(8,128)(2,1)}, bf16[8,64,512]{2,1,0:T(8,128)(2,1)}, bf16[96,2048]{1,0:T(8,128)(2,1)}) custom-call(s32[3]{0:T(128)} %pad_add_fusion.1.pos, f32[64,8192]{1,0:T(8,128)} %src.3, bf16[96,2048]{1,0:T(8,128)(2,1)} %hidden.3), custom_call_target="tpu_custom_call" | custom-call | tf_op jit(solution)/shard_map/pallas_call | solution.py:152
  14.5 1.7 collective-permute-start.2
  21.6 14.3 %collective-permute-done.2.refs_1_ = bf16[96,2048]{1,0:T(8,128)(2,1)S(1)} collective-permute-done((bf16[96,2048]{1,0:T(8,128)(2,1)}, bf16[96,2048]{1,0:T(8,128)(2,1)S(1)}, u32[]{:S(2)}, u32[]{:S(2)}) %collective-permute-start.2) | collective-permute-done | bytes 393248 | tf_op jit(solution)/shard_map/ppermute | solution.py:100
  35.9 2.3 %collective-permute-start.4 = (bf16[48,2048]{1,0:T(8,128)(2,1)S(1)}, bf16[48,2048]{1,0:T(8,128)(2,1)S(1)}, u32[]{:S(2)}, u32[]{:S(2)}) collective-permute-start(bf16[48,2048]{1,0:T(8,128)(2,1)S(1)} %slice.32), channel_id=1, source_target_pairs={{0,2},{1,3},{2,0},{3,1},{4,6},{5,7},{6,4},{7,5},{8,10},{9,11},{10,... | collective-permute-start | bytes 589832 | tf_op jit(solution)/shard_map/ppermute | solution.py:100
  39.5 10.6 %collective-permute-done.got = bf16[8,64,512]{2,1,0:T(8,128)(2,1)} collective-permute-done((bf16[8,64,512]{2,1,0:T(8,128)(2,1)}, bf16[8,64,512]{2,1,0:T(8,128)(2,1)}, u32[]{:S(2)}, u32[]{:S(2)}) %collective-permute-start) | collective-permute-done | bytes 524320 | tf_op jit(solution)/shard_map/ppermute | solution.py:100
  52.5 2.2 %shard_map.87 = bf16[8,128,512]{2,1,0:T(8,128)(2,1)} custom-call(bf16[8,64,512]{2,1,0:T(8,128)(2,1)} %get-tuple-element.94.own, bf16[8,64,512]{2,1,0:T(8,128)(2,1)} %collective-permute-done.got), custom_call_target="tpu_custom_call" | custom-call | tf_op jit(solution)/shard_map/pallas_call | solution.py:169
  54.7 3.6 %all-to-all-start.1 = ((bf16[8,128,512]{2,1,0:T(8,128)(2,1)}), bf16[8,128,512]{2,1,0:T(8,128)(2,1)S(1)}, u32[]{:S(2)}, u32[]{:S(2)}) async-start(bf16[8,128,512]{2,1,0:T(8,128)(2,1)} %shard_map.87), calls=%async_computation.1 | async-start | bytes 2097152 | tf_op jit(solution)/shard_map/all_to_all | solution.py:184
  65.1 6.9 %shard_map.88 = (bf16[768,256]{1,0:T(8,128)(2,1)}, bf16[3,2,2,128,128]{4,3,2,1,0:T(8,128)(2,1)}, bf16[3,2,2,128,128]{4,3,2,1,0:T(8,128)(2,1)}) custom-call(s32[3]{0:T(128)} %pad_add_fusion.1.pos, f32[2]{0:T(128)} %multiply_exponential_fusion.slope, s32[2,1,384]{2,1,0:T(1,128)} %broadcast_in_dim.3.seg_rows, bf16[96,2048]{1,0:T(8,128)(2,1)} %get-tuple-element.112.refs_0_, ...), custom_call_target="tpu_custom_call" | custom-call | tf_op jit(solution)/shard_map/pallas_call | solution.py:244
  72.0 16.6 %all-to-all-done.1.refs_6_.refs_4_ = bf16[8,128,512]{2,1,0:T(8,128)(2,1)S(1)} async-done(((bf16[8,128,512]{2,1,0:T(8,128)(2,1)}), bf16[8,128,512]{2,1,0:T(8,128)(2,1)S(1)}, u32[]{:S(2)}, u32[]{:S(2)}) %all-to-all-start.1) | async-done | bytes 1048608 | tf_op jit(solution)/shard_map/all_to_all | solution.py:184
  90.2 2.5 %collective-permute-start.15 = (bf16[4,128,512]{2,1,0:T(8,128)(2,1)S(1)}, bf16[4,128,512]{2,1,0:T(8,128)(2,1)S(1)}, u32[]{:S(2)}, u32[]{:S(2)}) collective-permute-start(bf16[4,128,512]{2,1,0:T(8,128)(2,1)S(1)} %slice.27), channel_id=1, source_target_pairs={{0,16},{1,17},{2,18},{3,19},{4,20},{5,21},{6,22},{7,23},{8,24},{9,... | collective-permute-start | bytes 1572872 | tf_op jit(solution)/shard_map/ppermute | solution.py:100
  95.8 7.3 %shard_map.89 = (bf16[768,256]{1,0:T(8,128)(2,1)}, bf16[3,2,2,128,128]{4,3,2,1,0:T(8,128)(2,1)}, bf16[3,2,2,128,128]{4,3,2,1,0:T(8,128)(2,1)}) custom-call(s32[3]{0:T(128)} %pad_add_fusion.1.pos, f32[2]{0:T(128)} %multiply_exponential_fusion.slope, s32[2,1,384]{2,1,0:T(1,128)} %broadcast_in_dim.3.seg_rows, bf16[96,2048]{1,0:T(8,128)(2,1)} %get-tuple-element.112.refs_0_, ...), custom_call_target="tpu_custom_call" | custom-call | tf_op jit(solution)/shard_map/pallas_call | solution.py:244
  103.7 13.6 %all_to_all.20.ctx = bf16[8,96,256]{2,1,0:T(8,128)(2,1)} all-to-all(bf16[8,96,256]{2,1,0:T(8,128)(2,1)} %bitcast.5), channel_id=1, replica_groups={{0,1,2,3,4,5,6,7},{8,9,10,11,12,13,14,15},{16,17,18,19,20,21,22,23},{24..., dimensions={0} | all-to-all | bytes 786432 | tf_op jit(solution)/shard_map/all_to_all | solution.py:184
  121.6 3.7 %all-to-all-start.3 = ((bf16[8,64,512]{2,1,0:T(8,128)(2,1)}), bf16[8,64,512]{2,1,0:T(8,128)(2,1)S(1)}, u32[]{:S(2)}, u32[]{:S(2)}) async-start(bf16[8,64,512]{2,1,0:T(8,128)(2,1)} %get-tuple-element.141), calls=%async_computation.3 | async-start | bytes 1048576 | tf_op jit(solution)/shard_map/all_to_all | solution.py:184
  125.3 6.2 %shard_map.90 = (bf16[96,2048]{1,0:T(8,128)(2,1)}, bf16[96,2048]{1,0:T(8,128)(2,1)}) custom-call(s32[3]{0:T(128)} %pad_add_fusion.1.pos, bf16[96,2048]{1,0:T(8,128)(2,1)} %hidden.3, bf16[8,96,256]{2,1,0:T(8,128)(2,1)} %all_to_all.20.ctx, bf16[512,2048]{1,0:T(8,128)(2,1)} %own, bf16[512,2048]{1,0:T(8,128)(2,1)} %collective-permute-done.8.cross, ...), custom_call_target="tpu_custom_call" | custom-call | tf_op jit(solution)/shard_map/pallas_call | solution.py:289
  131.5 2.1 %collective-permute-start.24 = (bf16[96,2048]{1,0:T(8,128)(2,1)}, bf16[96,2048]{1,0:T(8,128)(2,1)S(1)}, u32[]{:S(2)}, u32[]{:S(2)}) collective-permute-start(bf16[96,2048]{1,0:T(8,128)(2,1)} %get-tuple-element.172.refs_0_), channel_id=1, source_target_pairs={{0,4},{1,5},{2,6},{3,7},{4,0},{5,1},{6,2},{7,3},{8,12},{9,13},{10,... | collective-permute-start | bytes 1179656 | tf_op jit(solution)/shard_map/ppermute | solution.py:100
  135.0 11.3 %collective-permute-done.22.refs_8_.refs_6_ = bf16[4,128,512]{2,1,0:T(8,128)(2,1)} collective-permute-done((bf16[4,128,512]{2,1,0:T(8,128)(2,1)}, bf16[4,128,512]{2,1,0:T(8,128)(2,1)}, u32[]{:S(2)}, u32[]{:S(2)}) %collective-permute-start.22) | collective-permute-done | bytes 524320 | tf_op jit(solution)/shard_map/ppermute | solution.py:100
  149.5 3.4 %collective-permute-done.26.refs_1_ = bf16[48,2048]{1,0:T(8,128)(2,1)S(1)} collective-permute-done((bf16[48,2048]{1,0:T(8,128)(2,1)S(1)}, bf16[48,2048]{1,0:T(8,128)(2,1)S(1)}, u32[]{:S(2)}, u32[]{:S(2)}) %collective-permute-start.26) | collective-permute-done | bytes 196640 | tf_op jit(solution)/shard_map/ppermute | solution.py:100
  156.2 3.9 %shard_map.91 = bf16[384,512]{1,0:T(8,128)(2,1)S(1)} custom-call(s32[3]{0:T(128)S(1)} %copy-done.4, bf16[96,2048]{1,0:T(8,128)(2,1)S(1)} %collective-permute-done.24.refs_0_, bf16[48,2048]{1,0:T(8,128)(2,1)S(1)} %collective-permute-done.26.refs_1_, bf16[48,2048]{1,0:T(8,128)(2,1)S(1)} %collective-permute-done.27.refs_2_, ...), custom_call_target="tpu_custom_call" | custom-call | tf_op jit(solution)/shard_map/pallas_call | solution.py:340
  162.6 3.8 %shard_map.92 = bf16[384,512]{1,0:T(8,128)(2,1)S(1)} custom-call(s32[3]{0:T(128)S(1)} %copy-done.4, bf16[96,2048]{1,0:T(8,128)(2,1)S(1)} %collective-permute-done.24.refs_0_, bf16[48,2048]{1,0:T(8,128)(2,1)S(1)} %collective-permute-done.26.refs_1_, bf16[48,2048]{1,0:T(8,128)(2,1)S(1)} %collective-permute-done.27.refs_2_, ...), custom_call_target="tpu_custom_call" | custom-call | tf_op jit(solution)/shard_map/pallas_call | solution.py:340
  168.6 3.2 %shard_map.93.refs_1_ = bf16[384,512]{1,0:T(8,128)(2,1)S(1)} custom-call(s32[3]{0:T(128)S(1)} %copy-done.4, bf16[96,2048]{1,0:T(8,128)(2,1)S(1)} %copy-done, bf16[96,2048]{1,0:T(8,128)(2,1)S(1)} %collective-permute-done.25.refs_1_, bf16[96,2048]{1,0:T(8,128)(2,1)S(1)} %collective-permute-done.31.refs_2_, ...), custom_call_target="tpu_custom_call" | custom-call | tf_op jit(solution)/shard_map/pallas_call | solution.py:340
  171.8 3.2 %shard_map.94.refs_2_ = bf16[384,512]{1,0:T(8,128)(2,1)S(1)} custom-call(s32[3]{0:T(128)S(1)} %copy-done.4, bf16[96,2048]{1,0:T(8,128)(2,1)S(1)} %copy-done, bf16[96,2048]{1,0:T(8,128)(2,1)S(1)} %collective-permute-done.25.refs_1_, bf16[96,2048]{1,0:T(8,128)(2,1)S(1)} %collective-permute-done.31.refs_2_, ...), custom_call_target="tpu_custom_call" | custom-call | tf_op jit(solution)/shard_map/pallas_call | solution.py:340
  176.7 3.1 %collective-permute-done.35.refs_1_ = bf16[384,512]{1,0:T(8,128)(2,1)S(1)} collective-permute-done((bf16[384,512]{1,0:T(8,128)(2,1)S(1)}, bf16[384,512]{1,0:T(8,128)(2,1)S(1)}, u32[]{:S(2)}, u32[]{:S(2)}) %collective-permute-start.35) | collective-permute-done | bytes 393248 | tf_op jit(solution)/shard_map/ppermute | solution.py:100
  (118 shorter events, 41.5 us)
Async XLA Ops:
  3.3 46.8 %all-to-all-start = ((bf16[32,64,384]{2,1,0:T(8,128)(2,1)}), bf16[32,64,384]{2,1,0:T(8,128)(2,1)}, u32[]{:S(2)}, u32[]{:S(2)}) async-start(bf16[32,64,384]{2,1,0:T(8,128)(2,1)} %shard_map.85), calls=%async_computation | async-start | bytes 3145728 | tf_op jit(solution)/shard_map/all_to_all | solution.py:179
  14.5 21.4 %collective-permute-start.2 = (bf16[96,2048]{1,0:T(8,128)(2,1)}, bf16[96,2048]{1,0:T(8,128)(2,1)S(1)}, u32[]{:S(2)}, u32[]{:S(2)}) collective-permute-start(bf16[96,2048]{1,0:T(8,128)(2,1)} %get-tuple-element.112.refs_0_), channel_id=1, source_target_pairs={{0,4},{1,5},{2,6},{3,7},{4,0},{5,1},{6,2},{7,3},{8,12},{9,13},{10,... | collective-permute-start | bytes 1179656 | tf_op jit(solution)/shard_map/ppermute | solution.py:100
  16.2 22.0 %collective-permute-start.3 = (bf16[96,2048]{1,0:T(8,128)(2,1)}, bf16[96,2048]{1,0:T(8,128)(2,1)S(1)}, u32[]{:S(2)}, u32[]{:S(2)}) collective-permute-start(bf16[96,2048]{1,0:T(8,128)(2,1)} %get-tuple-element.112.refs_0_), channel_id=1, source_target_pairs={{0,2},{1,3},{2,0},{3,1},{4,6},{5,7},{6,4},{7,5},{8,10},{9,11},{10,... | collective-permute-start | bytes 1179656 | tf_op jit(solution)/shard_map/ppermute | solution.py:100
  17.6 32.5 %collective-permute-start = (bf16[8,64,512]{2,1,0:T(8,128)(2,1)}, bf16[8,64,512]{2,1,0:T(8,128)(2,1)}, u32[]{:S(2)}, u32[]{:S(2)}) collective-permute-start(bf16[8,64,512]{2,1,0:T(8,128)(2,1)} %get-tuple-element.141), channel_id=1, source_target_pairs={{0,8},{1,9},{2,10},{3,11},{4,12},{5,13},{6,14},{7,15},{8,0},{9,1},... | collective-permute-start | bytes 1572872 | tf_op jit(solution)/shard_map/ppermute | solution.py:100
  19.1 19.8 %collective-permute-start.1 = (s32[1,384]{1,0:T(1,128)S(1)}, s32[1,384]{1,0:T(1,128)S(1)}, u32[]{:S(2)}, u32[]{:S(2)}) collective-permute-start(s32[1,384]{1,0:T(1,128)S(1)} %copy-done.17), channel_id=1, source_target_pairs={{0,4},{1,5},{2,6},{3,7},{4,0},{5,1},{6,2},{7,3},{8,12},{9,13},{10,... | collective-permute-start | bytes 4616 | tf_op jit(solution)/shard_map/ppermute | solution.py:100
  35.9 14.2 %collective-permute-start.4 = (bf16[48,2048]{1,0:T(8,128)(2,1)S(1)}, bf16[48,2048]{1,0:T(8,128)(2,1)S(1)}, u32[]{:S(2)}, u32[]{:S(2)}) collective-permute-start(bf16[48,2048]{1,0:T(8,128)(2,1)S(1)} %slice.32), channel_id=1, source_target_pairs={{0,2},{1,3},{2,0},{3,1},{4,6},{5,7},{6,4},{7,5},{8,10},{9,11},{10,... | collective-permute-start | bytes 589832 | tf_op jit(solution)/shard_map/ppermute | solution.py:100
  38.2 11.9 %collective-permute-start.5 = (bf16[48,2048]{1,0:T(8,128)(2,1)S(1)}, bf16[48,2048]{1,0:T(8,128)(2,1)S(1)}, u32[]{:S(2)}, u32[]{:S(2)}) collective-permute-start(bf16[48,2048]{1,0:T(8,128)(2,1)S(1)} %slice.33), channel_id=1, source_target_pairs={{0,4},{1,5},{2,6},{3,7},{4,0},{5,1},{6,2},{7,3},{8,12},{9,13},{10,... | collective-permute-start | bytes 589832 | tf_op jit(solution)/shard_map/ppermute | solution.py:100
  50.1 38.4 %collective-permute-start.8 = (bf16[512,2048]{1,0:T(8,128)(2,1)S(1)}, bf16[512,2048]{1,0:T(8,128)(2,1)}, u32[]{:S(2)}, u32[]{:S(2)}) collective-permute-start(bf16[512,2048]{1,0:T(8,128)(2,1)S(1)} %copy-done.6), channel_id=1, source_target_pairs={{0,1},{1,0},{2,3},{3,2},{4,5},{5,4},{6,7},{7,6},{8,9},{9,8},{10,11... | collective-permute-start | bytes 6291464 | tf_op jit(solution)/shard_map/ppermute | solution.py:100
  50.2 38.3 %collective-permute-start.6 = (bf16[2048,384]{1,0:T(8,128)(2,1)}, bf16[2048,384]{1,0:T(8,128)(2,1)}, u32[]{:S(2)}, u32[]{:S(2)}) collective-permute-start(bf16[2048,384]{1,0:T(8,128)(2,1)} %bitcast.refs_10_), channel_id=1, source_target_pairs={{0,8},{1,9},{2,10},{3,11},{4,12},{5,13},{6,14},{7,15},{8,0},{9,1},... | collective-permute-start | bytes 4718600 | tf_op jit(solution)/shard_map/ppermute | solution.py:100
  51.1 37.5 %collective-permute-start.7 = (bf16[256,2048]{1,0:T(8,128)(2,1)}, bf16[256,2048]{1,0:T(8,128)(2,1)}, u32[]{:S(2)}, u32[]{:S(2)}) collective-permute-start(bf16[256,2048]{1,0:T(8,128)(2,1)} %constant_dynamic-slice_fusion.1), channel_id=1, source_target_pairs={{0,2},{1,3},{2,0},{3,1},{4,6},{5,7},{6,4},{7,5},{8,10},{9,11},{10,... | collective-permute-start | bytes 3145736 | tf_op jit(solution)/shard_map/ppermute | solution.py:100
  54.7 33.8 %all-to-all-start.1 = ((bf16[8,128,512]{2,1,0:T(8,128)(2,1)}), bf16[8,128,512]{2,1,0:T(8,128)(2,1)S(1)}, u32[]{:S(2)}, u32[]{:S(2)}) async-start(bf16[8,128,512]{2,1,0:T(8,128)(2,1)} %shard_map.87), calls=%async_computation.1 | async-start | bytes 2097152 | tf_op jit(solution)/shard_map/all_to_all | solution.py:184
  88.7 29.4 %collective-permute-start.14 = (bf16[8,64,512]{2,1,0:T(8,128)(2,1)S(1)}, bf16[8,64,512]{2,1,0:T(8,128)(2,1)S(1)}, u32[]{:S(2)}, u32[]{:S(2)}) collective-permute-start(bf16[8,64,512]{2,1,0:T(8,128)(2,1)S(1)} %slice.26), channel_id=1, source_target_pairs={{0,8},{1,9},{2,10},{3,11},{4,12},{5,13},{6,14},{7,15},{8,0},{9,1},... | collective-permute-start | bytes 1572872 | tf_op jit(solution)/shard_map/ppermute | solution.py:100
  90.2 27.9 %collective-permute-start.15 = (bf16[4,128,512]{2,1,0:T(8,128)(2,1)S(1)}, bf16[4,128,512]{2,1,0:T(8,128)(2,1)S(1)}, u32[]{:S(2)}, u32[]{:S(2)}) collective-permute-start(bf16[4,128,512]{2,1,0:T(8,128)(2,1)S(1)} %slice.27), channel_id=1, source_target_pairs={{0,16},{1,17},{2,18},{3,19},{4,20},{5,21},{6,22},{7,23},{8,24},{9,... | collective-permute-start | bytes 1572872 | tf_op jit(solution)/shard_map/ppermute | solution.py:100
  93.8 24.3 %collective-permute-start.16 = (bf16[128,2048]{1,0:T(8,128)(2,1)S(1)}, bf16[128,2048]{1,0:T(8,128)(2,1)}, u32[]{:S(2)}, u32[]{:S(2)}) collective-permute-start(bf16[128,2048]{1,0:T(8,128)(2,1)S(1)} %slice.28), channel_id=1, source_target_pairs={{0,4},{1,5},{2,6},{3,7},{4,0},{5,1},{6,2},{7,3},{8,12},{9,13},{10,... | collective-permute-start | bytes 1572872 | tf_op jit(solution)/shard_map/ppermute | solution.py:100
  94.3 23.8 %collective-permute-start.17 = (bf16[128,2048]{1,0:T(8,128)(2,1)S(1)}, bf16[128,2048]{1,0:T(8,128)(2,1)}, u32[]{:S(2)}, u32[]{:S(2)}) collective-permute-start(bf16[128,2048]{1,0:T(8,128)(2,1)S(1)} %copy-done.16), channel_id=1, source_target_pairs={{0,2},{1,3},{2,0},{3,1},{4,6},{5,7},{6,4},{7,5},{8,10},{9,11},{10,... | collective-permute-start | bytes 1572872 | tf_op jit(solution)/shard_map/ppermute | solution.py:100
  103.1 14.2 %collective-permute-start.18 = (bf16[3,2,2,128,128]{4,3,2,1,0:T(8,128)(2,1)}, bf16[3,2,2,128,128]{4,3,2,1,0:T(8,128)(2,1)S(1)}, u32[]{:S(2)}, u32[]{:S(2)}) collective-permute-start(bf16[3,2,2,128,128]{4,3,2,1,0:T(8,128)(2,1)} %get-tuple-element.132), channel_id=1, source_target_pairs={{0,4},{1,5},{2,6},{3,7},{4,0},{5,1},{6,2},{7,3},{8,12},{9,13},{10,... | collective-permute-start | bytes 1179656 | tf_op jit(solution)/shard_map/ppermute | solution.py:100
  119.6 26.7 %collective-permute-start.22 = (bf16[4,128,512]{2,1,0:T(8,128)(2,1)}, bf16[4,128,512]{2,1,0:T(8,128)(2,1)}, u32[]{:S(2)}, u32[]{:S(2)}) collective-permute-start(bf16[4,128,512]{2,1,0:T(8,128)(2,1)} %slice.29), channel_id=1, source_target_pairs={{0,16},{1,17},{2,18},{3,19},{4,20},{5,21},{6,22},{7,23},{8,24},{9,... | collective-permute-start | bytes 1572872 | tf_op jit(solution)/shard_map/ppermute | solution.py:100
  120.6 25.8 %collective-permute-start.23 = (bf16[4,128,512]{2,1,0:T(8,128)(2,1)S(1)}, bf16[4,128,512]{2,1,0:T(8,128)(2,1)}, u32[]{:S(2)}, u32[]{:S(2)}) collective-permute-start(bf16[4,128,512]{2,1,0:T(8,128)(2,1)S(1)} %collective-permute-done.15.refs_7_.refs_5_), channel_id=1, source_target_pairs={{0,8},{1,9},{2,10},{3,11},{4,12},{5,13},{6,14},{7,15},{8,0},{9,1},... | collective-permute-start | bytes 1572872 | tf_op jit(solution)/shard_map/ppermute | solution.py:100
  121.6 13.5 %all-to-all-start.3 = ((bf16[8,64,512]{2,1,0:T(8,128)(2,1)}), bf16[8,64,512]{2,1,0:T(8,128)(2,1)S(1)}, u32[]{:S(2)}, u32[]{:S(2)}) async-start(bf16[8,64,512]{2,1,0:T(8,128)(2,1)} %get-tuple-element.141), calls=%async_computation.3 | async-start | bytes 1048576 | tf_op jit(solution)/shard_map/all_to_all | solution.py:184
  131.5 14.8 %collective-permute-start.24 = (bf16[96,2048]{1,0:T(8,128)(2,1)}, bf16[96,2048]{1,0:T(8,128)(2,1)S(1)}, u32[]{:S(2)}, u32[]{:S(2)}) collective-permute-start(bf16[96,2048]{1,0:T(8,128)(2,1)} %get-tuple-element.172.refs_0_), channel_id=1, source_target_pairs={{0,4},{1,5},{2,6},{3,7},{4,0},{5,1},{6,2},{7,3},{8,12},{9,13},{10,... | collective-permute-start | bytes 1179656 | tf_op jit(solution)/shard_map/ppermute | solution.py:100
  133.6 12.8 %collective-permute-start.25 = (bf16[96,2048]{1,0:T(8,128)(2,1)}, bf16[96,2048]{1,0:T(8,128)(2,1)S(1)}, u32[]{:S(2)}, u32[]{:S(2)}) collective-permute-start(bf16[96,2048]{1,0:T(8,128)(2,1)} %get-tuple-element.172.refs_0_), channel_id=1, source_target_pairs={{0,2},{1,3},{2,0},{3,1},{4,6},{5,7},{6,4},{7,5},{8,10},{9,11},{10,... | collective-permute-start | bytes 1179656 | tf_op jit(solution)/shard_map/ppermute | solution.py:100
  149.4 13.1 %collective-permute-start.34 = (bf16[4,128,512]{2,1,0:T(8,128)(2,1)}, bf16[4,128,512]{2,1,0:T(8,128)(2,1)S(1)}, u32[]{:S(2)}, u32[]{:S(2)}) collective-permute-start(bf16[4,128,512]{2,1,0:T(8,128)(2,1)} %collective-permute-done.22.refs_8_.refs_6_), channel_id=1, source_target_pairs={{0,8},{1,9},{2,10},{3,11},{4,12},{5,13},{6,14},{7,15},{8,0},{9,1},... | collective-permute-start | bytes 1572872 | tf_op jit(solution)/shard_map/ppermute | solution.py:100
  160.1 14.9 %collective-permute-start.33 = (bf16[384,512]{1,0:T(8,128)(2,1)S(1)}, bf16[384,512]{1,0:T(8,128)(2,1)S(1)}, u32[]{:S(2)}, u32[]{:S(2)}) collective-permute-start(bf16[384,512]{1,0:T(8,128)(2,1)S(1)} %shard_map.91), channel_id=1, source_target_pairs={{0,4},{1,5},{2,6},{3,7},{4,0},{5,1},{6,2},{7,3},{8,12},{9,13},{10,... | collective-permute-start | bytes 1179656 | tf_op jit(solution)/shard_map/ppermute | solution.py:100
  166.5 13.3 %collective-permute-start.35 = (bf16[384,512]{1,0:T(8,128)(2,1)S(1)}, bf16[384,512]{1,0:T(8,128)(2,1)S(1)}, u32[]{:S(2)}, u32[]{:S(2)}) collective-permute-start(bf16[384,512]{1,0:T(8,128)(2,1)S(1)} %shard_map.92), channel_id=1, source_target_pairs={{0,4},{1,5},{2,6},{3,7},{4,0},{5,1},{6,2},{7,3},{8,12},{9,13},{10,... | collective-permute-start | bytes 1179656 | tf_op jit(solution)/shard_map/ppermute | solution.py:100
  (33 other events, 196.3 us)

commit v6 on v5

--- a/solution.py
+++ b/solution.py
@@ -13,7 +13,7 @@
 AXES = ("dp", "mp")
 BF = jnp.bfloat16
 F32 = jnp.float32
-VMEM_LIMIT = 56 * 1024 * 1024
+VMEM_LIMIT = 50 * 1024 * 1024
 SMALL_LIMIT = 16 * 1024 * 1024
 
 

time: 182 us -> 181 us (level)
  local copies, waits for them, and re-layouts: 6.28 us -> 13.3 us
  Pallas kernels: 46.8 us -> 40.5 us
    unnamed x36 -> x58, local copies, waits for them, and re-layouts: 1.75 us -> 6.93 us
  transfers between devices with their start and end apart: 39 -> 39, of which waited for: 14 -> 15; matrix products, arithmetic and copies ran while one was open for 3% -> 4% of each run, Pallas kernels for 24% -> 21%
where the time goes in v6:
time: 181 us; the launch traced here: 180 us
  waiting for transfers between devices  66.5 us (37%)
  starting transfers between devices  44.6 us (25%)
  Pallas kernels  40.5 us (22%)
  blocking collectives  14 us (8%)
  local copies, waits for them, and re-layouts  13.3 us (7%)
    ppermute x36, waiting for transfers between devices, send(): return lax.ppermute(value, AXES, moves)  50.2 us
    ppermute x36, starting transfers between devices, send(): return lax.ppermute(value, AXES, moves)  30 us
    all_to_all x2, waiting for transfers between devices, in_plane(): lax.all_to_all(pieces, AXES, split_axis=0, concat_axis=0, tiled=True, axi...  16.4 us
    all_to_all x1, blocking collectives, in_plane(): lax.all_to_all(pieces, AXES, split_axis=0, concat_axis=0, tiled=True, axi...  14 us
    pallas_call x4, Pallas kernels, up_part(): pl.pallas_call(functools.partial(up_kernel, len(pieces), half), in_specs=...  13.8 us
    pallas_call x2, Pallas kernels, one_head(): pl.pallas_call(functools.partial(head_kernel, bool(before)), in_specs=[SM...  12.7 us
    all_to_all x1, starting transfers between devices, to_all(): mine = lax.all_to_all(pieces, AXES, split_axis=0, concat_axis=0, tiled=True)  7.41 us
    all_to_all x2, starting transfers between devices, in_plane(): lax.all_to_all(pieces, AXES, split_axis=0, concat_axis=0, tiled=True, axi...  7.25 us
  transfers between devices with their start and end apart: 39, of which 15 were waited for; matrix products, arithmetic and copies ran while one was open for 4% of the time, Pallas kernels for 21%

profile of v6, /device:TPU:0, one launch (start us, length us, event | category | flops | bytes accessed | tf_op | source)
XLA Modules:
  0.0 180.3 jit_solution(13281632738386671828)
XLA Ops:
  3.3 7.4 %all-to-all-start = ((bf16[32,64,384]{2,1,0:T(8,128)(2,1)}), bf16[32,64,384]{2,1,0:T(8,128)(2,1)}, u32[]{:S(2)}, u32[]{:S(2)}) async-start(bf16[32,64,384]{2,1,0:T(8,128)(2,1)} %shard_map.85), calls=%async_computation | async-start | bytes 3145728 | tf_op jit(solution)/shard_map/all_to_all | solution.py:179
  10.9 1.7 shard_map.86
  13.4 1.7 collective-permute-start.2
  18.6 1.9 %constant_dynamic-slice_fusion = bf16[128,2048]{1,0:T(8,128)(2,1)} fusion(bf16[512,2048]{1,0:T(8,128)(2,1)} %own, s32[]{:T(128)S(6)} %select_n.20), kind=kLoop, calls=%fused_computation.3 | loop fusion | bytes 1048580 | tf_op jit(solution)/shard_map/dynamic_slice | solution.py:434
  20.5 2.4 %constant_dynamic-slice_fusion.1 = bf16[256,2048]{1,0:T(8,128)(2,1)} fusion(bf16[512,2048]{1,0:T(8,128)(2,1)} %own, s32[]{:T(128)S(6)} %select_n.19), kind=kLoop, calls=%fused_computation.4 | loop fusion | bytes 2097156 | tf_op jit(solution)/shard_map/dynamic_slice | solution.py:433
  22.9 13.0 %collective-permute-done.2.refs_1_ = bf16[96,2048]{1,0:T(8,128)(2,1)S(1)} collective-permute-done((bf16[96,2048]{1,0:T(8,128)(2,1)S(1)}, bf16[96,2048]{1,0:T(8,128)(2,1)S(1)}, u32[]{:S(2)}, u32[]{:S(2)}) %collective-permute-start.2) | collective-permute-done | bytes 393248 | tf_op jit(solution)/shard_map/ppermute | solution.py:100
  35.9 2.3 %collective-permute-start.4 = (bf16[48,2048]{1,0:T(8,128)(2,1)S(1)}, bf16[48,2048]{1,0:T(8,128)(2,1)S(1)}, u32[]{:S(2)}, u32[]{:S(2)}) collective-permute-start(bf16[48,2048]{1,0:T(8,128)(2,1)S(1)} %slice.32), channel_id=1, source_target_pairs={{0,2},{1,3},{2,0},{3,1},{4,6},{5,7},{6,4},{7,5},{8,10},{9,11},{10,... | collective-permute-start | bytes 589832 | tf_op jit(solution)/shard_map/ppermute | solution.py:100
  38.4 11.6 %collective-permute-done.got = bf16[8,64,512]{2,1,0:T(8,128)(2,1)S(1)} collective-permute-done((bf16[8,64,512]{2,1,0:T(8,128)(2,1)}, bf16[8,64,512]{2,1,0:T(8,128)(2,1)S(1)}, u32[]{:S(2)}, u32[]{:S(2)}) %collective-permute-start) | collective-permute-done | bytes 524320 | tf_op jit(solution)/shard_map/ppermute | solution.py:100
  53.4 3.6 %all-to-all-start.1 = ((bf16[8,128,512]{2,1,0:T(8,128)(2,1)}), bf16[8,128,512]{2,1,0:T(8,128)(2,1)S(1)}, u32[]{:S(2)}, u32[]{:S(2)}) async-start(bf16[8,128,512]{2,1,0:T(8,128)(2,1)} %shard_map.87), calls=%async_computation.1 | async-start | bytes 2097152 | tf_op jit(solution)/shard_map/all_to_all | solution.py:184
  62.5 6.0 %shard_map.88 = (bf16[768,256]{1,0:T(8,128)(2,1)S(1)}, bf16[3,2,2,128,128]{4,3,2,1,0:T(8,128)(2,1)S(1)}, bf16[3,2,2,128,128]{4,3,2,1,0:T(8,128)(2,1)S(1)}) custom-call(s32[3]{0:T(128)S(1)} %pad_add_fusion.1.pos, f32[2]{0:T(128)S(1)} %multiply_exponential_fusion.slope, s32[2,1,384]{2,1,0:T(1,128)S(1)} %broadcast_in_dim.3.seg_rows, ...), custom_call_target="tpu_custom_call" | custom-call | tf_op jit(solution)/shard_map/pallas_call | solution.py:244
  72.8 15.6 %all-to-all-done.1.refs_6_.refs_4_ = bf16[8,128,512]{2,1,0:T(8,128)(2,1)S(1)} async-done(((bf16[8,128,512]{2,1,0:T(8,128)(2,1)}), bf16[8,128,512]{2,1,0:T(8,128)(2,1)S(1)}, u32[]{:S(2)}, u32[]{:S(2)}) %all-to-all-start.1) | async-done | bytes 1048608 | tf_op jit(solution)/shard_map/all_to_all | solution.py:184
  90.1 2.5 %collective-permute-start.15 = (bf16[4,128,512]{2,1,0:T(8,128)(2,1)S(1)}, bf16[4,128,512]{2,1,0:T(8,128)(2,1)S(1)}, u32[]{:S(2)}, u32[]{:S(2)}) collective-permute-start(bf16[4,128,512]{2,1,0:T(8,128)(2,1)S(1)} %slice.27), channel_id=1, source_target_pairs={{0,16},{1,17},{2,18},{3,19},{4,20},{5,21},{6,22},{7,23},{8,24},{9,... | collective-permute-start | bytes 1572872 | tf_op jit(solution)/shard_map/ppermute | solution.py:100
  95.8 6.7 %shard_map.89 = (bf16[768,256]{1,0:T(8,128)(2,1)S(1)}, bf16[3,2,2,128,128]{4,3,2,1,0:T(8,128)(2,1)S(1)}, bf16[3,2,2,128,128]{4,3,2,1,0:T(8,128)(2,1)S(1)}) custom-call(s32[3]{0:T(128)S(1)} %pad_add_fusion.1.pos, f32[2]{0:T(128)S(1)} %multiply_exponential_fusion.slope, s32[2,1,384]{2,1,0:T(1,128)S(1)} %broadcast_in_dim.3.seg_rows, ...), custom_call_target="tpu_custom_call" | custom-call | tf_op jit(solution)/shard_map/pallas_call | solution.py:244
  103.2 14.0 %all_to_all.20.ctx = bf16[8,96,256]{2,1,0:T(8,128)(2,1)S(1)} all-to-all(bf16[8,96,256]{2,1,0:T(8,128)(2,1)S(1)} %bitcast.5), channel_id=1, replica_groups={{0,1,2,3,4,5,6,7},{8,9,10,11,12,13,14,15},{16,17,18,19,20,21,22,23},{24..., dimensions={0} | all-to-all | bytes 786432 | tf_op jit(solution)/shard_map/all_to_all | solution.py:184
  120.6 3.7 %all-to-all-start.3 = ((bf16[8,64,512]{2,1,0:T(8,128)(2,1)}), bf16[8,64,512]{2,1,0:T(8,128)(2,1)S(1)}, u32[]{:S(2)}, u32[]{:S(2)}) async-start(bf16[8,64,512]{2,1,0:T(8,128)(2,1)} %get-tuple-element.141), calls=%async_computation.3 | async-start | bytes 1048576 | tf_op jit(solution)/shard_map/all_to_all | solution.py:184
  124.4 5.5 %shard_map.90 = (bf16[96,2048]{1,0:T(8,128)(2,1)}, bf16[96,2048]{1,0:T(8,128)(2,1)}) custom-call(s32[3]{0:T(128)S(1)} %pad_add_fusion.1.pos, bf16[96,2048]{1,0:T(8,128)(2,1)S(1)} %copy-done.2, bf16[8,96,256]{2,1,0:T(8,128)(2,1)S(1)} %all_to_all.20.ctx, bf16[512,2048]{1,0:T(8,128)(2,1)} %own, bf16[512,2048]{1,0:T(8,128)(2,1)} %collective-permute-done.8.cross, ...), custom_call_target="tpu_custom_call" | custom-call | tf_op jit(solution)/shard_map/pallas_call | solution.py:289
  129.9 2.1 %collective-permute-start.24 = (bf16[96,2048]{1,0:T(8,128)(2,1)}, bf16[96,2048]{1,0:T(8,128)(2,1)S(1)}, u32[]{:S(2)}, u32[]{:S(2)}) collective-permute-start(bf16[96,2048]{1,0:T(8,128)(2,1)} %get-tuple-element.172.refs_0_), channel_id=1, source_target_pairs={{0,4},{1,5},{2,6},{3,7},{4,0},{5,1},{6,2},{7,3},{8,12},{9,13},{10,... | collective-permute-start | bytes 1179656 | tf_op jit(solution)/shard_map/ppermute | solution.py:100
  134.2 11.2 %collective-permute-done.22.refs_8_.refs_6_ = bf16[4,128,512]{2,1,0:T(8,128)(2,1)} collective-permute-done((bf16[4,128,512]{2,1,0:T(8,128)(2,1)}, bf16[4,128,512]{2,1,0:T(8,128)(2,1)}, u32[]{:S(2)}, u32[]{:S(2)}) %collective-permute-start.22) | collective-permute-done | bytes 524320 | tf_op jit(solution)/shard_map/ppermute | solution.py:100
  148.5 3.4 %collective-permute-done.26.refs_1_ = bf16[48,2048]{1,0:T(8,128)(2,1)S(1)} collective-permute-done((bf16[48,2048]{1,0:T(8,128)(2,1)S(1)}, bf16[48,2048]{1,0:T(8,128)(2,1)S(1)}, u32[]{:S(2)}, u32[]{:S(2)}) %collective-permute-start.26) | collective-permute-done | bytes 196640 | tf_op jit(solution)/shard_map/ppermute | solution.py:100
  155.3 3.9 %shard_map.91 = bf16[384,512]{1,0:T(8,128)(2,1)S(1)} custom-call(s32[3]{0:T(128)S(1)} %pad_add_fusion.1.pos, bf16[96,2048]{1,0:T(8,128)(2,1)S(1)} %collective-permute-done.24.refs_0_, bf16[48,2048]{1,0:T(8,128)(2,1)S(1)} %collective-permute-done.26.refs_1_, bf16[48,2048]{1,0:T(8,128)(2,1)S(1)} %collective-permute-done.27.refs_2_, ...), custom_call_target="tpu_custom_call" | custom-call | tf_op jit(solution)/shard_map/pallas_call | solution.py:340
  161.7 3.8 %shard_map.92 = bf16[384,512]{1,0:T(8,128)(2,1)S(1)} custom-call(s32[3]{0:T(128)S(1)} %pad_add_fusion.1.pos, bf16[96,2048]{1,0:T(8,128)(2,1)S(1)} %collective-permute-done.24.refs_0_, bf16[48,2048]{1,0:T(8,128)(2,1)S(1)} %collective-permute-done.26.refs_1_, bf16[48,2048]{1,0:T(8,128)(2,1)S(1)} %collective-permute-done.27.refs_2_, ...), custom_call_target="tpu_custom_call" | custom-call | tf_op jit(solution)/shard_map/pallas_call | solution.py:340
  167.6 3.1 %shard_map.93.refs_1_ = bf16[384,512]{1,0:T(8,128)(2,1)S(1)} custom-call(s32[3]{0:T(128)S(1)} %pad_add_fusion.1.pos, bf16[96,2048]{1,0:T(8,128)(2,1)} %get-tuple-element.172.refs_0_, bf16[96,2048]{1,0:T(8,128)(2,1)S(1)} %collective-permute-done.25.refs_1_, bf16[96,2048]{1,0:T(8,128)(2,1)S(1)} %collective-permute-done.31.refs_2_, ...), custom_call_target="tpu_custom_call" | custom-call | tf_op jit(solution)/shard_map/pallas_call | solution.py:340
  170.7 3.0 %shard_map.94.refs_2_ = bf16[384,512]{1,0:T(8,128)(2,1)S(1)} custom-call(s32[3]{0:T(128)S(1)} %pad_add_fusion.1.pos, bf16[96,2048]{1,0:T(8,128)(2,1)} %get-tuple-element.172.refs_0_, bf16[96,2048]{1,0:T(8,128)(2,1)S(1)} %collective-permute-done.25.refs_1_, bf16[96,2048]{1,0:T(8,128)(2,1)S(1)} %collective-permute-done.31.refs_2_, ...), custom_call_target="tpu_custom_call" | custom-call | tf_op jit(solution)/shard_map/pallas_call | solution.py:340
  175.4 3.4 %collective-permute-done.35.refs_1_ = bf16[384,512]{1,0:T(8,128)(2,1)S(1)} collective-permute-done((bf16[384,512]{1,0:T(8,128)(2,1)S(1)}, bf16[384,512]{1,0:T(8,128)(2,1)S(1)}, u32[]{:S(2)}, u32[]{:S(2)}) %collective-permute-start.35) | collective-permute-done | bytes 393248 | tf_op jit(solution)/shard_map/ppermute | solution.py:100
  (140 shorter events, 45.4 us)
Async XLA Ops:
  3.3 46.7 %all-to-all-start = ((bf16[32,64,384]{2,1,0:T(8,128)(2,1)}), bf16[32,64,384]{2,1,0:T(8,128)(2,1)}, u32[]{:S(2)}, u32[]{:S(2)}) async-start(bf16[32,64,384]{2,1,0:T(8,128)(2,1)} %shard_map.85), calls=%async_computation | async-start | bytes 3145728 | tf_op jit(solution)/shard_map/all_to_all | solution.py:179
  13.4 22.5 %collective-permute-start.2 = (bf16[96,2048]{1,0:T(8,128)(2,1)S(1)}, bf16[96,2048]{1,0:T(8,128)(2,1)S(1)}, u32[]{:S(2)}, u32[]{:S(2)}) collective-permute-start(bf16[96,2048]{1,0:T(8,128)(2,1)S(1)} %get-tuple-element.112.refs_0_), channel_id=1, source_target_pairs={{0,4},{1,5},{2,6},{3,7},{4,0},{5,1},{6,2},{7,3},{8,12},{9,13},{10,... | collective-permute-start | bytes 1179656 | tf_op jit(solution)/shard_map/ppermute | solution.py:100
  15.1 23.1 %collective-permute-start.3 = (bf16[96,2048]{1,0:T(8,128)(2,1)S(1)}, bf16[96,2048]{1,0:T(8,128)(2,1)S(1)}, u32[]{:S(2)}, u32[]{:S(2)}) collective-permute-start(bf16[96,2048]{1,0:T(8,128)(2,1)S(1)} %get-tuple-element.112.refs_0_), channel_id=1, source_target_pairs={{0,2},{1,3},{2,0},{3,1},{4,6},{5,7},{6,4},{7,5},{8,10},{9,11},{10,... | collective-permute-start | bytes 1179656 | tf_op jit(solution)/shard_map/ppermute | solution.py:100
  16.6 33.4 %collective-permute-start = (bf16[8,64,512]{2,1,0:T(8,128)(2,1)}, bf16[8,64,512]{2,1,0:T(8,128)(2,1)S(1)}, u32[]{:S(2)}, u32[]{:S(2)}) collective-permute-start(bf16[8,64,512]{2,1,0:T(8,128)(2,1)} %get-tuple-element.141), channel_id=1, source_target_pairs={{0,8},{1,9},{2,10},{3,11},{4,12},{5,13},{6,14},{7,15},{8,0},{9,1},... | collective-permute-start | bytes 1572872 | tf_op jit(solution)/shard_map/ppermute | solution.py:100
  18.0 20.3 %collective-permute-start.1 = (s32[1,384]{1,0:T(1,128)S(1)}, s32[1,384]{1,0:T(1,128)S(1)}, u32[]{:S(2)}, u32[]{:S(2)}) collective-permute-start(s32[1,384]{1,0:T(1,128)S(1)} %copy-done.28), channel_id=1, source_target_pairs={{0,4},{1,5},{2,6},{3,7},{4,0},{5,1},{6,2},{7,3},{8,12},{9,13},{10,... | collective-permute-start | bytes 4616 | tf_op jit(solution)/shard_map/ppermute | solution.py:100
  35.9 14.1 %collective-permute-start.4 = (bf16[48,2048]{1,0:T(8,128)(2,1)S(1)}, bf16[48,2048]{1,0:T(8,128)(2,1)S(1)}, u32[]{:S(2)}, u32[]{:S(2)}) collective-permute-start(bf16[48,2048]{1,0:T(8,128)(2,1)S(1)} %slice.32), channel_id=1, source_target_pairs={{0,2},{1,3},{2,0},{3,1},{4,6},{5,7},{6,4},{7,5},{8,10},{9,11},{10,... | collective-permute-start | bytes 589832 | tf_op jit(solution)/shard_map/ppermute | solution.py:100
  38.2 11.8 %collective-permute-start.5 = (bf16[48,2048]{1,0:T(8,128)(2,1)S(1)}, bf16[48,2048]{1,0:T(8,128)(2,1)S(1)}, u32[]{:S(2)}, u32[]{:S(2)}) collective-permute-start(bf16[48,2048]{1,0:T(8,128)(2,1)S(1)} %slice.33), channel_id=1, source_target_pairs={{0,4},{1,5},{2,6},{3,7},{4,0},{5,1},{6,2},{7,3},{8,12},{9,13},{10,... | collective-permute-start | bytes 589832 | tf_op jit(solution)/shard_map/ppermute | solution.py:100
  50.0 38.4 %collective-permute-start.8 = (bf16[512,2048]{1,0:T(8,128)(2,1)}, bf16[512,2048]{1,0:T(8,128)(2,1)}, u32[]{:S(2)}, u32[]{:S(2)}) collective-permute-start(bf16[512,2048]{1,0:T(8,128)(2,1)} %own), channel_id=1, source_target_pairs={{0,1},{1,0},{2,3},{3,2},{4,5},{5,4},{6,7},{7,6},{8,9},{9,8},{10,11... | collective-permute-start | bytes 6291464 | tf_op jit(solution)/shard_map/ppermute | solution.py:100
  50.1 38.3 %collective-permute-start.6 = (bf16[2048,384]{1,0:T(8,128)(2,1)}, bf16[2048,384]{1,0:T(8,128)(2,1)}, u32[]{:S(2)}, u32[]{:S(2)}) collective-permute-start(bf16[2048,384]{1,0:T(8,128)(2,1)} %bitcast.refs_10_), channel_id=1, source_target_pairs={{0,8},{1,9},{2,10},{3,11},{4,12},{5,13},{6,14},{7,15},{8,0},{9,1},... | collective-permute-start | bytes 4718600 | tf_op jit(solution)/shard_map/ppermute | solution.py:100
  51.0 37.5 %collective-permute-start.7 = (bf16[256,2048]{1,0:T(8,128)(2,1)}, bf16[256,2048]{1,0:T(8,128)(2,1)}, u32[]{:S(2)}, u32[]{:S(2)}) collective-permute-start(bf16[256,2048]{1,0:T(8,128)(2,1)} %constant_dynamic-slice_fusion.1), channel_id=1, source_target_pairs={{0,2},{1,3},{2,0},{3,1},{4,6},{5,7},{6,4},{7,5},{8,10},{9,11},{10,... | collective-permute-start | bytes 3145736 | tf_op jit(solution)/shard_map/ppermute | solution.py:100
  53.4 35.0 %all-to-all-start.1 = ((bf16[8,128,512]{2,1,0:T(8,128)(2,1)}), bf16[8,128,512]{2,1,0:T(8,128)(2,1)S(1)}, u32[]{:S(2)}, u32[]{:S(2)}) async-start(bf16[8,128,512]{2,1,0:T(8,128)(2,1)} %shard_map.87), calls=%async_computation.1 | async-start | bytes 2097152 | tf_op jit(solution)/shard_map/all_to_all | solution.py:184
  88.6 28.5 %collective-permute-start.14 = (bf16[8,64,512]{2,1,0:T(8,128)(2,1)S(1)}, bf16[8,64,512]{2,1,0:T(8,128)(2,1)S(1)}, u32[]{:S(2)}, u32[]{:S(2)}) collective-permute-start(bf16[8,64,512]{2,1,0:T(8,128)(2,1)S(1)} %slice.26), channel_id=1, source_target_pairs={{0,8},{1,9},{2,10},{3,11},{4,12},{5,13},{6,14},{7,15},{8,0},{9,1},... | collective-permute-start | bytes 1572872 | tf_op jit(solution)/shard_map/ppermute | solution.py:100
  90.1 27.0 %collective-permute-start.15 = (bf16[4,128,512]{2,1,0:T(8,128)(2,1)S(1)}, bf16[4,128,512]{2,1,0:T(8,128)(2,1)S(1)}, u32[]{:S(2)}, u32[]{:S(2)}) collective-permute-start(bf16[4,128,512]{2,1,0:T(8,128)(2,1)S(1)} %slice.27), channel_id=1, source_target_pairs={{0,16},{1,17},{2,18},{3,19},{4,20},{5,21},{6,22},{7,23},{8,24},{9,... | collective-permute-start | bytes 1572872 | tf_op jit(solution)/shard_map/ppermute | solution.py:100
  93.7 23.4 %collective-permute-start.16 = (bf16[128,2048]{1,0:T(8,128)(2,1)S(1)}, bf16[128,2048]{1,0:T(8,128)(2,1)}, u32[]{:S(2)}, u32[]{:S(2)}) collective-permute-start(bf16[128,2048]{1,0:T(8,128)(2,1)S(1)} %slice.28), channel_id=1, source_target_pairs={{0,4},{1,5},{2,6},{3,7},{4,0},{5,1},{6,2},{7,3},{8,12},{9,13},{10,... | collective-permute-start | bytes 1572872 | tf_op jit(solution)/shard_map/ppermute | solution.py:100
  94.2 23.0 %collective-permute-start.17 = (bf16[128,2048]{1,0:T(8,128)(2,1)S(1)}, bf16[128,2048]{1,0:T(8,128)(2,1)}, u32[]{:S(2)}, u32[]{:S(2)}) collective-permute-start(bf16[128,2048]{1,0:T(8,128)(2,1)S(1)} %copy-done.27), channel_id=1, source_target_pairs={{0,2},{1,3},{2,0},{3,1},{4,6},{5,7},{6,4},{7,5},{8,10},{9,11},{10,... | collective-permute-start | bytes 1572872 | tf_op jit(solution)/shard_map/ppermute | solution.py:100
  102.5 14.6 %collective-permute-start.18 = (bf16[3,2,2,128,128]{4,3,2,1,0:T(8,128)(2,1)S(1)}, bf16[3,2,2,128,128]{4,3,2,1,0:T(8,128)(2,1)S(1)}, u32[]{:S(2)}, u32[]{:S(2)}) collective-permute-start(bf16[3,2,2,128,128]{4,3,2,1,0:T(8,128)(2,1)S(1)} %get-tuple-element.132), channel_id=1, source_target_pairs={{0,4},{1,5},{2,6},{3,7},{4,0},{5,1},{6,2},{7,3},{8,12},{9,13},{10,... | collective-permute-start | bytes 1179656 | tf_op jit(solution)/shard_map/ppermute | solution.py:100
  118.7 26.7 %collective-permute-start.22 = (bf16[4,128,512]{2,1,0:T(8,128)(2,1)}, bf16[4,128,512]{2,1,0:T(8,128)(2,1)}, u32[]{:S(2)}, u32[]{:S(2)}) collective-permute-start(bf16[4,128,512]{2,1,0:T(8,128)(2,1)} %slice.29), channel_id=1, source_target_pairs={{0,16},{1,17},{2,18},{3,19},{4,20},{5,21},{6,22},{7,23},{8,24},{9,... | collective-permute-start | bytes 1572872 | tf_op jit(solution)/shard_map/ppermute | solution.py:100
  119.7 25.7 %collective-permute-start.23 = (bf16[4,128,512]{2,1,0:T(8,128)(2,1)S(1)}, bf16[4,128,512]{2,1,0:T(8,128)(2,1)}, u32[]{:S(2)}, u32[]{:S(2)}) collective-permute-start(bf16[4,128,512]{2,1,0:T(8,128)(2,1)S(1)} %collective-permute-done.15.refs_7_.refs_5_), channel_id=1, source_target_pairs={{0,8},{1,9},{2,10},{3,11},{4,12},{5,13},{6,14},{7,15},{8,0},{9,1},... | collective-permute-start | bytes 1572872 | tf_op jit(solution)/shard_map/ppermute | solution.py:100
  120.6 13.5 %all-to-all-start.3 = ((bf16[8,64,512]{2,1,0:T(8,128)(2,1)}), bf16[8,64,512]{2,1,0:T(8,128)(2,1)S(1)}, u32[]{:S(2)}, u32[]{:S(2)}) async-start(bf16[8,64,512]{2,1,0:T(8,128)(2,1)} %get-tuple-element.141), calls=%async_computation.3 | async-start | bytes 1048576 | tf_op jit(solution)/shard_map/all_to_all | solution.py:184
  129.9 15.5 %collective-permute-start.24 = (bf16[96,2048]{1,0:T(8,128)(2,1)}, bf16[96,2048]{1,0:T(8,128)(2,1)S(1)}, u32[]{:S(2)}, u32[]{:S(2)}) collective-permute-start(bf16[96,2048]{1,0:T(8,128)(2,1)} %get-tuple-element.172.refs_0_), channel_id=1, source_target_pairs={{0,4},{1,5},{2,6},{3,7},{4,0},{5,1},{6,2},{7,3},{8,12},{9,13},{10,... | collective-permute-start | bytes 1179656 | tf_op jit(solution)/shard_map/ppermute | solution.py:100
  131.9 13.5 %collective-permute-start.25 = (bf16[96,2048]{1,0:T(8,128)(2,1)}, bf16[96,2048]{1,0:T(8,128)(2,1)S(1)}, u32[]{:S(2)}, u32[]{:S(2)}) collective-permute-start(bf16[96,2048]{1,0:T(8,128)(2,1)} %get-tuple-element.172.refs_0_), channel_id=1, source_target_pairs={{0,2},{1,3},{2,0},{3,1},{4,6},{5,7},{6,4},{7,5},{8,10},{9,11},{10,... | collective-permute-start | bytes 1179656 | tf_op jit(solution)/shard_map/ppermute | solution.py:100
  148.5 13.1 %collective-permute-start.34 = (bf16[4,128,512]{2,1,0:T(8,128)(2,1)}, bf16[4,128,512]{2,1,0:T(8,128)(2,1)S(1)}, u32[]{:S(2)}, u32[]{:S(2)}) collective-permute-start(bf16[4,128,512]{2,1,0:T(8,128)(2,1)} %collective-permute-done.22.refs_8_.refs_6_), channel_id=1, source_target_pairs={{0,8},{1,9},{2,10},{3,11},{4,12},{5,13},{6,14},{7,15},{8,0},{9,1},... | collective-permute-start | bytes 1572872 | tf_op jit(solution)/shard_map/ppermute | solution.py:100
  159.2 14.6 %collective-permute-start.33 = (bf16[384,512]{1,0:T(8,128)(2,1)S(1)}, bf16[384,512]{1,0:T(8,128)(2,1)S(1)}, u32[]{:S(2)}, u32[]{:S(2)}) collective-permute-start(bf16[384,512]{1,0:T(8,128)(2,1)S(1)} %shard_map.91), channel_id=1, source_target_pairs={{0,4},{1,5},{2,6},{3,7},{4,0},{5,1},{6,2},{7,3},{8,12},{9,13},{10,... | collective-permute-start | bytes 1179656 | tf_op jit(solution)/shard_map/ppermute | solution.py:100
  165.5 13.3 %collective-permute-start.35 = (bf16[384,512]{1,0:T(8,128)(2,1)S(1)}, bf16[384,512]{1,0:T(8,128)(2,1)S(1)}, u32[]{:S(2)}, u32[]{:S(2)}) collective-permute-start(bf16[384,512]{1,0:T(8,128)(2,1)S(1)} %shard_map.92), channel_id=1, source_target_pairs={{0,4},{1,5},{2,6},{3,7},{4,0},{5,1},{6,2},{7,3},{8,12},{9,13},{10,... | collective-permute-start | bytes 1179656 | tf_op jit(solution)/shard_map/ppermute | solution.py:100
  (44 other events, 305.1 us)

commit v7 on v6

--- a/solution.py
+++ b/solution.py
@@ -166,10 +166,12 @@
 
 def stack_rows(own, got):
     count, rows, width = own.shape
+    step = count // 4
     return pl.pallas_call(
         stack_kernel,
-        in_specs=[VMEM, VMEM],
-        out_specs=VMEM,
+        grid=(count // step,),
+        in_specs=[pl.BlockSpec((step, rows, width), lambda i: (i, 0, 0))] * 2,
+        out_specs=pl.BlockSpec((step, 2 * rows, width), lambda i: (i, 0, 0)),
         out_shape=jax.ShapeDtypeStruct((count, 2 * rows, width), BF),
         compiler_params=params(),
     )(own, got)

time: 181 us -> 181 us (level)
  no operation moved by 1% of the time
where the time goes in v7:
time: 181 us; the launch traced here: 180 us
  waiting for transfers between devices  66.1 us (37%)
  starting transfers between devices  44.6 us (25%)
  Pallas kernels  41 us (23%)
  blocking collectives  14 us (8%)
  local copies, waits for them, and re-layouts  13.3 us (7%)
    ppermute x36, waiting for transfers between devices, send(): return lax.ppermute(value, AXES, moves)  50.2 us
    ppermute x36, starting transfers between devices, send(): return lax.ppermute(value, AXES, moves)  30 us
    all_to_all x2, waiting for transfers between devices, in_plane(): lax.all_to_all(pieces, AXES, split_axis=0, concat_axis=0, tiled=True, axi...  15.9 us
    all_to_all x1, blocking collectives, in_plane(): lax.all_to_all(pieces, AXES, split_axis=0, concat_axis=0, tiled=True, axi...  14 us
    pallas_call x4, Pallas kernels, up_part(): pl.pallas_call(functools.partial(up_kernel, len(pieces), half), in_specs=...  13.8 us
    pallas_call x2, Pallas kernels, one_head(): pl.pallas_call(functools.partial(head_kernel, bool(before)), in_specs=[SM...  12.7 us
    all_to_all x1, starting transfers between devices, to_all(): mine = lax.all_to_all(pieces, AXES, split_axis=0, concat_axis=0, tiled=True)  7.41 us
    all_to_all x2, starting transfers between devices, in_plane(): lax.all_to_all(pieces, AXES, split_axis=0, concat_axis=0, tiled=True, axi...  7.25 us
  transfers between devices with their start and end apart: 39, of which 15 were waited for; matrix products, arithmetic and copies ran while one was open for 4% of the time, Pallas kernels for 21%

profile of v7, /device:TPU:0, one launch (start us, length us, event | category | flops | bytes accessed | tf_op | source)
XLA Modules:
  0.0 180.3 jit_solution(5436281157205213814)
XLA Ops:
  3.3 7.4 %all-to-all-start = ((bf16[32,64,384]{2,1,0:T(8,128)(2,1)}), bf16[32,64,384]{2,1,0:T(8,128)(2,1)}, u32[]{:S(2)}, u32[]{:S(2)}) async-start(bf16[32,64,384]{2,1,0:T(8,128)(2,1)} %shard_map.85), calls=%async_computation | async-start | bytes 3145728 | tf_op jit(solution)/shard_map/all_to_all | solution.py:181
  10.9 1.7 shard_map.86
  13.4 1.7 collective-permute-start.2
  18.6 1.9 %constant_dynamic-slice_fusion = bf16[128,2048]{1,0:T(8,128)(2,1)} fusion(bf16[512,2048]{1,0:T(8,128)(2,1)} %own, s32[]{:T(128)S(6)} %select_n.20), kind=kLoop, calls=%fused_computation.3 | loop fusion | bytes 1048580 | tf_op jit(solution)/shard_map/dynamic_slice | solution.py:436
  20.5 2.4 %constant_dynamic-slice_fusion.1 = bf16[256,2048]{1,0:T(8,128)(2,1)} fusion(bf16[512,2048]{1,0:T(8,128)(2,1)} %own, s32[]{:T(128)S(6)} %select_n.19), kind=kLoop, calls=%fused_computation.4 | loop fusion | bytes 2097156 | tf_op jit(solution)/shard_map/dynamic_slice | solution.py:435
  22.9 13.0 %collective-permute-done.2.refs_1_ = bf16[96,2048]{1,0:T(8,128)(2,1)S(1)} collective-permute-done((bf16[96,2048]{1,0:T(8,128)(2,1)S(1)}, bf16[96,2048]{1,0:T(8,128)(2,1)S(1)}, u32[]{:S(2)}, u32[]{:S(2)}) %collective-permute-start.2) | collective-permute-done | bytes 393248 | tf_op jit(solution)/shard_map/ppermute | solution.py:100
  35.9 2.3 %collective-permute-start.4 = (bf16[48,2048]{1,0:T(8,128)(2,1)S(1)}, bf16[48,2048]{1,0:T(8,128)(2,1)S(1)}, u32[]{:S(2)}, u32[]{:S(2)}) collective-permute-start(bf16[48,2048]{1,0:T(8,128)(2,1)S(1)} %slice.32), channel_id=1, source_target_pairs={{0,2},{1,3},{2,0},{3,1},{4,6},{5,7},{6,4},{7,5},{8,10},{9,11},{10,... | collective-permute-start | bytes 589832 | tf_op jit(solution)/shard_map/ppermute | solution.py:100
  38.4 11.6 %collective-permute-done.got = bf16[8,64,512]{2,1,0:T(8,128)(2,1)S(1)} collective-permute-done((bf16[8,64,512]{2,1,0:T(8,128)(2,1)}, bf16[8,64,512]{2,1,0:T(8,128)(2,1)S(1)}, u32[]{:S(2)}, u32[]{:S(2)}) %collective-permute-start) | collective-permute-done | bytes 524320 | tf_op jit(solution)/shard_map/ppermute | solution.py:100
  53.9 3.6 %all-to-all-start.1 = ((bf16[8,128,512]{2,1,0:T(8,128)(2,1)}), bf16[8,128,512]{2,1,0:T(8,128)(2,1)S(1)}, u32[]{:S(2)}, u32[]{:S(2)}) async-start(bf16[8,128,512]{2,1,0:T(8,128)(2,1)} %shard_map.87), calls=%async_computation.1 | async-start | bytes 2097152 | tf_op jit(solution)/shard_map/all_to_all | solution.py:186
  62.9 6.0 %shard_map.88 = (bf16[768,256]{1,0:T(8,128)(2,1)S(1)}, bf16[3,2,2,128,128]{4,3,2,1,0:T(8,128)(2,1)S(1)}, bf16[3,2,2,128,128]{4,3,2,1,0:T(8,128)(2,1)S(1)}) custom-call(s32[3]{0:T(128)S(1)} %pad_add_fusion.1.pos, f32[2]{0:T(128)S(1)} %multiply_exponential_fusion.slope, s32[2,1,384]{2,1,0:T(1,128)S(1)} %broadcast_in_dim.3.seg_rows, ...), custom_call_target="tpu_custom_call" | custom-call | tf_op jit(solution)/shard_map/pallas_call | solution.py:246
  73.3 15.1 %all-to-all-done.1.refs_6_.refs_4_ = bf16[8,128,512]{2,1,0:T(8,128)(2,1)S(1)} async-done(((bf16[8,128,512]{2,1,0:T(8,128)(2,1)}), bf16[8,128,512]{2,1,0:T(8,128)(2,1)S(1)}, u32[]{:S(2)}, u32[]{:S(2)}) %all-to-all-start.1) | async-done | bytes 1048608 | tf_op jit(solution)/shard_map/all_to_all | solution.py:186
  90.1 2.5 %collective-permute-start.15 = (bf16[4,128,512]{2,1,0:T(8,128)(2,1)S(1)}, bf16[4,128,512]{2,1,0:T(8,128)(2,1)S(1)}, u32[]{:S(2)}, u32[]{:S(2)}) collective-permute-start(bf16[4,128,512]{2,1,0:T(8,128)(2,1)S(1)} %slice.27), channel_id=1, source_target_pairs={{0,16},{1,17},{2,18},{3,19},{4,20},{5,21},{6,22},{7,23},{8,24},{9,... | collective-permute-start | bytes 1572872 | tf_op jit(solution)/shard_map/ppermute | solution.py:100
  95.8 6.7 %shard_map.89 = (bf16[768,256]{1,0:T(8,128)(2,1)S(1)}, bf16[3,2,2,128,128]{4,3,2,1,0:T(8,128)(2,1)S(1)}, bf16[3,2,2,128,128]{4,3,2,1,0:T(8,128)(2,1)S(1)}) custom-call(s32[3]{0:T(128)S(1)} %pad_add_fusion.1.pos, f32[2]{0:T(128)S(1)} %multiply_exponential_fusion.slope, s32[2,1,384]{2,1,0:T(1,128)S(1)} %broadcast_in_dim.3.seg_rows, ...), custom_call_target="tpu_custom_call" | custom-call | tf_op jit(solution)/shard_map/pallas_call | solution.py:246
  103.2 14.0 %all_to_all.20.ctx = bf16[8,96,256]{2,1,0:T(8,128)(2,1)S(1)} all-to-all(bf16[8,96,256]{2,1,0:T(8,128)(2,1)S(1)} %bitcast.5), channel_id=1, replica_groups={{0,1,2,3,4,5,6,7},{8,9,10,11,12,13,14,15},{16,17,18,19,20,21,22,23},{24..., dimensions={0} | all-to-all | bytes 786432 | tf_op jit(solution)/shard_map/all_to_all | solution.py:186
  120.6 3.7 %all-to-all-start.3 = ((bf16[8,64,512]{2,1,0:T(8,128)(2,1)}), bf16[8,64,512]{2,1,0:T(8,128)(2,1)S(1)}, u32[]{:S(2)}, u32[]{:S(2)}) async-start(bf16[8,64,512]{2,1,0:T(8,128)(2,1)} %get-tuple-element.141), calls=%async_computation.3 | async-start | bytes 1048576 | tf_op jit(solution)/shard_map/all_to_all | solution.py:186
  124.4 5.5 %shard_map.90 = (bf16[96,2048]{1,0:T(8,128)(2,1)}, bf16[96,2048]{1,0:T(8,128)(2,1)}) custom-call(s32[3]{0:T(128)S(1)} %pad_add_fusion.1.pos, bf16[96,2048]{1,0:T(8,128)(2,1)S(1)} %copy-done.2, bf16[8,96,256]{2,1,0:T(8,128)(2,1)S(1)} %all_to_all.20.ctx, bf16[512,2048]{1,0:T(8,128)(2,1)} %own, bf16[512,2048]{1,0:T(8,128)(2,1)} %collective-permute-done.8.cross, ...), custom_call_target="tpu_custom_call" | custom-call | tf_op jit(solution)/shard_map/pallas_call | solution.py:291
  129.9 2.1 %collective-permute-start.24 = (bf16[96,2048]{1,0:T(8,128)(2,1)}, bf16[96,2048]{1,0:T(8,128)(2,1)S(1)}, u32[]{:S(2)}, u32[]{:S(2)}) collective-permute-start(bf16[96,2048]{1,0:T(8,128)(2,1)} %get-tuple-element.172.refs_0_), channel_id=1, source_target_pairs={{0,4},{1,5},{2,6},{3,7},{4,0},{5,1},{6,2},{7,3},{8,12},{9,13},{10,... | collective-permute-start | bytes 1179656 | tf_op jit(solution)/shard_map/ppermute | solution.py:100
  134.2 11.2 %collective-permute-done.22.refs_8_.refs_6_ = bf16[4,128,512]{2,1,0:T(8,128)(2,1)} collective-permute-done((bf16[4,128,512]{2,1,0:T(8,128)(2,1)}, bf16[4,128,512]{2,1,0:T(8,128)(2,1)}, u32[]{:S(2)}, u32[]{:S(2)}) %collective-permute-start.22) | collective-permute-done | bytes 524320 | tf_op jit(solution)/shard_map/ppermute | solution.py:100
  148.5 3.4 %collective-permute-done.26.refs_1_ = bf16[48,2048]{1,0:T(8,128)(2,1)S(1)} collective-permute-done((bf16[48,2048]{1,0:T(8,128)(2,1)S(1)}, bf16[48,2048]{1,0:T(8,128)(2,1)S(1)}, u32[]{:S(2)}, u32[]{:S(2)}) %collective-permute-start.26) | collective-permute-done | bytes 196640 | tf_op jit(solution)/shard_map/ppermute | solution.py:100
  155.3 3.9 %shard_map.91 = bf16[384,512]{1,0:T(8,128)(2,1)S(1)} custom-call(s32[3]{0:T(128)S(1)} %pad_add_fusion.1.pos, bf16[96,2048]{1,0:T(8,128)(2,1)S(1)} %collective-permute-done.24.refs_0_, bf16[48,2048]{1,0:T(8,128)(2,1)S(1)} %collective-permute-done.26.refs_1_, bf16[48,2048]{1,0:T(8,128)(2,1)S(1)} %collective-permute-done.27.refs_2_, ...), custom_call_target="tpu_custom_call" | custom-call | tf_op jit(solution)/shard_map/pallas_call | solution.py:342
  161.7 3.8 %shard_map.92 = bf16[384,512]{1,0:T(8,128)(2,1)S(1)} custom-call(s32[3]{0:T(128)S(1)} %pad_add_fusion.1.pos, bf16[96,2048]{1,0:T(8,128)(2,1)S(1)} %collective-permute-done.24.refs_0_, bf16[48,2048]{1,0:T(8,128)(2,1)S(1)} %collective-permute-done.26.refs_1_, bf16[48,2048]{1,0:T(8,128)(2,1)S(1)} %collective-permute-done.27.refs_2_, ...), custom_call_target="tpu_custom_call" | custom-call | tf_op jit(solution)/shard_map/pallas_call | solution.py:342
  167.6 3.1 %shard_map.93.refs_1_ = bf16[384,512]{1,0:T(8,128)(2,1)S(1)} custom-call(s32[3]{0:T(128)S(1)} %pad_add_fusion.1.pos, bf16[96,2048]{1,0:T(8,128)(2,1)} %get-tuple-element.172.refs_0_, bf16[96,2048]{1,0:T(8,128)(2,1)S(1)} %collective-permute-done.25.refs_1_, bf16[96,2048]{1,0:T(8,128)(2,1)S(1)} %collective-permute-done.31.refs_2_, ...), custom_call_target="tpu_custom_call" | custom-call | tf_op jit(solution)/shard_map/pallas_call | solution.py:342
  170.7 3.0 %shard_map.94.refs_2_ = bf16[384,512]{1,0:T(8,128)(2,1)S(1)} custom-call(s32[3]{0:T(128)S(1)} %pad_add_fusion.1.pos, bf16[96,2048]{1,0:T(8,128)(2,1)} %get-tuple-element.172.refs_0_, bf16[96,2048]{1,0:T(8,128)(2,1)S(1)} %collective-permute-done.25.refs_1_, bf16[96,2048]{1,0:T(8,128)(2,1)S(1)} %collective-permute-done.31.refs_2_, ...), custom_call_target="tpu_custom_call" | custom-call | tf_op jit(solution)/shard_map/pallas_call | solution.py:342
  175.4 3.4 %collective-permute-done.35.refs_1_ = bf16[384,512]{1,0:T(8,128)(2,1)S(1)} collective-permute-done((bf16[384,512]{1,0:T(8,128)(2,1)S(1)}, bf16[384,512]{1,0:T(8,128)(2,1)S(1)}, u32[]{:S(2)}, u32[]{:S(2)}) %collective-permute-start.35) | collective-permute-done | bytes 393248 | tf_op jit(solution)/shard_map/ppermute | solution.py:100
  (140 shorter events, 45.9 us)
Async XLA Ops:
  3.3 46.7 %all-to-all-start = ((bf16[32,64,384]{2,1,0:T(8,128)(2,1)}), bf16[32,64,384]{2,1,0:T(8,128)(2,1)}, u32[]{:S(2)}, u32[]{:S(2)}) async-start(bf16[32,64,384]{2,1,0:T(8,128)(2,1)} %shard_map.85), calls=%async_computation | async-start | bytes 3145728 | tf_op jit(solution)/shard_map/all_to_all | solution.py:181
  13.4 22.5 %collective-permute-start.2 = (bf16[96,2048]{1,0:T(8,128)(2,1)S(1)}, bf16[96,2048]{1,0:T(8,128)(2,1)S(1)}, u32[]{:S(2)}, u32[]{:S(2)}) collective-permute-start(bf16[96,2048]{1,0:T(8,128)(2,1)S(1)} %get-tuple-element.112.refs_0_), channel_id=1, source_target_pairs={{0,4},{1,5},{2,6},{3,7},{4,0},{5,1},{6,2},{7,3},{8,12},{9,13},{10,... | collective-permute-start | bytes 1179656 | tf_op jit(solution)/shard_map/ppermute | solution.py:100
  15.1 23.1 %collective-permute-start.3 = (bf16[96,2048]{1,0:T(8,128)(2,1)S(1)}, bf16[96,2048]{1,0:T(8,128)(2,1)S(1)}, u32[]{:S(2)}, u32[]{:S(2)}) collective-permute-start(bf16[96,2048]{1,0:T(8,128)(2,1)S(1)} %get-tuple-element.112.refs_0_), channel_id=1, source_target_pairs={{0,2},{1,3},{2,0},{3,1},{4,6},{5,7},{6,4},{7,5},{8,10},{9,11},{10,... | collective-permute-start | bytes 1179656 | tf_op jit(solution)/shard_map/ppermute | solution.py:100
  16.6 33.4 %collective-permute-start = (bf16[8,64,512]{2,1,0:T(8,128)(2,1)}, bf16[8,64,512]{2,1,0:T(8,128)(2,1)S(1)}, u32[]{:S(2)}, u32[]{:S(2)}) collective-permute-start(bf16[8,64,512]{2,1,0:T(8,128)(2,1)} %get-tuple-element.141), channel_id=1, source_target_pairs={{0,8},{1,9},{2,10},{3,11},{4,12},{5,13},{6,14},{7,15},{8,0},{9,1},... | collective-permute-start | bytes 1572872 | tf_op jit(solution)/shard_map/ppermute | solution.py:100
  18.0 20.3 %collective-permute-start.1 = (s32[1,384]{1,0:T(1,128)S(1)}, s32[1,384]{1,0:T(1,128)S(1)}, u32[]{:S(2)}, u32[]{:S(2)}) collective-permute-start(s32[1,384]{1,0:T(1,128)S(1)} %copy-done.28), channel_id=1, source_target_pairs={{0,4},{1,5},{2,6},{3,7},{4,0},{5,1},{6,2},{7,3},{8,12},{9,13},{10,... | collective-permute-start | bytes 4616 | tf_op jit(solution)/shard_map/ppermute | solution.py:100
  35.9 14.1 %collective-permute-start.4 = (bf16[48,2048]{1,0:T(8,128)(2,1)S(1)}, bf16[48,2048]{1,0:T(8,128)(2,1)S(1)}, u32[]{:S(2)}, u32[]{:S(2)}) collective-permute-start(bf16[48,2048]{1,0:T(8,128)(2,1)S(1)} %slice.32), channel_id=1, source_target_pairs={{0,2},{1,3},{2,0},{3,1},{4,6},{5,7},{6,4},{7,5},{8,10},{9,11},{10,... | collective-permute-start | bytes 589832 | tf_op jit(solution)/shard_map/ppermute | solution.py:100
  38.2 11.8 %collective-permute-start.5 = (bf16[48,2048]{1,0:T(8,128)(2,1)S(1)}, bf16[48,2048]{1,0:T(8,128)(2,1)S(1)}, u32[]{:S(2)}, u32[]{:S(2)}) collective-permute-start(bf16[48,2048]{1,0:T(8,128)(2,1)S(1)} %slice.33), channel_id=1, source_target_pairs={{0,4},{1,5},{2,6},{3,7},{4,0},{5,1},{6,2},{7,3},{8,12},{9,13},{10,... | collective-permute-start | bytes 589832 | tf_op jit(solution)/shard_map/ppermute | solution.py:100
  50.0 38.4 %collective-permute-start.8 = (bf16[512,2048]{1,0:T(8,128)(2,1)}, bf16[512,2048]{1,0:T(8,128)(2,1)}, u32[]{:S(2)}, u32[]{:S(2)}) collective-permute-start(bf16[512,2048]{1,0:T(8,128)(2,1)} %own), channel_id=1, source_target_pairs={{0,1},{1,0},{2,3},{3,2},{4,5},{5,4},{6,7},{7,6},{8,9},{9,8},{10,11... | collective-permute-start | bytes 6291464 | tf_op jit(solution)/shard_map/ppermute | solution.py:100
  50.1 38.3 %collective-permute-start.6 = (bf16[2048,384]{1,0:T(8,128)(2,1)}, bf16[2048,384]{1,0:T(8,128)(2,1)}, u32[]{:S(2)}, u32[]{:S(2)}) collective-permute-start(bf16[2048,384]{1,0:T(8,128)(2,1)} %bitcast.refs_10_), channel_id=1, source_target_pairs={{0,8},{1,9},{2,10},{3,11},{4,12},{5,13},{6,14},{7,15},{8,0},{9,1},... | collective-permute-start | bytes 4718600 | tf_op jit(solution)/shard_map/ppermute | solution.py:100
  51.0 37.5 %collective-permute-start.7 = (bf16[256,2048]{1,0:T(8,128)(2,1)}, bf16[256,2048]{1,0:T(8,128)(2,1)}, u32[]{:S(2)}, u32[]{:S(2)}) collective-permute-start(bf16[256,2048]{1,0:T(8,128)(2,1)} %constant_dynamic-slice_fusion.1), channel_id=1, source_target_pairs={{0,2},{1,3},{2,0},{3,1},{4,6},{5,7},{6,4},{7,5},{8,10},{9,11},{10,... | collective-permute-start | bytes 3145736 | tf_op jit(solution)/shard_map/ppermute | solution.py:100
  53.9 34.6 %all-to-all-start.1 = ((bf16[8,128,512]{2,1,0:T(8,128)(2,1)}), bf16[8,128,512]{2,1,0:T(8,128)(2,1)S(1)}, u32[]{:S(2)}, u32[]{:S(2)}) async-start(bf16[8,128,512]{2,1,0:T(8,128)(2,1)} %shard_map.87), calls=%async_computation.1 | async-start | bytes 2097152 | tf_op jit(solution)/shard_map/all_to_all | solution.py:186
  88.6 28.5 %collective-permute-start.14 = (bf16[8,64,512]{2,1,0:T(8,128)(2,1)S(1)}, bf16[8,64,512]{2,1,0:T(8,128)(2,1)S(1)}, u32[]{:S(2)}, u32[]{:S(2)}) collective-permute-start(bf16[8,64,512]{2,1,0:T(8,128)(2,1)S(1)} %slice.26), channel_id=1, source_target_pairs={{0,8},{1,9},{2,10},{3,11},{4,12},{5,13},{6,14},{7,15},{8,0},{9,1},... | collective-permute-start | bytes 1572872 | tf_op jit(solution)/shard_map/ppermute | solution.py:100
  90.1 27.0 %collective-permute-start.15 = (bf16[4,128,512]{2,1,0:T(8,128)(2,1)S(1)}, bf16[4,128,512]{2,1,0:T(8,128)(2,1)S(1)}, u32[]{:S(2)}, u32[]{:S(2)}) collective-permute-start(bf16[4,128,512]{2,1,0:T(8,128)(2,1)S(1)} %slice.27), channel_id=1, source_target_pairs={{0,16},{1,17},{2,18},{3,19},{4,20},{5,21},{6,22},{7,23},{8,24},{9,... | collective-permute-start | bytes 1572872 | tf_op jit(solution)/shard_map/ppermute | solution.py:100
  93.7 23.4 %collective-permute-start.16 = (bf16[128,2048]{1,0:T(8,128)(2,1)S(1)}, bf16[128,2048]{1,0:T(8,128)(2,1)}, u32[]{:S(2)}, u32[]{:S(2)}) collective-permute-start(bf16[128,2048]{1,0:T(8,128)(2,1)S(1)} %slice.28), channel_id=1, source_target_pairs={{0,4},{1,5},{2,6},{3,7},{4,0},{5,1},{6,2},{7,3},{8,12},{9,13},{10,... | collective-permute-start | bytes 1572872 | tf_op jit(solution)/shard_map/ppermute | solution.py:100
  94.2 23.0 %collective-permute-start.17 = (bf16[128,2048]{1,0:T(8,128)(2,1)S(1)}, bf16[128,2048]{1,0:T(8,128)(2,1)}, u32[]{:S(2)}, u32[]{:S(2)}) collective-permute-start(bf16[128,2048]{1,0:T(8,128)(2,1)S(1)} %copy-done.27), channel_id=1, source_target_pairs={{0,2},{1,3},{2,0},{3,1},{4,6},{5,7},{6,4},{7,5},{8,10},{9,11},{10,... | collective-permute-start | bytes 1572872 | tf_op jit(solution)/shard_map/ppermute | solution.py:100
  102.5 14.6 %collective-permute-start.18 = (bf16[3,2,2,128,128]{4,3,2,1,0:T(8,128)(2,1)S(1)}, bf16[3,2,2,128,128]{4,3,2,1,0:T(8,128)(2,1)S(1)}, u32[]{:S(2)}, u32[]{:S(2)}) collective-permute-start(bf16[3,2,2,128,128]{4,3,2,1,0:T(8,128)(2,1)S(1)} %get-tuple-element.132), channel_id=1, source_target_pairs={{0,4},{1,5},{2,6},{3,7},{4,0},{5,1},{6,2},{7,3},{8,12},{9,13},{10,... | collective-permute-start | bytes 1179656 | tf_op jit(solution)/shard_map/ppermute | solution.py:100
  118.7 26.7 %collective-permute-start.22 = (bf16[4,128,512]{2,1,0:T(8,128)(2,1)}, bf16[4,128,512]{2,1,0:T(8,128)(2,1)}, u32[]{:S(2)}, u32[]{:S(2)}) collective-permute-start(bf16[4,128,512]{2,1,0:T(8,128)(2,1)} %slice.29), channel_id=1, source_target_pairs={{0,16},{1,17},{2,18},{3,19},{4,20},{5,21},{6,22},{7,23},{8,24},{9,... | collective-permute-start | bytes 1572872 | tf_op jit(solution)/shard_map/ppermute | solution.py:100
  119.7 25.7 %collective-permute-start.23 = (bf16[4,128,512]{2,1,0:T(8,128)(2,1)S(1)}, bf16[4,128,512]{2,1,0:T(8,128)(2,1)}, u32[]{:S(2)}, u32[]{:S(2)}) collective-permute-start(bf16[4,128,512]{2,1,0:T(8,128)(2,1)S(1)} %collective-permute-done.15.refs_7_.refs_5_), channel_id=1, source_target_pairs={{0,8},{1,9},{2,10},{3,11},{4,12},{5,13},{6,14},{7,15},{8,0},{9,1},... | collective-permute-start | bytes 1572872 | tf_op jit(solution)/shard_map/ppermute | solution.py:100
  120.6 13.5 %all-to-all-start.3 = ((bf16[8,64,512]{2,1,0:T(8,128)(2,1)}), bf16[8,64,512]{2,1,0:T(8,128)(2,1)S(1)}, u32[]{:S(2)}, u32[]{:S(2)}) async-start(bf16[8,64,512]{2,1,0:T(8,128)(2,1)} %get-tuple-element.141), calls=%async_computation.3 | async-start | bytes 1048576 | tf_op jit(solution)/shard_map/all_to_all | solution.py:186
  129.9 15.5 %collective-permute-start.24 = (bf16[96,2048]{1,0:T(8,128)(2,1)}, bf16[96,2048]{1,0:T(8,128)(2,1)S(1)}, u32[]{:S(2)}, u32[]{:S(2)}) collective-permute-start(bf16[96,2048]{1,0:T(8,128)(2,1)} %get-tuple-element.172.refs_0_), channel_id=1, source_target_pairs={{0,4},{1,5},{2,6},{3,7},{4,0},{5,1},{6,2},{7,3},{8,12},{9,13},{10,... | collective-permute-start | bytes 1179656 | tf_op jit(solution)/shard_map/ppermute | solution.py:100
  131.9 13.5 %collective-permute-start.25 = (bf16[96,2048]{1,0:T(8,128)(2,1)}, bf16[96,2048]{1,0:T(8,128)(2,1)S(1)}, u32[]{:S(2)}, u32[]{:S(2)}) collective-permute-start(bf16[96,2048]{1,0:T(8,128)(2,1)} %get-tuple-element.172.refs_0_), channel_id=1, source_target_pairs={{0,2},{1,3},{2,0},{3,1},{4,6},{5,7},{6,4},{7,5},{8,10},{9,11},{10,... | collective-permute-start | bytes 1179656 | tf_op jit(solution)/shard_map/ppermute | solution.py:100
  148.5 13.1 %collective-permute-start.34 = (bf16[4,128,512]{2,1,0:T(8,128)(2,1)}, bf16[4,128,512]{2,1,0:T(8,128)(2,1)S(1)}, u32[]{:S(2)}, u32[]{:S(2)}) collective-permute-start(bf16[4,128,512]{2,1,0:T(8,128)(2,1)} %collective-permute-done.22.refs_8_.refs_6_), channel_id=1, source_target_pairs={{0,8},{1,9},{2,10},{3,11},{4,12},{5,13},{6,14},{7,15},{8,0},{9,1},... | collective-permute-start | bytes 1572872 | tf_op jit(solution)/shard_map/ppermute | solution.py:100
  159.2 14.6 %collective-permute-start.33 = (bf16[384,512]{1,0:T(8,128)(2,1)S(1)}, bf16[384,512]{1,0:T(8,128)(2,1)S(1)}, u32[]{:S(2)}, u32[]{:S(2)}) collective-permute-start(bf16[384,512]{1,0:T(8,128)(2,1)S(1)} %shard_map.91), channel_id=1, source_target_pairs={{0,4},{1,5},{2,6},{3,7},{4,0},{5,1},{6,2},{7,3},{8,12},{9,13},{10,... | collective-permute-start | bytes 1179656 | tf_op jit(solution)/shard_map/ppermute | solution.py:100
  165.5 13.3 %collective-permute-start.35 = (bf16[384,512]{1,0:T(8,128)(2,1)S(1)}, bf16[384,512]{1,0:T(8,128)(2,1)S(1)}, u32[]{:S(2)}, u32[]{:S(2)}) collective-permute-start(bf16[384,512]{1,0:T(8,128)(2,1)S(1)} %shard_map.92), channel_id=1, source_target_pairs={{0,4},{1,5},{2,6},{3,7},{4,0},{5,1},{6,2},{7,3},{8,12},{9,13},{10,... | collective-permute-start | bytes 1179656 | tf_op jit(solution)/shard_map/ppermute | solution.py:100
  (44 other events, 306.6 us)

commit v8 on v6

--- a/solution.py
+++ b/solution.py
@@ -14,7 +14,7 @@
 BF = jnp.bfloat16
 F32 = jnp.float32
 VMEM_LIMIT = 50 * 1024 * 1024
-SMALL_LIMIT = 16 * 1024 * 1024
+SMALL_LIMIT = 12 * 1024 * 1024
 
 
 def layer_norm(values):

time: 181 us -> 181 us (level)
  no operation moved by 1% of the time
where the time goes in v8:
time: 181 us; the launch traced here: 180 us
  waiting for transfers between devices  66.5 us (37%)
  starting transfers between devices  44.6 us (25%)
  Pallas kernels  40.5 us (22%)
  blocking collectives  14 us (8%)
  local copies, waits for them, and re-layouts  13.3 us (7%)
    ppermute x36, waiting for transfers between devices, send(): return lax.ppermute(value, AXES, moves)  50.2 us
    ppermute x36, starting transfers between devices, send(): return lax.ppermute(value, AXES, moves)  30 us
    all_to_all x2, waiting for transfers between devices, in_plane(): lax.all_to_all(pieces, AXES, split_axis=0, concat_axis=0, tiled=True, axi...  16.4 us
    all_to_all x1, blocking collectives, in_plane(): lax.all_to_all(pieces, AXES, split_axis=0, concat_axis=0, tiled=True, axi...  14 us
    pallas_call x4, Pallas kernels, up_part(): pl.pallas_call(functools.partial(up_kernel, len(pieces), half), in_specs=...  13.8 us
    pallas_call x2, Pallas kernels, one_head(): pl.pallas_call(functools.partial(head_kernel, bool(before)), in_specs=[SM...  12.7 us
    all_to_all x1, starting transfers between devices, to_all(): mine = lax.all_to_all(pieces, AXES, split_axis=0, concat_axis=0, tiled=True)  7.41 us
    all_to_all x2, starting transfers between devices, in_plane(): lax.all_to_all(pieces, AXES, split_axis=0, concat_axis=0, tiled=True, axi...  7.25 us
  transfers between devices with their start and end apart: 39, of which 15 were waited for; matrix products, arithmetic and copies ran while one was open for 4% of the time, Pallas kernels for 21%

profile of v8, /device:TPU:0, one launch (start us, length us, event | category | flops | bytes accessed | tf_op | source)
XLA Modules:
  0.0 180.3 jit_solution(16283164908211771877)
XLA Ops:
  3.3 7.4 %all-to-all-start = ((bf16[32,64,384]{2,1,0:T(8,128)(2,1)}), bf16[32,64,384]{2,1,0:T(8,128)(2,1)}, u32[]{:S(2)}, u32[]{:S(2)}) async-start(bf16[32,64,384]{2,1,0:T(8,128)(2,1)} %shard_map.85), calls=%async_computation | async-start | bytes 3145728 | tf_op jit(solution)/shard_map/all_to_all | solution.py:179
  10.9 1.7 shard_map.86
  13.4 1.7 collective-permute-start.2
  18.6 1.9 %constant_dynamic-slice_fusion = bf16[128,2048]{1,0:T(8,128)(2,1)} fusion(bf16[512,2048]{1,0:T(8,128)(2,1)} %own, s32[]{:T(128)S(6)} %select_n.20), kind=kLoop, calls=%fused_computation.3 | loop fusion | bytes 1048580 | tf_op jit(solution)/shard_map/dynamic_slice | solution.py:434
  20.5 2.4 %constant_dynamic-slice_fusion.1 = bf16[256,2048]{1,0:T(8,128)(2,1)} fusion(bf16[512,2048]{1,0:T(8,128)(2,1)} %own, s32[]{:T(128)S(6)} %select_n.19), kind=kLoop, calls=%fused_computation.4 | loop fusion | bytes 2097156 | tf_op jit(solution)/shard_map/dynamic_slice | solution.py:433
  22.9 13.0 %collective-permute-done.2.refs_1_ = bf16[96,2048]{1,0:T(8,128)(2,1)S(1)} collective-permute-done((bf16[96,2048]{1,0:T(8,128)(2,1)S(1)}, bf16[96,2048]{1,0:T(8,128)(2,1)S(1)}, u32[]{:S(2)}, u32[]{:S(2)}) %collective-permute-start.2) | collective-permute-done | bytes 393248 | tf_op jit(solution)/shard_map/ppermute | solution.py:100
  35.9 2.3 %collective-permute-start.4 = (bf16[48,2048]{1,0:T(8,128)(2,1)S(1)}, bf16[48,2048]{1,0:T(8,128)(2,1)S(1)}, u32[]{:S(2)}, u32[]{:S(2)}) collective-permute-start(bf16[48,2048]{1,0:T(8,128)(2,1)S(1)} %slice.32), channel_id=1, source_target_pairs={{0,2},{1,3},{2,0},{3,1},{4,6},{5,7},{6,4},{7,5},{8,10},{9,11},{10,... | collective-permute-start | bytes 589832 | tf_op jit(solution)/shard_map/ppermute | solution.py:100
  38.4 11.6 %collective-permute-done.got = bf16[8,64,512]{2,1,0:T(8,128)(2,1)S(1)} collective-permute-done((bf16[8,64,512]{2,1,0:T(8,128)(2,1)}, bf16[8,64,512]{2,1,0:T(8,128)(2,1)S(1)}, u32[]{:S(2)}, u32[]{:S(2)}) %collective-permute-start) | collective-permute-done | bytes 524320 | tf_op jit(solution)/shard_map/ppermute | solution.py:100
  53.4 3.6 %all-to-all-start.1 = ((bf16[8,128,512]{2,1,0:T(8,128)(2,1)}), bf16[8,128,512]{2,1,0:T(8,128)(2,1)S(1)}, u32[]{:S(2)}, u32[]{:S(2)}) async-start(bf16[8,128,512]{2,1,0:T(8,128)(2,1)} %shard_map.87), calls=%async_computation.1 | async-start | bytes 2097152 | tf_op jit(solution)/shard_map/all_to_all | solution.py:184
  62.5 6.0 %shard_map.88 = (bf16[768,256]{1,0:T(8,128)(2,1)S(1)}, bf16[3,2,2,128,128]{4,3,2,1,0:T(8,128)(2,1)S(1)}, bf16[3,2,2,128,128]{4,3,2,1,0:T(8,128)(2,1)S(1)}) custom-call(s32[3]{0:T(128)S(1)} %pad_add_fusion.1.pos, f32[2]{0:T(128)S(1)} %multiply_exponential_fusion.slope, s32[2,1,384]{2,1,0:T(1,128)S(1)} %broadcast_in_dim.3.seg_rows, ...), custom_call_target="tpu_custom_call" | custom-call | tf_op jit(solution)/shard_map/pallas_call | solution.py:244
  72.8 15.6 %all-to-all-done.1.refs_6_.refs_4_ = bf16[8,128,512]{2,1,0:T(8,128)(2,1)S(1)} async-done(((bf16[8,128,512]{2,1,0:T(8,128)(2,1)}), bf16[8,128,512]{2,1,0:T(8,128)(2,1)S(1)}, u32[]{:S(2)}, u32[]{:S(2)}) %all-to-all-start.1) | async-done | bytes 1048608 | tf_op jit(solution)/shard_map/all_to_all | solution.py:184
  90.1 2.5 %collective-permute-start.15 = (bf16[4,128,512]{2,1,0:T(8,128)(2,1)S(1)}, bf16[4,128,512]{2,1,0:T(8,128)(2,1)S(1)}, u32[]{:S(2)}, u32[]{:S(2)}) collective-permute-start(bf16[4,128,512]{2,1,0:T(8,128)(2,1)S(1)} %slice.27), channel_id=1, source_target_pairs={{0,16},{1,17},{2,18},{3,19},{4,20},{5,21},{6,22},{7,23},{8,24},{9,... | collective-permute-start | bytes 1572872 | tf_op jit(solution)/shard_map/ppermute | solution.py:100
  95.8 6.7 %shard_map.89 = (bf16[768,256]{1,0:T(8,128)(2,1)S(1)}, bf16[3,2,2,128,128]{4,3,2,1,0:T(8,128)(2,1)S(1)}, bf16[3,2,2,128,128]{4,3,2,1,0:T(8,128)(2,1)S(1)}) custom-call(s32[3]{0:T(128)S(1)} %pad_add_fusion.1.pos, f32[2]{0:T(128)S(1)} %multiply_exponential_fusion.slope, s32[2,1,384]{2,1,0:T(1,128)S(1)} %broadcast_in_dim.3.seg_rows, ...), custom_call_target="tpu_custom_call" | custom-call | tf_op jit(solution)/shard_map/pallas_call | solution.py:244
  103.2 14.0 %all_to_all.20.ctx = bf16[8,96,256]{2,1,0:T(8,128)(2,1)S(1)} all-to-all(bf16[8,96,256]{2,1,0:T(8,128)(2,1)S(1)} %bitcast.5), channel_id=1, replica_groups={{0,1,2,3,4,5,6,7},{8,9,10,11,12,13,14,15},{16,17,18,19,20,21,22,23},{24..., dimensions={0} | all-to-all | bytes 786432 | tf_op jit(solution)/shard_map/all_to_all | solution.py:184
  120.6 3.7 %all-to-all-start.3 = ((bf16[8,64,512]{2,1,0:T(8,128)(2,1)}), bf16[8,64,512]{2,1,0:T(8,128)(2,1)S(1)}, u32[]{:S(2)}, u32[]{:S(2)}) async-start(bf16[8,64,512]{2,1,0:T(8,128)(2,1)} %get-tuple-element.141), calls=%async_computation.3 | async-start | bytes 1048576 | tf_op jit(solution)/shard_map/all_to_all | solution.py:184
  124.4 5.5 %shard_map.90 = (bf16[96,2048]{1,0:T(8,128)(2,1)}, bf16[96,2048]{1,0:T(8,128)(2,1)}) custom-call(s32[3]{0:T(128)S(1)} %pad_add_fusion.1.pos, bf16[96,2048]{1,0:T(8,128)(2,1)S(1)} %copy-done.2, bf16[8,96,256]{2,1,0:T(8,128)(2,1)S(1)} %all_to_all.20.ctx, bf16[512,2048]{1,0:T(8,128)(2,1)} %own, bf16[512,2048]{1,0:T(8,128)(2,1)} %collective-permute-done.8.cross, ...), custom_call_target="tpu_custom_call" | custom-call | tf_op jit(solution)/shard_map/pallas_call | solution.py:289
  129.9 2.1 %collective-permute-start.24 = (bf16[96,2048]{1,0:T(8,128)(2,1)}, bf16[96,2048]{1,0:T(8,128)(2,1)S(1)}, u32[]{:S(2)}, u32[]{:S(2)}) collective-permute-start(bf16[96,2048]{1,0:T(8,128)(2,1)} %get-tuple-element.172.refs_0_), channel_id=1, source_target_pairs={{0,4},{1,5},{2,6},{3,7},{4,0},{5,1},{6,2},{7,3},{8,12},{9,13},{10,... | collective-permute-start | bytes 1179656 | tf_op jit(solution)/shard_map/ppermute | solution.py:100
  134.2 11.2 %collective-permute-done.22.refs_8_.refs_6_ = bf16[4,128,512]{2,1,0:T(8,128)(2,1)} collective-permute-done((bf16[4,128,512]{2,1,0:T(8,128)(2,1)}, bf16[4,128,512]{2,1,0:T(8,128)(2,1)}, u32[]{:S(2)}, u32[]{:S(2)}) %collective-permute-start.22) | collective-permute-done | bytes 524320 | tf_op jit(solution)/shard_map/ppermute | solution.py:100
  148.5 3.4 %collective-permute-done.26.refs_1_ = bf16[48,2048]{1,0:T(8,128)(2,1)S(1)} collective-permute-done((bf16[48,2048]{1,0:T(8,128)(2,1)S(1)}, bf16[48,2048]{1,0:T(8,128)(2,1)S(1)}, u32[]{:S(2)}, u32[]{:S(2)}) %collective-permute-start.26) | collective-permute-done | bytes 196640 | tf_op jit(solution)/shard_map/ppermute | solution.py:100
  155.3 3.9 %shard_map.91 = bf16[384,512]{1,0:T(8,128)(2,1)S(1)} custom-call(s32[3]{0:T(128)S(1)} %pad_add_fusion.1.pos, bf16[96,2048]{1,0:T(8,128)(2,1)S(1)} %collective-permute-done.24.refs_0_, bf16[48,2048]{1,0:T(8,128)(2,1)S(1)} %collective-permute-done.26.refs_1_, bf16[48,2048]{1,0:T(8,128)(2,1)S(1)} %collective-permute-done.27.refs_2_, ...), custom_call_target="tpu_custom_call" | custom-call | tf_op jit(solution)/shard_map/pallas_call | solution.py:340
  161.7 3.8 %shard_map.92 = bf16[384,512]{1,0:T(8,128)(2,1)S(1)} custom-call(s32[3]{0:T(128)S(1)} %pad_add_fusion.1.pos, bf16[96,2048]{1,0:T(8,128)(2,1)S(1)} %collective-permute-done.24.refs_0_, bf16[48,2048]{1,0:T(8,128)(2,1)S(1)} %collective-permute-done.26.refs_1_, bf16[48,2048]{1,0:T(8,128)(2,1)S(1)} %collective-permute-done.27.refs_2_, ...), custom_call_target="tpu_custom_call" | custom-call | tf_op jit(solution)/shard_map/pallas_call | solution.py:340
  167.6 3.1 %shard_map.93.refs_1_ = bf16[384,512]{1,0:T(8,128)(2,1)S(1)} custom-call(s32[3]{0:T(128)S(1)} %pad_add_fusion.1.pos, bf16[96,2048]{1,0:T(8,128)(2,1)} %get-tuple-element.172.refs_0_, bf16[96,2048]{1,0:T(8,128)(2,1)S(1)} %collective-permute-done.25.refs_1_, bf16[96,2048]{1,0:T(8,128)(2,1)S(1)} %collective-permute-done.31.refs_2_, ...), custom_call_target="tpu_custom_call" | custom-call | tf_op jit(solution)/shard_map/pallas_call | solution.py:340
  170.7 3.0 %shard_map.94.refs_2_ = bf16[384,512]{1,0:T(8,128)(2,1)S(1)} custom-call(s32[3]{0:T(128)S(1)} %pad_add_fusion.1.pos, bf16[96,2048]{1,0:T(8,128)(2,1)} %get-tuple-element.172.refs_0_, bf16[96,2048]{1,0:T(8,128)(2,1)S(1)} %collective-permute-done.25.refs_1_, bf16[96,2048]{1,0:T(8,128)(2,1)S(1)} %collective-permute-done.31.refs_2_, ...), custom_call_target="tpu_custom_call" | custom-call | tf_op jit(solution)/shard_map/pallas_call | solution.py:340
  175.4 3.4 %collective-permute-done.35.refs_1_ = bf16[384,512]{1,0:T(8,128)(2,1)S(1)} collective-permute-done((bf16[384,512]{1,0:T(8,128)(2,1)S(1)}, bf16[384,512]{1,0:T(8,128)(2,1)S(1)}, u32[]{:S(2)}, u32[]{:S(2)}) %collective-permute-start.35) | collective-permute-done | bytes 393248 | tf_op jit(solution)/shard_map/ppermute | solution.py:100
  (140 shorter events, 45.4 us)
Async XLA Ops:
  3.3 46.7 %all-to-all-start = ((bf16[32,64,384]{2,1,0:T(8,128)(2,1)}), bf16[32,64,384]{2,1,0:T(8,128)(2,1)}, u32[]{:S(2)}, u32[]{:S(2)}) async-start(bf16[32,64,384]{2,1,0:T(8,128)(2,1)} %shard_map.85), calls=%async_computation | async-start | bytes 3145728 | tf_op jit(solution)/shard_map/all_to_all | solution.py:179
  13.4 22.5 %collective-permute-start.2 = (bf16[96,2048]{1,0:T(8,128)(2,1)S(1)}, bf16[96,2048]{1,0:T(8,128)(2,1)S(1)}, u32[]{:S(2)}, u32[]{:S(2)}) collective-permute-start(bf16[96,2048]{1,0:T(8,128)(2,1)S(1)} %get-tuple-element.112.refs_0_), channel_id=1, source_target_pairs={{0,4},{1,5},{2,6},{3,7},{4,0},{5,1},{6,2},{7,3},{8,12},{9,13},{10,... | collective-permute-start | bytes 1179656 | tf_op jit(solution)/shard_map/ppermute | solution.py:100
  15.1 23.1 %collective-permute-start.3 = (bf16[96,2048]{1,0:T(8,128)(2,1)S(1)}, bf16[96,2048]{1,0:T(8,128)(2,1)S(1)}, u32[]{:S(2)}, u32[]{:S(2)}) collective-permute-start(bf16[96,2048]{1,0:T(8,128)(2,1)S(1)} %get-tuple-element.112.refs_0_), channel_id=1, source_target_pairs={{0,2},{1,3},{2,0},{3,1},{4,6},{5,7},{6,4},{7,5},{8,10},{9,11},{10,... | collective-permute-start | bytes 1179656 | tf_op jit(solution)/shard_map/ppermute | solution.py:100
  16.6 33.4 %collective-permute-start = (bf16[8,64,512]{2,1,0:T(8,128)(2,1)}, bf16[8,64,512]{2,1,0:T(8,128)(2,1)S(1)}, u32[]{:S(2)}, u32[]{:S(2)}) collective-permute-start(bf16[8,64,512]{2,1,0:T(8,128)(2,1)} %get-tuple-element.141), channel_id=1, source_target_pairs={{0,8},{1,9},{2,10},{3,11},{4,12},{5,13},{6,14},{7,15},{8,0},{9,1},... | collective-permute-start | bytes 1572872 | tf_op jit(solution)/shard_map/ppermute | solution.py:100
  18.0 20.3 %collective-permute-start.1 = (s32[1,384]{1,0:T(1,128)S(1)}, s32[1,384]{1,0:T(1,128)S(1)}, u32[]{:S(2)}, u32[]{:S(2)}) collective-permute-start(s32[1,384]{1,0:T(1,128)S(1)} %copy-done.28), channel_id=1, source_target_pairs={{0,4},{1,5},{2,6},{3,7},{4,0},{5,1},{6,2},{7,3},{8,12},{9,13},{10,... | collective-permute-start | bytes 4616 | tf_op jit(solution)/shard_map/ppermute | solution.py:100
  35.9 14.1 %collective-permute-start.4 = (bf16[48,2048]{1,0:T(8,128)(2,1)S(1)}, bf16[48,2048]{1,0:T(8,128)(2,1)S(1)}, u32[]{:S(2)}, u32[]{:S(2)}) collective-permute-start(bf16[48,2048]{1,0:T(8,128)(2,1)S(1)} %slice.32), channel_id=1, source_target_pairs={{0,2},{1,3},{2,0},{3,1},{4,6},{5,7},{6,4},{7,5},{8,10},{9,11},{10,... | collective-permute-start | bytes 589832 | tf_op jit(solution)/shard_map/ppermute | solution.py:100
  38.2 11.8 %collective-permute-start.5 = (bf16[48,2048]{1,0:T(8,128)(2,1)S(1)}, bf16[48,2048]{1,0:T(8,128)(2,1)S(1)}, u32[]{:S(2)}, u32[]{:S(2)}) collective-permute-start(bf16[48,2048]{1,0:T(8,128)(2,1)S(1)} %slice.33), channel_id=1, source_target_pairs={{0,4},{1,5},{2,6},{3,7},{4,0},{5,1},{6,2},{7,3},{8,12},{9,13},{10,... | collective-permute-start | bytes 589832 | tf_op jit(solution)/shard_map/ppermute | solution.py:100
  50.0 38.4 %collective-permute-start.8 = (bf16[512,2048]{1,0:T(8,128)(2,1)}, bf16[512,2048]{1,0:T(8,128)(2,1)}, u32[]{:S(2)}, u32[]{:S(2)}) collective-permute-start(bf16[512,2048]{1,0:T(8,128)(2,1)} %own), channel_id=1, source_target_pairs={{0,1},{1,0},{2,3},{3,2},{4,5},{5,4},{6,7},{7,6},{8,9},{9,8},{10,11... | collective-permute-start | bytes 6291464 | tf_op jit(solution)/shard_map/ppermute | solution.py:100
  50.1 38.3 %collective-permute-start.6 = (bf16[2048,384]{1,0:T(8,128)(2,1)}, bf16[2048,384]{1,0:T(8,128)(2,1)}, u32[]{:S(2)}, u32[]{:S(2)}) collective-permute-start(bf16[2048,384]{1,0:T(8,128)(2,1)} %bitcast.refs_10_), channel_id=1, source_target_pairs={{0,8},{1,9},{2,10},{3,11},{4,12},{5,13},{6,14},{7,15},{8,0},{9,1},... | collective-permute-start | bytes 4718600 | tf_op jit(solution)/shard_map/ppermute | solution.py:100
  51.0 37.5 %collective-permute-start.7 = (bf16[256,2048]{1,0:T(8,128)(2,1)}, bf16[256,2048]{1,0:T(8,128)(2,1)}, u32[]{:S(2)}, u32[]{:S(2)}) collective-permute-start(bf16[256,2048]{1,0:T(8,128)(2,1)} %constant_dynamic-slice_fusion.1), channel_id=1, source_target_pairs={{0,2},{1,3},{2,0},{3,1},{4,6},{5,7},{6,4},{7,5},{8,10},{9,11},{10,... | collective-permute-start | bytes 3145736 | tf_op jit(solution)/shard_map/ppermute | solution.py:100
  53.4 35.0 %all-to-all-start.1 = ((bf16[8,128,512]{2,1,0:T(8,128)(2,1)}), bf16[8,128,512]{2,1,0:T(8,128)(2,1)S(1)}, u32[]{:S(2)}, u32[]{:S(2)}) async-start(bf16[8,128,512]{2,1,0:T(8,128)(2,1)} %shard_map.87), calls=%async_computation.1 | async-start | bytes 2097152 | tf_op jit(solution)/shard_map/all_to_all | solution.py:184
  88.6 28.5 %collective-permute-start.14 = (bf16[8,64,512]{2,1,0:T(8,128)(2,1)S(1)}, bf16[8,64,512]{2,1,0:T(8,128)(2,1)S(1)}, u32[]{:S(2)}, u32[]{:S(2)}) collective-permute-start(bf16[8,64,512]{2,1,0:T(8,128)(2,1)S(1)} %slice.26), channel_id=1, source_target_pairs={{0,8},{1,9},{2,10},{3,11},{4,12},{5,13},{6,14},{7,15},{8,0},{9,1},... | collective-permute-start | bytes 1572872 | tf_op jit(solution)/shard_map/ppermute | solution.py:100
  90.1 27.0 %collective-permute-start.15 = (bf16[4,128,512]{2,1,0:T(8,128)(2,1)S(1)}, bf16[4,128,512]{2,1,0:T(8,128)(2,1)S(1)}, u32[]{:S(2)}, u32[]{:S(2)}) collective-permute-start(bf16[4,128,512]{2,1,0:T(8,128)(2,1)S(1)} %slice.27), channel_id=1, source_target_pairs={{0,16},{1,17},{2,18},{3,19},{4,20},{5,21},{6,22},{7,23},{8,24},{9,... | collective-permute-start | bytes 1572872 | tf_op jit(solution)/shard_map/ppermute | solution.py:100
  93.7 23.4 %collective-permute-start.16 = (bf16[128,2048]{1,0:T(8,128)(2,1)S(1)}, bf16[128,2048]{1,0:T(8,128)(2,1)}, u32[]{:S(2)}, u32[]{:S(2)}) collective-permute-start(bf16[128,2048]{1,0:T(8,128)(2,1)S(1)} %slice.28), channel_id=1, source_target_pairs={{0,4},{1,5},{2,6},{3,7},{4,0},{5,1},{6,2},{7,3},{8,12},{9,13},{10,... | collective-permute-start | bytes 1572872 | tf_op jit(solution)/shard_map/ppermute | solution.py:100
  94.2 23.0 %collective-permute-start.17 = (bf16[128,2048]{1,0:T(8,128)(2,1)S(1)}, bf16[128,2048]{1,0:T(8,128)(2,1)}, u32[]{:S(2)}, u32[]{:S(2)}) collective-permute-start(bf16[128,2048]{1,0:T(8,128)(2,1)S(1)} %copy-done.27), channel_id=1, source_target_pairs={{0,2},{1,3},{2,0},{3,1},{4,6},{5,7},{6,4},{7,5},{8,10},{9,11},{10,... | collective-permute-start | bytes 1572872 | tf_op jit(solution)/shard_map/ppermute | solution.py:100
  102.5 14.6 %collective-permute-start.18 = (bf16[3,2,2,128,128]{4,3,2,1,0:T(8,128)(2,1)S(1)}, bf16[3,2,2,128,128]{4,3,2,1,0:T(8,128)(2,1)S(1)}, u32[]{:S(2)}, u32[]{:S(2)}) collective-permute-start(bf16[3,2,2,128,128]{4,3,2,1,0:T(8,128)(2,1)S(1)} %get-tuple-element.132), channel_id=1, source_target_pairs={{0,4},{1,5},{2,6},{3,7},{4,0},{5,1},{6,2},{7,3},{8,12},{9,13},{10,... | collective-permute-start | bytes 1179656 | tf_op jit(solution)/shard_map/ppermute | solution.py:100
  118.7 26.7 %collective-permute-start.22 = (bf16[4,128,512]{2,1,0:T(8,128)(2,1)}, bf16[4,128,512]{2,1,0:T(8,128)(2,1)}, u32[]{:S(2)}, u32[]{:S(2)}) collective-permute-start(bf16[4,128,512]{2,1,0:T(8,128)(2,1)} %slice.29), channel_id=1, source_target_pairs={{0,16},{1,17},{2,18},{3,19},{4,20},{5,21},{6,22},{7,23},{8,24},{9,... | collective-permute-start | bytes 1572872 | tf_op jit(solution)/shard_map/ppermute | solution.py:100
  119.7 25.7 %collective-permute-start.23 = (bf16[4,128,512]{2,1,0:T(8,128)(2,1)S(1)}, bf16[4,128,512]{2,1,0:T(8,128)(2,1)}, u32[]{:S(2)}, u32[]{:S(2)}) collective-permute-start(bf16[4,128,512]{2,1,0:T(8,128)(2,1)S(1)} %collective-permute-done.15.refs_7_.refs_5_), channel_id=1, source_target_pairs={{0,8},{1,9},{2,10},{3,11},{4,12},{5,13},{6,14},{7,15},{8,0},{9,1},... | collective-permute-start | bytes 1572872 | tf_op jit(solution)/shard_map/ppermute | solution.py:100
  120.6 13.5 %all-to-all-start.3 = ((bf16[8,64,512]{2,1,0:T(8,128)(2,1)}), bf16[8,64,512]{2,1,0:T(8,128)(2,1)S(1)}, u32[]{:S(2)}, u32[]{:S(2)}) async-start(bf16[8,64,512]{2,1,0:T(8,128)(2,1)} %get-tuple-element.141), calls=%async_computation.3 | async-start | bytes 1048576 | tf_op jit(solution)/shard_map/all_to_all | solution.py:184
  129.9 15.5 %collective-permute-start.24 = (bf16[96,2048]{1,0:T(8,128)(2,1)}, bf16[96,2048]{1,0:T(8,128)(2,1)S(1)}, u32[]{:S(2)}, u32[]{:S(2)}) collective-permute-start(bf16[96,2048]{1,0:T(8,128)(2,1)} %get-tuple-element.172.refs_0_), channel_id=1, source_target_pairs={{0,4},{1,5},{2,6},{3,7},{4,0},{5,1},{6,2},{7,3},{8,12},{9,13},{10,... | collective-permute-start | bytes 1179656 | tf_op jit(solution)/shard_map/ppermute | solution.py:100
  131.9 13.5 %collective-permute-start.25 = (bf16[96,2048]{1,0:T(8,128)(2,1)}, bf16[96,2048]{1,0:T(8,128)(2,1)S(1)}, u32[]{:S(2)}, u32[]{:S(2)}) collective-permute-start(bf16[96,2048]{1,0:T(8,128)(2,1)} %get-tuple-element.172.refs_0_), channel_id=1, source_target_pairs={{0,2},{1,3},{2,0},{3,1},{4,6},{5,7},{6,4},{7,5},{8,10},{9,11},{10,... | collective-permute-start | bytes 1179656 | tf_op jit(solution)/shard_map/ppermute | solution.py:100
  148.5 13.1 %collective-permute-start.34 = (bf16[4,128,512]{2,1,0:T(8,128)(2,1)}, bf16[4,128,512]{2,1,0:T(8,128)(2,1)S(1)}, u32[]{:S(2)}, u32[]{:S(2)}) collective-permute-start(bf16[4,128,512]{2,1,0:T(8,128)(2,1)} %collective-permute-done.22.refs_8_.refs_6_), channel_id=1, source_target_pairs={{0,8},{1,9},{2,10},{3,11},{4,12},{5,13},{6,14},{7,15},{8,0},{9,1},... | collective-permute-start | bytes 1572872 | tf_op jit(solution)/shard_map/ppermute | solution.py:100
  159.2 14.6 %collective-permute-start.33 = (bf16[384,512]{1,0:T(8,128)(2,1)S(1)}, bf16[384,512]{1,0:T(8,128)(2,1)S(1)}, u32[]{:S(2)}, u32[]{:S(2)}) collective-permute-start(bf16[384,512]{1,0:T(8,128)(2,1)S(1)} %shard_map.91), channel_id=1, source_target_pairs={{0,4},{1,5},{2,6},{3,7},{4,0},{5,1},{6,2},{7,3},{8,12},{9,13},{10,... | collective-permute-start | bytes 1179656 | tf_op jit(solution)/shard_map/ppermute | solution.py:100
  165.5 13.3 %collective-permute-start.35 = (bf16[384,512]{1,0:T(8,128)(2,1)S(1)}, bf16[384,512]{1,0:T(8,128)(2,1)S(1)}, u32[]{:S(2)}, u32[]{:S(2)}) collective-permute-start(bf16[384,512]{1,0:T(8,128)(2,1)S(1)} %shard_map.92), channel_id=1, source_target_pairs={{0,4},{1,5},{2,6},{3,7},{4,0},{5,1},{6,2},{7,3},{8,12},{9,13},{10,... | collective-permute-start | bytes 1179656 | tf_op jit(solution)/shard_map/ppermute | solution.py:100
  (44 other events, 305.1 us)
